TPU v7x, 32 devices: a whole 2x2x4 slice. The times are simulated.
32 devices in a mesh: row: 8 (over z, y), col: 4 (over x, core).
Axes of the slice: x: 2, y: 2, z: 4, core: 2. Of those that a mesh axis runs over, the one named last changes fastest.
Arguments:
- hidden_in: bfloat16 [16384, 2048], P('row', 'col'), may hold values from -6 to 6
- lengths: int32 [16], P('row'), may hold values from 256 to 1024
- routes: int32 [16384, 8], P('row'), may hold values from 0 to 15, all different within a row; in each aligned block of 2048 rows (0 to 2047, 2048 to 4095, ...) at most 1152 rows name the same one
- attn_gain: float32 [2048], P('col'), may hold values from 0.5 to 1.5
- query_gain: float32 [128], replicated, may hold values from 0.5 to 1.5
- key_gain: float32 [128], replicated, may hold values from 0.5 to 1.5
- query_weight: float32 [2048, 2048], P('row', 'col'), may hold values from -0.125 to 0.125
- key_weight: float32 [2048, 2048], P('row', 'col'), may hold values from -0.125 to 0.125
- value_weight: float32 [2048, 2048], P('row', 'col'), may hold values from -0.125 to 0.125
- out_weight: float32 [2048, 2048], P('col', 'row'), may hold values from -1.5 to 1.5
- moe_gain: float32 [2048], P('col'), may hold values from 0.5 to 1.5
- router: float32 [2048, 16], P('row'), may hold values from -0.0625 to 0.0625
- gate_weight: float32 [16, 2048, 1024], P('col', 'row'), may hold values from -0.125 to 0.125
- up_weight: float32 [16, 2048, 1024], P('col', 'row'), may hold values from -0.125 to 0.125
- down_weight: float32 [16, 1024, 2048], P('col', None, 'row'), may hold values from -0.75 to 0.75
- cotangent: bfloat16 [16384, 2048], P('row', 'col'), may hold values from -6 to 6
Outputs:
- output: bfloat16 [16384, 2048], P('row', 'col')
- input_grad: float32 [16384, 2048], P('row', 'col')
- attn_gain_grad: float32 [2048], P('col')
- query_gain_grad: float32 [128], replicated
- key_gain_grad: float32 [128], replicated
- query_grad: float32 [2048, 2048], P('row', 'col')
- key_grad: float32 [2048, 2048], P('row', 'col')
- value_grad: float32 [2048, 2048], P('row', 'col')
- out_grad: float32 [2048, 2048], P('col', 'row')
- moe_gain_grad: float32 [2048], P('col')
- router_grad: float32 [2048, 16], P('row')
- gate_grad: float32 [16, 2048, 1024], P('col', 'row')
- up_grad: float32 [16, 2048, 1024], P('col', 'row')
- down_grad: float32 [16, 1024, 2048], P('col', None, 'row')
Inputs may be any that keep to these rules, and one draw needn't show every extreme that they name: `routes`: each token names 8 different experts. Among the 2048 tokens of each aligned block of rows (the tokens of one index of row), no expert is named by more than 1152 tokens, and in some block one expert is named by exactly 1152.
All inputs are finite; a program needn't handle non-finite values.
Results may differ from a plain program's by a relative error of at most 0.02.
Values may be sent and summed in bfloat16 or wider, within the bound.
No kernel may reach another device: no remote copies, remote signals or barrier semaphores. Data moves between devices by JAX's collectives and lax.ppermute only.
A program may use at most 512 MiB of HBM per device.

v0:
```python
import functools
import math

import jax
import jax.numpy as jnp
from jax import lax
from jax.experimental import pallas as pl
from jax.experimental.pallas import tpu as pltpu
from jax.sharding import Mesh, PartitionSpec as P

D = 2048
HD = 128
EXPERTS = 16
SEQ_LEN = 1024
CAP = 1152

BLOCK = 128
WINDOW = 144
EDGE = 16
TILE = 384
COST_SHARE = 50
EXPERT_WIDE, EXPERT_UNROLL = 512, 2
GRAD_WIDE, GRAD_UNROLL = 512, 1

epsilon = 1e-06
rope_base = 10000.0
masked_score = -1e30

F32 = jnp.float32
BF16 = jnp.bfloat16
ANY = pl.ANY
VMEM_LIMIT = 56 * 1024 * 1024


def dot_of(a, b, da, db):
    return lax.dot_general(a, b, (((da,), (db,)), ((), ())), preferred_element_type=F32)


def params(*semantics):
    return pltpu.CompilerParams(
        vmem_limit_bytes=VMEM_LIMIT, dimension_semantics=semantics or None
    )


def cost(flops, bytes_accessed, transcendentals=0):
    return pl.CostEstimate(
        flops=int(flops) // COST_SHARE,
        bytes_accessed=int(bytes_accessed) // COST_SHARE,
        transcendentals=int(transcendentals) // COST_SHARE,
    )


def turn(values, cosine, sine):
    return values * cosine + pltpu.roll(values, HD // 2, 1) * sine


def attend_forward_kernel(
    live_ref, q_ref, k_ref, v_ref, cos_ref, sin_ref, qg_ref, kg_ref, mix_ref, ql_ref, kl_ref, vl_ref
):
    live = live_ref[0]
    cosine = cos_ref[...]
    sine = sin_ref[...]

    def normed(values, gain):
        inverse = lax.rsqrt(jnp.mean(values * values, axis=1, keepdims=True) + epsilon)
        return turn(values * inverse * gain, cosine, sine).astype(BF16)

    ql_ref[...] = normed(q_ref[...], qg_ref[...])
    kl_ref[...] = normed(k_ref[...], kg_ref[...])
    vl_ref[...] = v_ref[...].astype(BF16)
    keys = kl_ref[...]
    values = vl_ref[...]
    rows = 256
    place = lax.broadcasted_iota(jnp.int32, (rows, SEQ_LEN), 1)
    for part in range(SEQ_LEN // rows):
        here = pl.ds(part * rows, rows)
        scores = dot_of(ql_ref[here, :], keys, 1, 1) * (1.0 / math.sqrt(HD))
        scores = jnp.where(place < live, scores, masked_score)
        top = jnp.max(scores, axis=1, keepdims=True)
        shifted = jnp.exp(scores - top)
        total = jnp.sum(shifted, axis=1, keepdims=True)
        probs = (shifted * (1.0 / total)).astype(BF16)
        mix_ref[here, :] = dot_of(probs, values, 1, 0).astype(BF16)


def attend_forward(seq, live, qkv, tables, query_gain, key_gain, heads):
    width = heads * HD

    def pick(offset):
        return pl.BlockSpec((SEQ_LEN, HD), lambda h, live, o=offset: (seq, o + h))

    def whole(shape):
        return pl.BlockSpec(shape, lambda h, live: (0, 0))

    out = pl.BlockSpec((SEQ_LEN, HD), lambda h, live: (0, h))
    return pl.pallas_call(
        attend_forward_kernel,
        grid_spec=pltpu.PrefetchScalarGridSpec(
            num_scalar_prefetch=1,
            grid=(heads,),
            in_specs=[
                pick(0),
                pick(heads),
                pick(2 * heads),
                whole((SEQ_LEN, HD)),
                whole((SEQ_LEN, HD)),
                whole((1, HD)),
                whole((1, HD)),
            ],
            out_specs=[out] * 4,
        ),
        out_shape=[jax.ShapeDtypeStruct((SEQ_LEN, width), BF16)] * 4,
        compiler_params=params("arbitrary"),
        cost_estimate=cost(
            heads * 8 * SEQ_LEN * SEQ_LEN * HD, 20 * SEQ_LEN * width, heads * SEQ_LEN * SEQ_LEN
        ),
        name="attend_forward",
    )(live, qkv, qkv, qkv, tables[0], tables[1], query_gain, key_gain)


def attend_backward_kernel(
    live_ref,
    ql_ref,
    kl_ref,
    vl_ref,
    do_ref,
    q_ref,
    k_ref,
    cos_ref,
    sin_ref,
    qg_ref,
    kg_ref,
    qc_ref,
    kc_ref,
    vc_ref,
    qpart_ref,
    kpart_ref,
    inner_ref,
    dq_ref,
    dk_ref,
    dv_ref,
):
    head = pl.program_id(0)
    live = live_ref[0]
    scale = 1.0 / math.sqrt(HD)
    keys = kl_ref[...]
    values = vl_ref[...]
    rows = 256
    place = lax.broadcasted_iota(jnp.int32, (SEQ_LEN, rows), 0)
    for part in range(SEQ_LEN // rows):
        here = pl.ds(part * rows, rows)
        queries = ql_ref[here, :]
        incoming = do_ref[here, :]
        scores = dot_of(keys, queries, 1, 1) * scale
        scores = jnp.where(place < live, scores, masked_score)
        top = jnp.max(scores, axis=0, keepdims=True)
        shifted = jnp.exp(scores - top)
        total = jnp.sum(shifted, axis=0, keepdims=True)
        probs = shifted * (1.0 / total)
        dv = dot_of(probs.astype(BF16), incoming, 1, 0)
        probs_cot = dot_of(values, incoming, 1, 1)
        weighted = probs * probs_cot
        centre = jnp.sum(weighted, axis=0, keepdims=True)
        raw = ((weighted - probs * centre) * scale).astype(BF16)
        dk = dot_of(raw, queries, 1, 0)
        dq_ref[here, :] = dot_of(raw, keys, 0, 0)
        if part == 0:
            dv_ref[...] = dv
            dk_ref[...] = dk
        else:
            dv_ref[...] += dv
            dk_ref[...] += dk
    cosine = cos_ref[...]
    sine = -sin_ref[...]

    def back(values, gain, rotated_cot):
        incoming = turn(rotated_cot, cosine, sine)
        inverse = lax.rsqrt(jnp.mean(values * values, axis=1, keepdims=True) + epsilon)
        scaled = incoming * gain
        inner = jnp.mean(scaled * values, axis=1, keepdims=True)
        grad = inverse * scaled - values * (inverse * inverse * inverse * inner)
        part = jnp.sum(incoming * values * inverse, axis=0, keepdims=True)
        return grad.astype(BF16), part, jnp.sum(grad * values, axis=1, keepdims=True)

    qc_ref[...], qpart, inner = back(q_ref[...], qg_ref[...], dq_ref[...])
    kc_ref[...], kpart, key_inner = back(k_ref[...], kg_ref[...], dk_ref[...])
    vc_ref[...] = dv_ref[...].astype(BF16)
    inner += key_inner
    inner += jnp.sum(dv_ref[...] * values.astype(F32), axis=1, keepdims=True)

    @pl.when(head == 0)
    def _():
        qpart_ref[...] = qpart
        kpart_ref[...] = kpart
        inner_ref[...] = inner

    @pl.when(head > 0)
    def _():
        qpart_ref[...] += qpart
        kpart_ref[...] += kpart
        inner_ref[...] += inner


def attend_backward(seq, live, lows, mixture_cot, qkv, tables, query_gain, key_gain, heads):
    width = heads * HD
    block = pl.BlockSpec((SEQ_LEN, HD), lambda h, live: (0, h))

    def pick(offset):
        return pl.BlockSpec((SEQ_LEN, HD), lambda h, live, o=offset: (seq, o + h))

    def whole(shape):
        return pl.BlockSpec(shape, lambda h, live: (0, 0))

    return pl.pallas_call(
        attend_backward_kernel,
        grid_spec=pltpu.PrefetchScalarGridSpec(
            num_scalar_prefetch=1,
            grid=(heads,),
            in_specs=[block] * 4
            + [
                pick(0),
                pick(heads),
                whole((SEQ_LEN, HD)),
                whole((SEQ_LEN, HD)),
                whole((1, HD)),
                whole((1, HD)),
            ],
            out_specs=[block] * 3 + [whole((1, HD))] * 2 + [whole((SEQ_LEN, 1))],
            scratch_shapes=[pltpu.VMEM((SEQ_LEN, HD), F32)] * 3,
        ),
        out_shape=[jax.ShapeDtypeStruct((SEQ_LEN, width), BF16)] * 3
        + [jax.ShapeDtypeStruct((1, HD), F32)] * 2
        + [jax.ShapeDtypeStruct((SEQ_LEN, 1), F32)],
        compiler_params=params("arbitrary"),
        cost_estimate=cost(
            heads * 20 * SEQ_LEN * SEQ_LEN * HD, 24 * SEQ_LEN * width, heads * SEQ_LEN * SEQ_LEN
        ),
        name="attend_backward",
    )(live, *lows, mixture_cot, qkv, qkv, tables[0], tables[1], query_gain, key_gain)


def compact_kernel(start_ref, where_ref, pos_ref, source_ref, *outs):
    group, groups = pl.program_id(0), pl.num_programs(0)
    row_of = lax.broadcasted_iota(jnp.int32, (WINDOW, BLOCK), 0)
    for out in outs:
        out[...] = jnp.zeros_like(out)
    for number in range(source_ref.shape[1] // BLOCK):
        here = slice(number * BLOCK, (number + 1) * BLOCK)
        for expert, out in enumerate(outs):
            start = pl.multiple_of(start_ref[expert * groups + group, number], EDGE)
            place = pos_ref[expert, 0, :, here]
            choice = jnp.where(row_of + start == place, 1.0, 0.0).astype(BF16)
            rows = dot_of(choice, source_ref[0, here, :], 1, 0)
            out[pl.ds(start, WINDOW), :] += rows.astype(BF16)


def compact(starts, where, pos_row, source, groups, cols):
    tokens, width = source.shape[1:]
    count = pos_row.shape[0] // groups
    return pl.pallas_call(
        compact_kernel,
        grid_spec=pltpu.PrefetchScalarGridSpec(
            num_scalar_prefetch=2,
            grid=(groups, cols),
            in_specs=[
                pl.BlockSpec((count, 1, 1, tokens), lambda q, j, s, w: (0, q, 0, 0)),
                pl.BlockSpec(
                    (1, tokens, width), lambda q, j, s, w: ((w[0] ^ q) * cols + j, 0, 0)
                ),
            ],
            out_specs=[pl.BlockSpec((CAP, width), lambda q, j, s, w: (q, j))] * count,
        ),
        out_shape=[jax.ShapeDtypeStruct((groups * CAP, cols * width), BF16)] * count,
        compiler_params=params("arbitrary", "arbitrary"),
        cost_estimate=cost(
            count * groups * cols * 2 * tokens * WINDOW * width * 2,
            groups * cols * 2 * width * (tokens + count * CAP),
        ),
        name="compact",
    )(starts, where, pos_row.reshape(count, groups, 1, tokens), source)


def compact_scalars_kernel(start_ref, pos_ref, *refs):
    count = len(refs) // 2
    group = pl.program_id(0)
    row_of = lax.broadcasted_iota(jnp.int32, (WINDOW, BLOCK), 0)
    for number in range(count):
        refs[count + number][...] = jnp.zeros_like(refs[count + number])
    for number in range(pos_ref.shape[2] // BLOCK):
        start = pl.multiple_of(start_ref[group, number], EDGE)
        here = slice(number * BLOCK, (number + 1) * BLOCK)
        choice = row_of + start == pos_ref[0, :, here]
        for source, out in zip(refs[:count], refs[count:]):
            picked = jnp.sum(jnp.where(choice, source[0, :, here], 0.0), axis=1, keepdims=True)
            out[pl.ds(start, WINDOW), :] += picked


def compact_scalars(starts, pos_row, sources):
    groups, _, tokens = pos_row.shape
    block = pl.BlockSpec((1, 1, tokens), lambda q, s: (q, 0, 0))
    return pl.pallas_call(
        compact_scalars_kernel,
        grid_spec=pltpu.PrefetchScalarGridSpec(
            num_scalar_prefetch=1,
            grid=(groups,),
            in_specs=[block] * (1 + len(sources)),
            out_specs=[pl.BlockSpec((CAP, 1), lambda q, s: (q, 0))] * len(sources),
        ),
        out_shape=[jax.ShapeDtypeStruct((groups * CAP, 1), F32)] * len(sources),
        compiler_params=params("arbitrary"),
        cost_estimate=cost(0, 4 * groups * CAP * 128 * len(sources)),
        name="compact_scalars",
    )(starts, pos_row, *sources)


def expand_scalars_kernel(start_ref, pos_ref, *refs):
    count = len(refs) // 2
    group = pl.program_id(0)
    row_of = lax.broadcasted_iota(jnp.int32, (WINDOW, BLOCK), 0)
    for number in range(pos_ref.shape[2] // BLOCK):
        start = pl.multiple_of(start_ref[group, number], EDGE)
        here = slice(number * BLOCK, (number + 1) * BLOCK)
        choice = row_of + start == pos_ref[0, :, here]
        for source, out in zip(refs[:count], refs[count:]):
            held = source[pl.ds(start, WINDOW), :]
            out[0, :, here] = jnp.sum(jnp.where(choice, held, 0.0), axis=0, keepdims=True)


def expand_scalars(starts, pos_row, sources):
    groups, _, tokens = pos_row.shape
    block = pl.BlockSpec((1, 1, tokens), lambda q, s: (q, 0, 0))
    return pl.pallas_call(
        expand_scalars_kernel,
        grid_spec=pltpu.PrefetchScalarGridSpec(
            num_scalar_prefetch=1,
            grid=(groups,),
            in_specs=[block] + [pl.BlockSpec((CAP, 1), lambda q, s: (q, 0))] * len(sources),
            out_specs=[block] * len(sources),
        ),
        out_shape=[jax.ShapeDtypeStruct((groups, 1, tokens), F32)] * len(sources),
        compiler_params=params("arbitrary"),
        cost_estimate=cost(0, 4 * groups * CAP * 128 * len(sources)),
        name="expand_scalars",
    )(starts, pos_row, *sources)


def expand_kernel(sizes, count, start_ref, where_ref, pos_ref, *refs):
    group, groups = pl.program_id(0), pl.num_programs(0)
    sides = len(refs) // (count + len(sizes))
    sources, outs = refs[: count * sides], refs[count * sides :]
    column_of = lax.broadcasted_iota(jnp.int32, (BLOCK, WINDOW), 1)
    number = 0
    for part, size in enumerate(sizes):
        for step in range(size // BLOCK):
            totals = [None] * sides
            for expert in range(count):
                start = pl.multiple_of(start_ref[expert * groups + group, number], EDGE)
                place = pos_ref[expert, 0, number * BLOCK : (number + 1) * BLOCK, :]
                choice = jnp.where(column_of + start == place, 1.0, 0.0).astype(BF16)
                for side in range(sides):
                    held = sources[expert * sides + side][pl.ds(start, WINDOW), :]
                    rows = dot_of(choice, held, 1, 0)
                    totals[side] = rows if totals[side] is None else totals[side] + rows
            here = slice(step * BLOCK, (step + 1) * BLOCK)
            for side in range(sides):
                outs[part * sides + side][0, 0, here, :] = totals[side].astype(BF16)
            number += 1


def expand(starts, where, pos_col, sources, sizes, groups, cols):
    width = sources[0].shape[1] // cols
    tokens = sum(sizes)
    count = len(sources)

    def side(odd):
        return pl.BlockSpec((CAP, width), lambda q, j, s, w: (q, w[1] ^ (2 * j + odd)))

    outs = pl.pallas_call(
        functools.partial(expand_kernel, sizes, count),
        grid_spec=pltpu.PrefetchScalarGridSpec(
            num_scalar_prefetch=2,
            grid=(groups, cols // 2),
            in_specs=[pl.BlockSpec((count, 1, tokens, 1), lambda q, j, s, w: (0, q, 0, 0))]
            + [side(0), side(1)] * count,
            out_specs=[
                pl.BlockSpec((1, 1, size, width), lambda q, j, s, w: (q, j, 0, 0))
                for size in sizes
                for _ in range(2)
            ],
        ),
        out_shape=[
            jax.ShapeDtypeStruct((groups, cols // 2, size, width), BF16)
            for size in sizes
            for _ in range(2)
        ],
        compiler_params=params("arbitrary", "arbitrary"),
        cost_estimate=cost(
            4 * count * groups * cols * tokens * WINDOW * width,
            groups * cols * width * (2 * tokens + 2 * count * CAP),
        ),
        name="expand",
    )(
        starts,
        where,
        pos_col.reshape(count, groups, tokens, 1),
        *[source for source in sources for _ in range(2)],
    )
    return list(zip(outs[::2], outs[1::2]))


def expand_all(starts, where, pos_col, sources, groups, cols):
    width = sources[0].shape[1] // cols
    tokens = pos_col.shape[1]
    count = len(sources)
    return pl.pallas_call(
        functools.partial(expand_kernel, [tokens], count),
        grid_spec=pltpu.PrefetchScalarGridSpec(
            num_scalar_prefetch=2,
            grid=(groups, cols),
            in_specs=[pl.BlockSpec((count, 1, tokens, 1), lambda q, j, s, w: (0, q, 0, 0))]
            + [pl.BlockSpec((CAP, width), lambda q, j, s, w: (q, j))] * count,
            out_specs=pl.BlockSpec((1, 1, tokens, width), lambda q, j, s, w: (w[0] ^ q, j, 0, 0)),
        ),
        out_shape=jax.ShapeDtypeStruct((groups, cols, tokens, width), BF16),
        compiler_params=params("arbitrary", "arbitrary"),
        cost_estimate=cost(
            4 * count * groups * cols * tokens * WINDOW * width,
            groups * cols * width * (2 * tokens + 2 * count * CAP),
        ),
        name="expand_all",
    )(starts, where, pos_col.reshape(count, groups, tokens, 1), *sources)


def pack_kernel(where_ref, gate_ref, up_ref, down_ref, out_ref):
    hidden = gate_ref.shape[2]
    out_ref[0, :, :hidden] = gate_ref[0].astype(BF16)
    out_ref[0, :, hidden : 2 * hidden] = up_ref[0].astype(BF16)
    out_ref[0, :, 2 * hidden :] = down_ref[0].T.astype(BF16)


def pack_weights(where, gate, up, down, each):
    experts, depth, hidden = gate.shape

    def pick(shape):
        return pl.BlockSpec(shape, lambda q, w: ((w[0] ^ (q // each)) * each + q % each, 0, 0))

    return pl.pallas_call(
        pack_kernel,
        grid_spec=pltpu.PrefetchScalarGridSpec(
            num_scalar_prefetch=1,
            grid=(experts,),
            in_specs=[pick((1, depth, hidden)), pick((1, depth, hidden)), pick((1, hidden, depth))],
            out_specs=pl.BlockSpec((1, depth, 3 * hidden), lambda q, w: (q, 0, 0)),
        ),
        out_shape=jax.ShapeDtypeStruct((experts, depth, 3 * hidden), BF16),
        compiler_params=params("arbitrary"),
        cost_estimate=cost(0, 18 * experts * depth * hidden),
        name="pack_weights",
    )(where, gate, up, down)


def unpack_kernel(where_ref, *refs):
    sources, (gate_ref, up_ref, down_ref) = refs[:-3], refs[-3:]
    hidden = gate_ref.shape[2]
    for number, source in enumerate(sources):

        @pl.when(pl.program_id(0) == number)
        def _(source=source):
            gate_ref[0] = source[:, :hidden].astype(F32)
            up_ref[0] = source[:, hidden : 2 * hidden].astype(F32)
            down_ref[0] = source[:, 2 * hidden :].astype(F32).T


def unpack_grads(where, sources, each):
    count = len(sources)
    depth, wide = sources[0].shape
    hidden = wide // 3

    def pick(shape):
        return pl.BlockSpec(shape, lambda q, w: ((w[0] ^ (q // each)) * each + q % each, 0, 0))

    shapes = [(count, depth, hidden), (count, depth, hidden), (count, hidden, depth)]
    return pl.pallas_call(
        unpack_kernel,
        grid_spec=pltpu.PrefetchScalarGridSpec(
            num_scalar_prefetch=1,
            grid=(count,),
            in_specs=[pl.BlockSpec((depth, wide), lambda q, w: (0, 0))] * count,
            out_specs=[pick((1,) + shape[1:]) for shape in shapes],
        ),
        out_shape=[jax.ShapeDtypeStruct(shape, F32) for shape in shapes],
        compiler_params=params("arbitrary"),
        cost_estimate=cost(0, 18 * count * depth * hidden),
        name="unpack_grads",
    )(where, *sources)


def expert_kernel(count, hidden, row_ref, x_ref, m_ref, gate_ref, scale_ref, *refs):
    pieces = refs[:count]
    rows_ref, pre_ref, act_ref, cot_ref, inner_ref, result_ref, held, sems = refs[count:]
    depth = pieces[0].shape[0]

    @pl.when(pl.program_id(0) == 0)
    def _():
        copies = []
        for number, piece in enumerate(pieces):
            place = pl.ds(pl.multiple_of(row_ref[number] * depth, depth), depth)
            copies.append(pltpu.make_async_copy(piece, held.at[place, :], sems.at[number]))
        for copy in copies:
            copy.start()
        for copy in copies:
            copy.wait()

    gate = gate_ref[...]
    scale = scale_ref[...]
    wide = EXPERT_WIDE
    cot_ref[...] = jnp.zeros_like(cot_ref)
    inner_ref[...] = jnp.zeros_like(inner_ref)

    @pl.loop(0, hidden // wide, unroll=EXPERT_UNROLL)
    def _(step):
        first = pl.multiple_of(step * wide, wide)
        gate_pre = dot_of(x_ref[...], held[:, pl.ds(first, wide)], 1, 0) * scale
        up_pre = dot_of(x_ref[...], held[:, pl.ds(hidden + first, wide)], 1, 0) * scale
        back = dot_of(m_ref[...], held[:, pl.ds(2 * hidden + first, wide)], 1, 0)
        squash = 1.0 / (1.0 + jnp.exp(-gate_pre))
        silu = gate_pre * squash
        active = silu * up_pre
        cot_ref[...] += jnp.sum(active.astype(BF16).astype(F32) * back, axis=1, keepdims=True)
        act_ref[:, pl.ds(first, wide)] = (active * gate).astype(BF16)
        back = back * gate
        slope = squash * (1.0 + gate_pre * (1.0 - squash))
        gate_cot = back * up_pre * slope
        up_cot = back * silu
        inner_ref[...] += jnp.sum(gate_cot * gate_pre + up_cot * up_pre, axis=1, keepdims=True)
        pre_ref[:, pl.ds(first, wide)] = (gate_cot * scale).astype(BF16)
        pre_ref[:, pl.ds(hidden + first, wide)] = (up_cot * scale).astype(BF16)

    @pl.loop(0, held.shape[0] // wide, unroll=EXPERT_UNROLL)
    def _(step):
        first = pl.multiple_of(step * wide, wide)
        here = pl.ds(first, wide)
        rows_ref[:, here] = dot_of(pre_ref[...], held[here, : 2 * hidden], 1, 1).astype(BF16)
        result_ref[:, here] = dot_of(act_ref[...], held[here, 2 * hidden :], 1, 1).astype(BF16)


def expert_step(row_numbers, x, m, gate, scale, pieces):
    total, wide = x.shape
    hidden = pieces[0].shape[1] // 3
    count = len(pieces)

    def tile(columns):
        return pl.BlockSpec((TILE, columns), lambda i, r: (i, 0))

    return pl.pallas_call(
        functools.partial(expert_kernel, count, hidden),
        grid_spec=pltpu.PrefetchScalarGridSpec(
            num_scalar_prefetch=1,
            grid=(total // TILE,),
            in_specs=[tile(wide), tile(wide), tile(1), tile(1)]
            + [pl.BlockSpec(memory_space=ANY)] * count,
            out_specs=[tile(wide), tile(2 * hidden), tile(hidden), tile(1), tile(1), tile(wide)],
            scratch_shapes=[
                pltpu.VMEM((wide, 3 * hidden), BF16),
                pltpu.SemaphoreType.DMA((count,)),
            ],
        ),
        out_shape=[
            jax.ShapeDtypeStruct((total, wide), BF16),
            jax.ShapeDtypeStruct((total, 2 * hidden), BF16),
            jax.ShapeDtypeStruct((total, hidden), BF16),
            jax.ShapeDtypeStruct((total, 1), F32),
            jax.ShapeDtypeStruct((total, 1), F32),
            jax.ShapeDtypeStruct((total, wide), BF16),
        ],
        compiler_params=params("arbitrary"),
        cost_estimate=cost(
            2 * total * wide * hidden * 6, 2 * total * (4 * wide + 3 * hidden), total * hidden
        ),
        name="expert_step",
    )(row_numbers, x, m, gate, scale, *pieces)


def weight_grad_kernel(mids, place_ref, x_ref, m_ref, pre_ref, act_ref, out_ref, turned_ref):
    wide = GRAD_WIDE
    first = pre_ref.shape[1]
    depth = x_ref.shape[1] // mids
    turned_ref[0] = x_ref[...].T
    turned_ref[1] = m_ref[...].T
    mid = place_ref[place_ref.shape[0] - 1]

    def put(grad, here):
        for number in range(mids):
            block = grad[number * depth : (number + 1) * depth].astype(BF16)
            out_ref[0, number ^ mid, 0, :, here] = block

    @pl.loop(0, first // wide, unroll=GRAD_UNROLL)
    def _(step):
        here = pl.ds(pl.multiple_of(step * wide, wide), wide)
        put(dot_of(turned_ref[0], pre_ref[:, here], 1, 0), here)

    @pl.loop(0, act_ref.shape[1] // wide, unroll=GRAD_UNROLL)
    def _(step):
        here = pl.ds(pl.multiple_of(step * wide, wide), wide)
        there = pl.ds(pl.multiple_of(first + step * wide, wide), wide)
        put(dot_of(turned_ref[1], act_ref[:, here], 1, 0), there)


def weight_grads(places, x, m, pre, act, depth, groups, mids, high):
    total = x.shape[0]
    wide = pre.shape[1] + act.shape[1]

    def column(first):
        return pl.BlockSpec((total, mids * depth), lambda f, h, r: (0, r[first + f * high + h]))

    def whole(array):
        return pl.BlockSpec(array.shape, lambda f, h, r: (0, 0), pipeline_mode=pl.Buffered(1))

    return pl.pallas_call(
        functools.partial(weight_grad_kernel, mids),
        grid_spec=pltpu.PrefetchScalarGridSpec(
            num_scalar_prefetch=1,
            grid=(groups, high),
            in_specs=[column(0), column(groups * high), whole(pre), whole(act)],
            out_specs=pl.BlockSpec(
                (1, mids, 1, depth, wide), lambda f, h, r: (f, 0, h, 0, 0)
            ),
            scratch_shapes=[pltpu.VMEM((2, mids * depth, total), BF16)],
        ),
        out_shape=jax.ShapeDtypeStruct((groups, mids, high, depth, wide), BF16),
        compiler_params=params("arbitrary", "arbitrary"),
        cost_estimate=cost(
            2 * total * depth * groups * mids * high * wide,
            2 * total * (2 * depth * groups * mids * high + wide),
        ),
        name="weight_grads",
    )(places, x, m, pre, act)


def bits_of(size):
    return [1 << n for n in range(size.bit_length() - 1)]


def swap(values, axis, bit):
    size = lax.axis_size(axis) if isinstance(axis, str) else math.prod(map(lax.axis_size, axis))
    return lax.ppermute(values, axis, [(n, n ^ bit) for n in range(size)])


class Flow:
    def __init__(self, steps):
        self.steps = steps
        self.result = None
        self.sends = next(steps)

    def advance(self, got):
        try:
            self.sends = self.steps.send(got)
        except StopIteration as stop:
            self.sends = None
            self.result = stop.value

    def step(self, count=1):
        for _ in range(count):
            if self.sends is not None:
                self.advance([swap(*send) for send in self.sends])
        return self

    def finish(self):
        while self.sends is not None:
            self.step()
        return self.result

    def holds(self):
        return self.result if self.sends is None else [send[0] for send in self.sends]

    def replace(self, arrays):
        if self.sends is None:
            self.result = arrays
        else:
            self.sends = [(array, *send[1:]) for array, send in zip(arrays, self.sends)]


def stage(live, flows=(), work=(), sync=()):
    flows = [flow for flow in flows if flow.sends is not None]
    got = [[swap(*send) for send in flow.sends] for flow in flows]
    done = [each() for each in work]
    held = [flow.holds() for flow in sync]
    got, done, held, kept = lax.optimization_barrier((got, done, held, dict(live)))
    live.update(kept)
    for flow, arrays in zip(flows, got):
        flow.advance(arrays)
    for flow, arrays in zip(sync, held):
        flow.replace(arrays)
    return done


def spread_steps(values, axis, bits):
    blocks = {0: values}
    for bit in bits:
        places = sorted(blocks)
        got = yield [(blocks[place], axis, bit) for place in places]
        blocks.update({place | bit: block for place, block in zip(places, got)})
    return [blocks[place] for place in sorted(blocks)]


def spread_rows_steps(values, row_bits, strides):
    held = values[None]
    places = [0]
    for axis, bit in row_bits:
        (got,) = yield [(held, axis, bit)]
        held = jnp.concatenate([held, got], axis=0)
        places += [place | (bit * strides[axis]) for place in places]
    return jnp.stack([held[places.index(place)] for place in range(len(places))])


def spread_cube_steps(values, groups, cols):
    held = values[None]
    for axis, bits in (("lo", bits_of(groups)), ("col", bits_of(cols))):
        for bit in bits:
            (got,) = yield [(held, axis, bit)]
            held = jnp.concatenate([held, got], axis=0)
    return jnp.swapaxes(held.reshape((cols, groups) + values.shape), 0, 1)


def col_reduce_steps(blocks, cols):
    held = dict(enumerate(blocks))
    for bit in bits_of(cols):
        away = [place for place in sorted(held) if place & bit]
        (got,) = yield [(jnp.stack([held[place].astype(BF16) for place in away]), "col", bit)]
        held = {
            place & ~bit: held[place & ~bit] + got[number].astype(F32)
            for number, place in enumerate(away)
        }
    return held[0]


def total_steps(values, axes):
    for axis in axes:
        size = math.prod(map(lax.axis_size, axis))
        got = yield [(values, axis, place) for place in range(1, size)]
        values = values + sum(got)
    return values


def row_reduce_steps(grads, groups, mids, high):
    names = [("lo", bit) for bit in reversed(bits_of(groups))]
    names += [("mid", bit) for bit in reversed(bits_of(mids))]
    names += [("hi", bit) for bit in reversed(bits_of(high))]
    grads = grads.reshape((2,) * len(names) + grads.shape[3:])
    half = grads.shape[-1] // 2
    held = []
    for number in range(2):
        order = [name for name in names if name[0] != "hi"][:: 1 if number else -1]
        order += [name for name in reversed(names) if name[0] == "hi"]
        held.append((grads[..., number * half : (number + 1) * half], names, order))
    for step in range(len(names)):
        sends, rest = [], []
        for array, left, order in held:
            name = order[step]
            axis = left.index(name)
            away = 0 if name[0] == "lo" else 1
            sends.append((lax.index_in_dim(array, away, axis, False).astype(BF16), *name))
            kept = lax.index_in_dim(array, 1 - away, axis, False)
            rest.append((kept, [other for other in left if other != name], order))
        got = yield sends
        held = [
            (kept.astype(F32) + more.astype(F32), left, order)
            for (kept, left, order), more in zip(rest, got)
        ]
    return jnp.concatenate([array for array, _, _ in held], axis=1)


def links_of(groups, cols):
    return [("col", bit) for bit in bits_of(cols)[1:]] + [("lo", bit) for bit in bits_of(groups)]


def turned(links, number):
    number %= len(links)
    return links[number:] + links[:number]


def reduce_steps(parts, groups, cols):
    links = links_of(groups, cols)
    got = yield [(away, "col", 1) for _, away in parts]
    held = []
    for number, (keep, _) in enumerate(parts):
        shape = (2,) * len(links) + keep.shape[2:]
        names = [("lo", bit) for bit in reversed(bits_of(groups))]
        names += [("col", bit) for bit in reversed(bits_of(cols)[1:])]
        held.append((keep.reshape(shape), got[number].reshape(shape), names))
    for step in range(len(links)):
        sends, rest = [], []
        for number, (keep, more, names) in enumerate(held):
            link = turned(links, number)[step]
            axis = names.index(link)

            def half(place):
                total = lax.index_in_dim(keep, place, axis, False).astype(F32)
                return total + lax.index_in_dim(more, place, axis, False).astype(F32)

            sends.append((half(1).astype(BF16), *link))
            kept = half(0)
            rest.append(
                (
                    kept if step + 1 == len(links) else kept.astype(BF16),
                    [name for name in names if name != link],
                )
            )
        got = yield sends
        held = [(keep, more, names) for (keep, names), more in zip(rest, got)]
    return jnp.concatenate([keep.astype(F32) + more.astype(F32) for keep, more, _ in held], axis=0)


def part_sizes(tokens, count):
    whole = tokens // BLOCK
    return [BLOCK * ((whole + count - 1 - n) // count) for n in range(count)]


def expert_weight_steps(piece, far, bits):
    if far:
        (piece,) = yield [(piece, "lo", far)]
    held = {(): piece}
    fresh = [()]
    while True:
        ways = [
            (place, number)
            for place in fresh
            for number in range(place[-1] + 1 if place else 0, len(bits))
        ]
        if not ways:
            return held
        got = yield [(held[place], *bits[number]) for place, number in ways]
        fresh = [place + (number,) for place, number in ways]
        held.update(zip(fresh, got))


def expert_grad_steps(blocks, far, bits):
    for number in reversed(range(len(bits))):
        half = blocks.shape[0] // 2
        (got,) = yield [(blocks[half:], *bits[number])]
        blocks = blocks[:half].astype(F32) + got.astype(F32)
        if number or far:
            blocks = blocks.astype(BF16)
    total = blocks[0]
    if far:
        (total,) = yield [(total, "lo", far)]
    return total


def per_device(
    hidden_in,
    lengths,
    routes,
    attn_gain,
    query_gain,
    key_gain,
    query_weight,
    key_weight,
    value_weight,
    out_weight,
    moe_gain,
    router,
    gate_weight,
    up_weight,
    down_weight,
    cotangent,
):
    tok_rows, width = hidden_in.shape
    cols = lax.axis_size("col")
    groups = lax.axis_size("lo")
    high = lax.axis_size("hi")
    mids = lax.axis_size("mid")
    col = lax.axis_index("col")
    lo = lax.axis_index("lo")
    hi = lax.axis_index("hi")
    mid = lax.axis_index("mid")
    row = (hi * groups + lo) * mids + mid
    where = jnp.stack([lo, col])
    heads = width // HD
    seqs = lengths.shape[0]
    depth = gate_weight.shape[1]
    each = gate_weight.shape[0] // groups
    cube = ("lo", "col")
    rows_axes = ("hi", "lo", "mid")
    strides = {"hi": groups * mids, "lo": mids, "mid": 1}
    seq_rows = [slice(s * SEQ_LEN, (s + 1) * SEQ_LEN) for s in range(seqs)]
    links = links_of(groups, cols)
    col_bits = list(reversed(bits_of(cols)))
    hi_bits = [("hi", bit) for bit in bits_of(high)]
    mid_bits = [("mid", bit) for bit in bits_of(mids)]
    row_bits = hi_bits + [("lo", bit) for bit in bits_of(groups)] + mid_bits
    far_bits = hi_bits + mid_bits
    live = {}

    def row_of_set(place, far):
        other = row ^ (far * mids)
        for number in place:
            axis, bit = far_bits[number]
            other = other ^ (bit * strides[axis])
        return other

    hidden_flow = Flow(spread_steps(hidden_in, "col", col_bits))
    gain_flow = Flow(spread_steps(attn_gain, "col", col_bits))
    routes_flow = Flow(spread_steps(routes.T, "lo", bits_of(groups)))
    router_flow = Flow(spread_rows_steps(router.T.astype(BF16), row_bits, strides))
    out_flow = Flow(spread_rows_steps(out_weight.T.astype(BF16), row_bits, strides))
    qkv_local = jnp.concatenate([query_weight, key_weight, value_weight], axis=1).astype(BF16)
    qkv_full = lax.all_gather(qkv_local, rows_axes, axis=0, tiled=True)
    live_key = jnp.arange(SEQ_LEN)[None, :] < lengths[:, None]
    out_cot = jnp.where(live_key.reshape(tok_rows, 1), cotangent, jnp.zeros_like(cotangent))
    packed = pack_weights(where, gate_weight, up_weight, down_weight, each)
    units = [(expert, far) for expert in range(each) for far in range(groups)]
    live["packed"] = packed

    def rotary_tables():
        places = jnp.arange(SEQ_LEN).astype(F32)
        powers = jnp.arange(HD // 2).astype(F32) * (2.0 / HD)
        angles = places[:, None] * jnp.exp(-powers * math.log(rope_base))[None, :]
        cosine, sine = jnp.cos(angles), jnp.sin(angles)
        return (
            jnp.concatenate([cosine, cosine], axis=1),
            jnp.concatenate([-sine, sine], axis=1),
        )

    live["out_cot"] = out_cot
    (tables,) = stage(
        live,
        [hidden_flow, gain_flow, routes_flow, router_flow, out_flow],
        [rotary_tables],
    )

    hidden = hidden_in.astype(F32)

    def norm_attn():
        blocks = hidden_flow.finish()
        gains = gain_flow.finish()
        square = sum(jnp.sum(jnp.square(block.astype(F32)), axis=1) for block in blocks)
        inverse = lax.rsqrt(square / D + epsilon)[:, None]
        normed = jnp.zeros((tok_rows, D), BF16)
        for place, (block, gain) in enumerate(zip(blocks, gains)):
            piece = (block.astype(F32) * inverse * gain).astype(BF16)
            normed = lax.dynamic_update_slice_in_dim(normed, piece, (col ^ place) * width, 1)
        return normed, inverse

    def routing():
        rel = jnp.stack(routes_flow.finish())
        named = jnp.any(rel[:, :, None, :] == jnp.arange(EXPERTS)[None, None, :, None], axis=1)
        first = (col * groups + lo) * each
        member = lax.dynamic_slice_in_dim(named, first, each, 1)
        member = jnp.swapaxes(member, 0, 1).reshape(each * groups, tok_rows)
        count = member.astype(jnp.int32)
        rank = jnp.cumsum(count, axis=1) - count
        pos = jnp.where(member, rank, -(1 << 20))
        starts = jnp.minimum(rank[:, ::BLOCK] // EDGE * EDGE, CAP - WINDOW)
        return named, starts, pos[:, None, :], pos[:, :, None]

    live["qkv_full"] = qkv_full
    ((live["normed_attn"], attn_inverse),) = stage(live, [router_flow, out_flow], [norm_attn])
    weight_flows = {}

    def start_weights(expert):
        for far in range(groups):
            weight_flows[expert, far] = Flow(
                expert_weight_steps(live["packed"][far * each + expert], far, far_bits)
            )

    start_weights(0)
    moe_cot = lax.all_gather(live["out_cot"], cube, axis=0, tiled=False)
    hidden_blocks = hidden_flow.result
    query_scale, key_scale = query_gain[None, :], key_gain[None, :]

    def attend(s):
        return attend_forward(
            s, lengths[s : s + 1], live["qkv"], tables, query_scale, key_scale, heads
        )

    def project_and_attend():
        live["qkv"] = dot_of(live["normed_attn"], live["qkv_full"], 1, 0)
        return attend(0)

    firsts = [weight_flows[0, far] for far in range(1, groups)]
    (first_seq,) = stage(live, [router_flow, out_flow], [project_and_attend])
    for expert in range(1, each):
        start_weights(expert)
    seconds = [weight_flows[unit] for unit in units if unit[0] == 1]
    named, starts, pos_row, pos_col = routing()

    span = width // depth

    def col_rows(blocks, place, axis):
        first = (col ^ place) * span
        return jnp.concatenate(
            [
                lax.dynamic_index_in_dim(blocks, (first + n) ^ row, 0, False)
                for n in range(span)
            ],
            axis=axis,
        )

    out_spread = out_flow.finish()
    out_rel = jnp.concatenate([col_rows(out_spread, place, 0) for place in range(cols)], axis=0)
    router_rows = col_rows(router_flow.finish(), 0, 1)

    def branch(mixture):
        partial = dot_of(mixture, out_rel, 1, 1)
        blocks = [partial[:, n * width : (n + 1) * width] for n in range(cols)]
        return Flow(col_reduce_steps(blocks, cols)).finish()

    def attend_rest():
        outs = [first_seq]
        sums = [branch(first_seq[0])]
        for s in range(1, seqs):
            outs.append(attend(s))
            sums.append(branch(outs[s][0]))
        return outs, sums

    ((attended, branches),) = stage(live, [weight_flows[0, 0]] + firsts, [attend_rest])
    middle = hidden + jnp.concatenate(branches, axis=0)
    live["scaled_rows"] = (middle * moe_gain).astype(BF16)
    scaled_rows = live["scaled_rows"]
    moe_in = lax.all_gather(scaled_rows, cube, axis=0, tiled=False)
    square = jnp.sum(middle * middle, axis=1)[None, :]
    stat = jnp.concatenate([dot_of(router_rows, scaled_rows, 1, 1), square], axis=0)
    stat_flow = Flow(spread_cube_steps(stat, groups, cols))
    stage(live, [stat_flow], sync=[weight_flows[0, 0]] + firsts + seconds)
    (live["cot_rows"],) = stage(
        live,
        [stat_flow, weight_flows[0, 0]] + firsts,
        [lambda: compact(starts, where, pos_row, moe_cot, groups, cols)],
    )
    stage(live, [stat_flow] + firsts + seconds[1:])
    stat = stat_flow.finish()

    stat = jnp.sum(stat, axis=1)
    moe_inverse = lax.rsqrt(stat[:, EXPERTS] / D + epsilon)
    all_logits = stat[:, :EXPERTS] * moe_inverse[:, None, :]
    logits = jnp.where(named, all_logits, masked_score)
    shifted = jnp.where(named, jnp.exp(logits - jnp.max(logits, axis=1, keepdims=True)), 0.0)
    gates = shifted / jnp.sum(shifted, axis=1, keepdims=True)
    own_gate = lax.dynamic_slice_in_dim(gates, (col * groups + lo) * each, each, 1)
    own_gate = jnp.swapaxes(own_gate, 0, 1).reshape(each * groups, 1, tok_rows)
    row_gate, row_scale = compact_scalars(
        starts, pos_row, (own_gate, jnp.tile(moe_inverse, (each, 1))[:, None, :])
    )
    total_rows = groups * CAP

    live["moe_rows"] = compact(starts, where, pos_row, moe_in, groups, cols)

    def run_expert(expert):
        pieces, row_numbers = [], []
        for far in range(groups):
            for place, piece in weight_flows[expert, far].finish().items():
                pieces.append(piece)
                row_numbers.append(row_of_set(place, far))
        here = slice(expert * total_rows, (expert + 1) * total_rows)
        return expert_step(
            jnp.stack(row_numbers),
            live["moe_rows"][expert],
            live["cot_rows"][expert],
            row_gate[here],
            row_scale[here],
            pieces,
        )

    blocks_here = [
        (hi ^ above) * groups + (lo ^ far)
        for far in reversed(range(groups))
        for above in range(high)
    ]
    grad_places = jnp.stack(blocks_here + blocks_here + [mid])
    grad_flows = {}

    def start_grads(expert, outs):
        grads = weight_grads(
            grad_places,
            live["moe_rows"][expert],
            live["cot_rows"][expert],
            outs[1],
            outs[2],
            depth,
            groups,
            mids,
            high,
        )
        return grads.reshape((groups, mids * high) + grads.shape[3:])

    def grad_flow(expert, grads):
        for number, far in enumerate(reversed(range(groups))):
            grad_flows[expert, far] = Flow(expert_grad_steps(grads[number], far, far_bits))

    def running():
        return list(grad_flows.values())

    ran = []
    for expert in range(each):
        others = [flow for (number, _), flow in weight_flows.items() if number > expert]
        (outs,) = stage(
            live,
            others + running()[:1],
            [functools.partial(run_expert, expert)],
            sync=running()[1:],
        )
        ran.append(outs)
        if expert + 1 < each:
            (grads,) = stage(live, others, [functools.partial(start_grads, expert, outs)])
            grad_flow(expert, grads)
    early = running()
    live["result"] = [outs[5] for outs in ran]
    last = ran[-1]
    gate_cot = jnp.concatenate([outs[3] for outs in ran], axis=0)
    row_inner = jnp.concatenate([outs[4] for outs in ran], axis=0)
    sizes = part_sizes(tok_rows, len(links))
    live["scalars"] = (gate_cot, row_inner)
    (rows_parts,) = stage(
        live,
        [],
        [
            lambda: expand(
                starts, where, pos_col, [outs[0] for outs in ran], sizes, groups, cols
            )
        ],
    )
    gate_cot, row_inner = expand_scalars(starts, pos_row, live.pop("scalars"))
    gate_cot = gate_cot.reshape(each, groups, tok_rows)
    row_inner = jnp.sum(row_inner.reshape(each, groups, tok_rows), axis=0)[None]
    scalars = jnp.concatenate([gate_cot, row_inner], axis=0)
    scalars = scalars.reshape((each + 1) * groups, tok_rows)
    scalar_flow = Flow(spread_cube_steps(scalars, groups, cols))
    moe_in_flow = Flow(reduce_steps(rows_parts, groups, cols))
    (grads,) = stage(
        live,
        [moe_in_flow, scalar_flow] + early,
        [functools.partial(start_grads, each - 1, last)],
    )
    grad_flow(each - 1, grads)
    late = running()[len(early) :]
    scalar_flow.finish()
    (branch_parts,) = stage(
        live,
        [moe_in_flow] + early[1:] + late[:1],
        [lambda: expand_all(starts, where, pos_col, live["result"], groups, cols)],
        sync=[scalar_flow],
    )
    live["moe_branch"] = branch_parts.reshape(groups * cols, tok_rows, width)
    while moe_in_flow.sends is not None:
        stage(live, [moe_in_flow], sync=early + late)
    scalar_all = scalar_flow.finish().reshape(groups, cols, each + 1, groups, tok_rows)
    scalar_all = jnp.stack([scalar_all[place, :, :, place] for place in range(groups)])
    by_expert = jnp.stack(
        [
            ((lo ^ (number // each % groups)) * cols + (col ^ (number // (each * groups)))) * each
            + number % each
            for number in range(EXPERTS)
        ]
    )
    gate_cot = jnp.take(scalar_all[:, :, :each].reshape(EXPERTS, tok_rows), by_expert, axis=0)
    my_gates, my_logits = gates[0], all_logits[0]
    logit_cot = my_gates * (gate_cot - jnp.sum(my_gates * gate_cot, axis=0, keepdims=True))
    inner = jnp.sum(scalar_all[:, :, each], axis=(0, 1)) + jnp.sum(logit_cot * my_logits, axis=0)
    scaled_logit = (logit_cot * moe_inverse[0][None, :]).astype(BF16)
    logit_cot = logit_cot.astype(BF16)
    my_inverse = moe_inverse[0][:, None]

    back = moe_in_flow.finish() + my_inverse * dot_of(logit_cot, router_rows, 0, 0)
    middle_cot = (
        out_cot.astype(F32)
        + back * moe_gain
        - middle * (my_inverse * my_inverse * (inner[:, None] / D))
    )
    cot_flow = Flow(spread_steps(middle_cot.astype(BF16), "col", col_bits))
    router_part, moe_gain_part = stage(
        live,
        [cot_flow] + early[:1],
        [
            lambda: dot_of(scaled_logit, scaled_rows, 1, 0),
            lambda: jnp.sum(back * middle, axis=0)[None],
        ],
    )
    cot_blocks = cot_flow.finish()
    moe_branch = lax.psum_scatter(
        live.pop("moe_branch"), cube, scatter_dimension=0, tiled=True
    )[0]

    cot_all = jnp.concatenate(cot_blocks, axis=1)

    def attend_back(s):
        mixture_cot = dot_of(cot_all[seq_rows[s]], out_rel, 1, 0).astype(BF16)
        *cots, query_part, key_part, token_inner = attend_backward(
            s,
            lengths[s : s + 1],
            attended[s][1:],
            mixture_cot,
            live["qkv"],
            tables,
            query_scale,
            key_scale,
            heads,
        )
        cots = jnp.concatenate(cots, axis=1)
        return cots, query_part, key_part, token_inner[:, 0]

    qkv_rel = jnp.concatenate(
        [
            lax.dynamic_slice_in_dim(live["qkv_full"], (col ^ place) * width, width, 0)
            for place in range(cols)
        ],
        axis=0,
    )
    mixture = jnp.concatenate([outs[0] for outs in attended], axis=0)
    live.update(qkv_rel=qkv_rel, mixture=mixture, cot_all=cot_all)
    done = stage(
        live,
        late,
        [functools.partial(attend_back, s) for s in range(seqs)],
    )
    share = width // (mids * depth)
    cot_places = [((n // share) ^ col) * share + n % share for n in blocks_here]

    live["qkv_cot"] = jnp.concatenate([outs[0] for outs in done], axis=0)

    def projection_grads():
        grads = weight_grads(
            jnp.stack(blocks_here + cot_places + [mid]),
            live["normed_attn"],
            live["cot_all"],
            live["qkv_cot"],
            live["mixture"],
            depth,
            groups,
            mids,
            high,
        )
        return grads

    def widen(blocks):
        full = jnp.zeros((blocks[0].shape[0], D), F32)
        for place, block in enumerate(blocks):
            full = lax.dynamic_update_slice_in_dim(full, block, (col ^ place) * width, 1)
        return full

    def input_cots():
        partial = dot_of(live["qkv_cot"], live["qkv_rel"], 1, 1)
        backs = [partial[:, n * width : (n + 1) * width] for n in range(cols)]
        attn_flow = Flow(col_reduce_steps(backs, cols)).step(len(bits_of(cols)) - 1)
        attn_gain_parts = [
            jnp.sum(part * (block.astype(F32) * attn_inverse), axis=0)[None]
            for part, block in zip(backs, hidden_blocks)
        ]
        token_inner = jnp.concatenate([outs[3] for outs in done], axis=0)
        inner_flow = Flow(total_steps(token_inner, [("col",)]))
        inner_flow.finish()
        query_part = sum(outs[1] for outs in done)
        key_part = sum(outs[2] for outs in done)
        head_parts = jnp.concatenate([query_part, key_part], 1)
        small = jnp.concatenate(
            [
                widen([router_part]),
                widen([moe_gain_part]),
                widen(attn_gain_parts),
                jnp.pad(head_parts, ((0, 0), (0, D - 2 * HD))),
            ],
            axis=0,
        )
        small_flow = Flow(total_steps(small, [("col",), ("lo", "mid"), ("hi",)])).step()
        flows.extend([attn_flow, inner_flow, small_flow])
        return [flow.holds() for flow in flows]

    flows = []
    late[1].step()
    (held,) = stage(live, [], [input_cots])
    for flow, arrays in zip(flows, held):
        flow.replace(arrays)
    attn_flow, inner_flow, small_flow = flows
    attn_flow.step()
    (grads,) = stage(live, [], [projection_grads])
    qkv_flow = Flow(row_reduce_steps(grads, groups, mids, high))
    stage(live, [qkv_flow, small_flow], sync=[attn_flow, late[1]])
    live["moe_branch"] = moe_branch

    def input_sums():
        return (
            middle_cot
            + attn_inverse * (attn_flow.finish() * attn_gain)
            - hidden * (attn_inverse * attn_inverse * (inner_flow.finish()[:, None] / D))
        )

    (input_grad,) = stage(live, [qkv_flow, small_flow] + early[:1] + late, [input_sums])
    flows = [qkv_flow, small_flow] + early + late
    while any(flow.sends is not None for flow in flows):
        stage(live, flows)
    moe_branch = live["moe_branch"]
    weight_sum = qkv_flow.finish()
    out_sum = weight_sum[:, 3 * width :]
    small = small_flow.finish()

    output = (middle + moe_branch.astype(F32)).astype(BF16)
    gate_grad, up_grad, down_grad = unpack_grads(
        where,
        [grad_flows[expert, far].finish() for far in range(groups) for expert in range(each)],
        each,
    )
    own = lax.dynamic_slice_in_dim(small, col * width, width, 1)
    router_grad = lax.dynamic_slice_in_dim(small[:EXPERTS], row * depth, depth, 1).T
    return (
        output,
        input_grad,
        own[EXPERTS + 1],
        small[EXPERTS + 2, :HD],
        small[EXPERTS + 2, HD : 2 * HD],
        weight_sum[:, :width],
        weight_sum[:, width : 2 * width],
        weight_sum[:, 2 * width : 3 * width],
        out_sum.T,
        own[EXPERTS],
        router_grad,
        gate_grad,
        up_grad,
        down_grad,
    )


def solution(mesh):
    row_count, col_count = mesh.shape["row"], mesh.shape["col"]
    groups = 2
    between = EXPERTS // col_count // groups
    shape = (row_count // (groups * between), groups, between, col_count)
    inner = Mesh(mesh.devices.reshape(shape), ("hi", "lo", "mid", "col"))
    row = ("hi", "lo", "mid")
    return jax.shard_map(
        per_device,
        mesh=inner,
        in_specs=(
            P(row, "col"),
            P(row),
            P(row, None),
            P("col"),
            P(),
            P(),
            P(row, "col"),
            P(row, "col"),
            P(row, "col"),
            P("col", row),
            P("col"),
            P(row, None),
            P("col", row, None),
            P("col", row, None),
            P("col", None, row),
            P(row, "col"),
        ),
        out_specs=(
            P(row, "col"),
            P(row, "col"),
            P("col"),
            P(),
            P(),
            P(row, "col"),
            P(row, "col"),
            P(row, "col"),
            P("col", row),
            P("col"),
            P(row, None),
            P("col", row, None),
            P("col", row, None),
            P("col", None, row),
        ),
        check_vma=False,
    )
```

profile of v0, /device:TPU:0, one launch (start us, length us, event | category | flops | bytes accessed | tf_op | source)
XLA Modules:
  0.0 1415.5 jit_solution(11216816112481502175)
XLA Ops:
  25.8 34.6 %collective-permute-done.1 = f32[512]{0:T(512)S(1)} collective-permute-done((f32[512]{0:T(512)S(1)}, f32[512]{0:T(512)S(1)}, u32[]{:S(2)}, u32[]{:S(2)}) %collective-permute-start.1) | collective-permute-done | bytes 2080 | tf_op jit(solution)/shard_map/ppermute | solution.py:646
  62.9 8.3 pack_weights.1
  97.6 21.0 %collective-permute-done.5 = bf16[2,16,256]{2,1,0:T(8,128)(2,1)S(1)} collective-permute-done((bf16[2,16,256]{2,1,0:T(8,128)(2,1)S(1)}, bf16[2,16,256]{2,1,0:T(8,128)(2,1)S(1)}, u32[]{:S(2)}, u32[]{:S(2)}) %collective-permute-start.5) | collective-permute-done | bytes 16416 | tf_op jit(solution)/shard_map/ppermute | solution.py:646
  118.6 8.7 all-gather.6.cloned.1.call-done
  130.8 19.3 %fusion.107.q_ref.k_ref.v_ref = f32[2048,1536]{1,0:T(8,128)} fusion(bf16[2048,2048]{1,0:T(8,128)(2,1)} %fusion.40.x_ref, bf16[2048,1536]{1,0:T(8,128)(2,1)} %all-gather.6.cloned.1.call-done), kind=kOutput, calls=%fused_computation.307 | convolution fusion | flops 12884901888 | bytes 27262976 | tf_op jit(solution)/shard_map/dot_general | solution.py:36
  150.1 18.0 %attend_forward.2 = (bf16[1024,512]{1,0:T(8,128)(2,1)}, bf16[1024,512]{1,0:T(8,128)(2,1)}, bf16[1024,512]{1,0:T(8,128)(2,1)}, bf16[1024,512]{1,0:T(8,128)(2,1)}) custom-call(s32[1]{0:T(128)} %get-tuple-element.667.live_ref, f32[2048,1536]{1,0:T(8,128)} %fusion.107.q_ref.k_ref.v_ref, f32[2048,1536]{1,0:T(8,128)} %fusion.107.q_ref.k_ref.v_ref, ...), custom_call_target="tpu_custom_call" | custom-call | flops 85899344 | bytes 209715 | tf_op jit(solution)/shard_map/attend_forward/pallas_call | solution.py:96
  168.2 18.3 %attend_forward.3 = (bf16[1024,512]{1,0:T(8,128)(2,1)}, bf16[1024,512]{1,0:T(8,128)(2,1)}, bf16[1024,512]{1,0:T(8,128)(2,1)}, bf16[1024,512]{1,0:T(8,128)(2,1)}) custom-call(s32[1]{0:T(128)} %get-tuple-element.666.live_ref, f32[2048,1536]{1,0:T(8,128)} %fusion.107.q_ref.k_ref.v_ref, f32[2048,1536]{1,0:T(8,128)} %fusion.107.q_ref.k_ref.v_ref, ...), custom_call_target="tpu_custom_call" | custom-call | flops 85899344 | bytes 209715 | tf_op jit(solution)/shard_map/attend_forward/pallas_call | solution.py:96
  204.3 28.7 %collective-permute-done.19 = bf16[1,1024,512]{2,1,0:T(8,128)(2,1)S(1)} collective-permute-done((bf16[1,1024,512]{2,1,0:T(8,128)(2,1)S(1)}, bf16[1,1024,512]{2,1,0:T(8,128)(2,1)S(1)}, u32[]{:S(2)}, u32[]{:S(2)}) %collective-permute-start.19) | collective-permute-done | bytes 1048608 | tf_op jit(solution)/shard_map/ppermute | solution.py:646
  233.6 21.8 %collective-permute-done.17 = bf16[1,1024,512]{2,1,0:T(8,128)(2,1)S(1)} collective-permute-done((bf16[1,1024,512]{2,1,0:T(8,128)(2,1)S(1)}, bf16[1,1024,512]{2,1,0:T(8,128)(2,1)S(1)}, u32[]{:S(2)}, u32[]{:S(2)}) %collective-permute-start.17) | collective-permute-done | bytes 1048608 | tf_op jit(solution)/shard_map/ppermute | solution.py:646
  255.9 12.9 collective-permute-done.11.refs_1_
  270.0 6.8 collective-permute-done.13.refs_4_
  298.9 19.1 %compact.2 = (bf16[2304,2048]{1,0:T(8,128)(2,1)}, bf16[2304,2048]{1,0:T(8,128)(2,1)}) custom-call(s32[4,16]{1,0:T(4,128)} %fusion.90.start_ref, s32[2]{0:T(128)} %pad_add_fusion.1.where_ref, s32[2,2,1,2048]{3,2,1,0:T(1,128)} %select_n.151.pos_ref, bf16[8,2048,512]{2,1,0:T(8,128)(2,1)} %bitcast.350), custom_call_target="tpu_custom_call" | custom-call | flops 193273536 | bytes 713031 | tf_op jit(solution)/shard_map/compact/pallas_call | solution.py:260
  318.0 10.6 collective-permute-done.24.refs_3_
  328.6 35.2 %collective-permute-done.25.refs_5_ = bf16[256,3072]{1,0:T(8,128)(2,1)} collective-permute-done((bf16[256,3072]{1,0:T(8,128)(2,1)}, bf16[256,3072]{1,0:T(8,128)(2,1)}, u32[]{:S(2)}, u32[]{:S(2)}) %collective-permute-start.25) | collective-permute-done | bytes 1572896 | tf_op jit(solution)/shard_map/ppermute | solution.py:646
  375.4 56.5 %collective-permute-done.29.refs_4_ = bf16[256,3072]{1,0:T(8,128)(2,1)} collective-permute-done((bf16[256,3072]{1,0:T(8,128)(2,1)}, bf16[256,3072]{1,0:T(8,128)(2,1)}, u32[]{:S(2)}, u32[]{:S(2)}) %collective-permute-start.29) | collective-permute-done | bytes 1572896 | tf_op jit(solution)/shard_map/ppermute | solution.py:646
  442.8 5.7 compact_scalars.1
  453.4 17.4 %all-gather.10.cloned.1.call-done = bf16[16384,512]{1,0:T(8,128)(2,1)} async-done(((bf16[2048,512]{1,0:T(8,128)(2,1)}), bf16[16384,512]{1,0:T(8,128)(2,1)}) %all-gather.10.cloned.1.call-update) | async-done | bytes 16777232 | tf_op jit(solution)/shard_map/all_gather | solution.py:1021
  470.8 19.1 %compact.3 = (bf16[2304,2048]{1,0:T(8,128)(2,1)}, bf16[2304,2048]{1,0:T(8,128)(2,1)}) custom-call(s32[4,16]{1,0:T(4,128)} %fusion.90.start_ref, s32[2]{0:T(128)} %pad_add_fusion.1.where_ref, s32[2,2,1,2048]{3,2,1,0:T(1,128)} %select_n.151.pos_ref, bf16[8,2048,512]{2,1,0:T(8,128)(2,1)} %bitcast.351), custom_call_target="tpu_custom_call" | custom-call | flops 193273536 | bytes 713031 | tf_op jit(solution)/shard_map/compact/pallas_call | solution.py:260
  489.9 77.8 %expert_step.2 = (bf16[2304,2048]{1,0:T(8,128)(2,1)}, bf16[2304,2048]{1,0:T(8,128)(2,1)}, bf16[2304,1024]{1,0:T(8,128)(2,1)}, f32[2304,1]{1,0:T(8,128)}, f32[2304,1]{1,0:T(8,128)}, /*index=5*/bf16[2304,2048]{1,0:T(8,128)(2,1)}) custom-call(s32[8]{0:T(128)} %stack.260.row_ref, bf16[2304,2048]{1,0:T(8,128)(2,1)} %get-tuple-element.360.x_ref, ...), custom_call_target="tpu_custom_call" | custom-call | flops 1159641216 | bytes 1038090 | tf_op jit(solution)/shard_map/expert_step/pallas_call | solution.py:555
  570.5 47.5 %weight_grads.3 = bf16[2,2,2,256,3072]{4,3,2,1,0:T(8,128)(2,1)} custom-call(s32[9]{0:T(128)} %stack.261.place_ref, bf16[2304,2048]{1,0:T(8,128)(2,1)} %get-tuple-element.360.x_ref, bf16[2304,2048]{1,0:T(8,128)(2,1)} %get-tuple-element.361.m_ref, bf16[2304,2048]{1,0:T(8,128)(2,1)} %get-tuple-element.362.pre_ref, bf16[2304,1024]{1,0:T(8,128)(2,1)} %get-tuple-element.363.act_ref), custom_call_target="tpu_custom_call" | custom-call | flops 579820608 | bytes 660602 | tf_op jit(solution)/shard_map/weight_grads/pallas_call | solution.py:619
  618.0 20.5 %collective-permute-done.33.refs_7_ = bf16[256,3072]{1,0:T(8,128)(2,1)} collective-permute-done((bf16[256,3072]{1,0:T(8,128)(2,1)}, bf16[256,3072]{1,0:T(8,128)(2,1)}, u32[]{:S(2)}, u32[]{:S(2)}) %collective-permute-start.33) | collective-permute-done | bytes 1572896 | tf_op jit(solution)/shard_map/ppermute | solution.py:646
  638.5 6.0 slice_bitcast_fusion.2
  652.2 77.6 %expert_step.3 = (bf16[2304,2048]{1,0:T(8,128)(2,1)}, bf16[2304,2048]{1,0:T(8,128)(2,1)}, bf16[2304,1024]{1,0:T(8,128)(2,1)}, f32[2304,1]{1,0:T(8,128)}, f32[2304,1]{1,0:T(8,128)}, /*index=5*/bf16[2304,2048]{1,0:T(8,128)(2,1)}) custom-call(s32[8]{0:T(128)} %stack.260.row_ref, bf16[2304,2048]{1,0:T(8,128)(2,1)} %get-tuple-element.410.x_ref, ...), custom_call_target="tpu_custom_call" | custom-call | flops 1159641216 | bytes 1038090 | tf_op jit(solution)/shard_map/expert_step/pallas_call | solution.py:555
  733.1 18.7 %expand.1 = (bf16[2,2,1024,512]{3,2,1,0:T(8,128)(2,1)}, bf16[2,2,1024,512]{3,2,1,0:T(8,128)(2,1)}, bf16[2,2,1024,512]{3,2,1,0:T(8,128)(2,1)}, bf16[2,2,1024,512]{3,2,1,0:T(8,128)(2,1)}) custom-call(s32[4,16]{1,0:T(4,128)} %fusion.90.start_ref, s32[2]{0:T(128)} %pad_add_fusion.1.where_ref, s32[2,2,2048,1]{3,2,1,0:T(8,128)} %copy.111.pos_ref, ...), custom_call_target="tpu_custom_call" | custom-call | flops 193273536 | bytes 713031 | tf_op jit(solution)/shard_map/expand/pallas_call | solution.py:378
  767.1 6.2 expand_scalars.1
  779.9 47.5 %weight_grads.4 = bf16[2,2,2,256,3072]{4,3,2,1,0:T(8,128)(2,1)} custom-call(s32[9]{0:T(128)} %stack.261.place_ref, bf16[2304,2048]{1,0:T(8,128)(2,1)} %get-tuple-element.410.x_ref, bf16[2304,2048]{1,0:T(8,128)(2,1)} %get-tuple-element.411.m_ref, bf16[2304,2048]{1,0:T(8,128)(2,1)} %get-tuple-element.412.pre_ref, bf16[2304,1024]{1,0:T(8,128)(2,1)} %get-tuple-element.413.act_ref), custom_call_target="tpu_custom_call" | custom-call | flops 579820608 | bytes 660602 | tf_op jit(solution)/shard_map/weight_grads/pallas_call | solution.py:619
  831.0 6.2 slice_bitcast_fusion
  865.7 20.6 %expand_all.1 = bf16[2,4,2048,512]{3,2,1,0:T(8,128)(2,1)} custom-call(s32[4,16]{1,0:T(4,128)} %fusion.90.start_ref, s32[2]{0:T(128)} %pad_add_fusion.1.where_ref, s32[2,2,2048,1]{3,2,1,0:T(8,128)} %copy.111.pos_ref, bf16[2304,2048]{1,0:T(8,128)(2,1)} %get-tuple-element.424.refs_0_, bf16[2304,2048]{1,0:T(8,128)(2,1)} %get-tuple-element.425.refs_1_), custom_call_target="tpu_custom_call" | custom-call | flops 193273536 | bytes 713031 | tf_op jit(solution)/shard_map/expand_all/pallas_call | solution.py:415
  886.2 15.3 %collective-permute-done.45 = f32[4,6,2048]{2,1,0:T(8,128)} collective-permute-done((f32[4,6,2048]{2,1,0:T(8,128)}, f32[4,6,2048]{2,1,0:T(8,128)}, u32[]{:S(2)}, u32[]{:S(2)}) %collective-permute-start.45) | collective-permute-done | bytes 196640 | tf_op jit(solution)/shard_map/ppermute | solution.py:646
  902.8 24.9 %collective-permute-done.42 = bf16[1,256,3072]{2,1,0:T(8,128)(2,1)} collective-permute-done((bf16[1,256,3072]{2,1,0:T(8,128)(2,1)}, bf16[1,256,3072]{2,1,0:T(8,128)(2,1)}, u32[]{:S(2)}, u32[]{:S(2)}) %collective-permute-start.42) | collective-permute-done | bytes 1572896 | tf_op jit(solution)/shard_map/ppermute | solution.py:646
  944.5 16.6 %collective-permute-done.47 = bf16[1024,512]{1,0:T(8,128)(2,1)S(1)} collective-permute-done((bf16[1024,512]{1,0:T(8,128)(2,1)S(1)}, bf16[1024,512]{1,0:T(8,128)(2,1)S(1)}, u32[]{:S(2)}, u32[]{:S(2)}) %collective-permute-start.47) | collective-permute-done | bytes 1048608 | tf_op jit(solution)/shard_map/ppermute | solution.py:646
  976.4 31.9 %collective-permute-done.52.refs_2_ = bf16[256,3072]{1,0:T(8,128)(2,1)S(1)} collective-permute-done((bf16[256,3072]{1,0:T(8,128)(2,1)S(1)}, bf16[256,3072]{1,0:T(8,128)(2,1)S(1)}, u32[]{:S(2)}, u32[]{:S(2)}) %collective-permute-start.52) | collective-permute-done | bytes 1572896 | tf_op jit(solution)/shard_map/ppermute | solution.py:646
  1008.3 11.2 collective-permute-done.51
  1041.7 32.0 %attend_backward.3 = (bf16[1024,512]{1,0:T(8,128)(2,1)}, bf16[1024,512]{1,0:T(8,128)(2,1)}, bf16[1024,512]{1,0:T(8,128)(2,1)}, f32[1,128]{1,0:T(1,128)}, f32[1,128]{1,0:T(1,128)}, /*index=5*/f32[1024,1]{1,0:T(8,128)}) custom-call(s32[1]{0:T(128)} %get-tuple-element.666.live_ref, bf16[1024,512]{1,0:T(8,128)(2,1)} %get-tuple-element.460.ql_ref, ...), custom_call_target="tpu_custom_call" | custom-call | flops 214748368 | bytes 251658 | tf_op jit(solution)/shard_map/attend_backward/pallas_call | solution.py:214
  1075.0 6.3 fusion.58.do_ref
  1081.3 32.1 %attend_backward.2 = (bf16[1024,512]{1,0:T(8,128)(2,1)}, bf16[1024,512]{1,0:T(8,128)(2,1)}, bf16[1024,512]{1,0:T(8,128)(2,1)}, f32[1,128]{1,0:T(1,128)}, f32[1,128]{1,0:T(1,128)}, /*index=5*/f32[1024,1]{1,0:T(8,128)}) custom-call(s32[1]{0:T(128)} %get-tuple-element.667.live_ref, bf16[1024,512]{1,0:T(8,128)(2,1)} %get-tuple-element.441.ql_ref, ...), custom_call_target="tpu_custom_call" | custom-call | flops 214748368 | bytes 251658 | tf_op jit(solution)/shard_map/attend_backward/pallas_call | solution.py:214
  1121.2 19.2 %fusion.108 = f32[2048,2048]{1,0:T(8,128)S(1)} fusion(bf16[2048,1536]{1,0:T(8,128)(2,1)} %constant_dynamic-update-slice_fusion.10.pre_ref, bf16[2048,1536]{1,0:T(8,128)(2,1)} %pad_maximum_fusion.1), kind=kOutput, calls=%fused_computation.308 | convolution fusion | flops 12884901888 | bytes 29360128 | tf_op jit(solution)/shard_map/dot_general | solution.py:36
  1140.4 5.8 copy-done.9
  1172.3 10.5 collective-permute-done.59
  1182.8 8.4 collective-permute-done.60
  1194.9 32.0 %weight_grads.5 = bf16[2,2,2,256,2048]{4,3,2,1,0:T(8,128)(2,1)} custom-call(s32[9]{0:T(128)} %stack.247.place_ref, bf16[2048,2048]{1,0:T(8,128)(2,1)} %fusion.40.x_ref, bf16[2048,2048]{1,0:T(8,128)(2,1)} %copy-done.11, bf16[2048,1536]{1,0:T(8,128)(2,1)} %constant_dynamic-update-slice_fusion.10.pre_ref, bf16[2048,512]{1,0:T(8,128)(2,1)} %pad_maximum_fusion.7.act_ref), custom_call_target="tpu_custom_call" | custom-call | flops 343597376 | bytes 503316 | tf_op jit(solution)/shard_map/weight_grads/pallas_call | solution.py:619
  1238.4 15.9 %collective-permute-done.66 = bf16[1,2048,512]{2,1,0:T(8,128)(2,1)} collective-permute-done((bf16[1,2048,512]{2,1,0:T(8,128)(2,1)S(1)}, bf16[1,2048,512]{2,1,0:T(8,128)(2,1)}, u32[]{:S(2)}, u32[]{:S(2)}) %collective-permute-start.66) | collective-permute-done | bytes 2097184 | tf_op jit(solution)/shard_map/ppermute | solution.py:646
  1258.6 22.5 %collective-permute-done.63 = f32[19,2048]{1,0:T(8,128)} collective-permute-done((f32[19,2048]{1,0:T(8,128)}, f32[19,2048]{1,0:T(8,128)}, u32[]{:S(2)}, u32[]{:S(2)}) %collective-permute-start.63) | collective-permute-done | bytes 155680 | tf_op jit(solution)/shard_map/ppermute | solution.py:646
  1304.3 22.7 %collective-permute-done.71.refs_3_ = bf16[256,3072]{1,0:T(8,128)(2,1)S(1)} collective-permute-done((bf16[256,3072]{1,0:T(8,128)(2,1)S(1)}, bf16[256,3072]{1,0:T(8,128)(2,1)S(1)}, u32[]{:S(2)}, u32[]{:S(2)}) %collective-permute-start.71) | collective-permute-done | bytes 1572896 | tf_op jit(solution)/shard_map/ppermute | solution.py:646
  1328.2 18.7 %collective-permute-done.70 = f32[19,2048]{1,0:T(8,128)S(1)} collective-permute-done((f32[19,2048]{1,0:T(8,128)S(1)}, f32[19,2048]{1,0:T(8,128)S(1)}, u32[]{:S(2)}, u32[]{:S(2)}) %collective-permute-start.70) | collective-permute-done | bytes 155680 | tf_op jit(solution)/shard_map/ppermute | solution.py:646
  1359.3 9.6 unpack_grads.1
  1370.6 19.7 %collective-permute-done.73 = bf16[256,1024]{1,0:T(8,128)(2,1)S(1)} collective-permute-done((bf16[256,1024]{1,0:T(8,128)(2,1)}, bf16[256,1024]{1,0:T(8,128)(2,1)S(1)}, u32[]{:S(2)}, u32[]{:S(2)}) %collective-permute-start.73) | collective-permute-done | bytes 524320 | tf_op jit(solution)/shard_map/ppermute | solution.py:646
  1390.3 10.1 collective-permute-done.72
  (536 shorter events, 343.5 us)
Async XLA Ops:
  7.2 120.1 %all-gather.6.cloned.1.call-start = ((), (), s32[]{:S(2)}) async-start(), calls=%async_computation.1 | async-start | bytes 7077888 | tf_op jit(solution)/shard_map/all_gather | solution.py:908
  11.6 287.3 %all-gather.8.cloned.1.call-start = ((), (), s32[]{:S(2)}) async-start(), calls=%async_computation.3 | async-start | bytes 18874368 | tf_op jit(solution)/shard_map/all_gather | solution.py:968
  11.7 59.5 %collective-permute-start = (bf16[2048,512]{1,0:T(8,128)(2,1)S(1)}, bf16[2048,512]{1,0:T(8,128)(2,1)}, u32[]{:S(2)}, u32[]{:S(2)}) collective-permute-start(bf16[2048,512]{1,0:T(8,128)(2,1)S(1)} %copy-done), channel_id=1, source_target_pairs={{0,2},{1,3},{2,0},{3,1},{4,6},{5,7},{6,4},{7,5},{8,10},{9,11},{10,... | collective-permute-start | bytes 6291464 | tf_op jit(solution)/shard_map/ppermute | solution.py:646
  14.7 60.7 %collective-permute-start.7 = (bf16[2048,512]{1,0:T(8,128)(2,1)S(1)}, bf16[2048,512]{1,0:T(8,128)(2,1)}, u32[]{:S(2)}, u32[]{:S(2)}) collective-permute-start(bf16[2048,512]{1,0:T(8,128)(2,1)S(1)} %copy-done), channel_id=1, source_target_pairs={{0,1},{1,0},{2,3},{3,2},{4,5},{5,4},{6,7},{7,6},{8,9},{9,8},{10,11... | collective-permute-start | bytes 6291464 | tf_op jit(solution)/shard_map/ppermute | solution.py:646
  15.4 55.8 %collective-permute-start.4 = (bf16[1,256,512]{1,2,0:T(8,128)(2,1)S(1)}, bf16[1,256,512]{1,2,0:T(8,128)(2,1)S(1)}, u32[]{:S(2)}, u32[]{:S(2)}) collective-permute-start(bf16[1,256,512]{1,2,0:T(8,128)(2,1)S(1)} %get-tuple-element.615), channel_id=1, source_target_pairs={{0,16},{16,0},{1,17},{17,1},{2,18},{18,2},{3,19},{19,3},{4,20},{20... | collective-permute-start | bytes 786440 | tf_op jit(solution)/shard_map/ppermute | solution.py:646
  18.6 52.5 %collective-permute-start.3 = (bf16[1,16,256]{2,1,0:T(8,128)(2,1)S(1)}, bf16[1,16,256]{2,1,0:T(8,128)(2,1)S(1)}, u32[]{:S(2)}, u32[]{:S(2)}) collective-permute-start(bf16[1,16,256]{2,1,0:T(8,128)(2,1)S(1)} %get-tuple-element.613), channel_id=1, source_target_pairs={{0,16},{16,0},{1,17},{17,1},{2,18},{18,2},{3,19},{19,3},{4,20},{20... | collective-permute-start | bytes 24584 | tf_op jit(solution)/shard_map/ppermute | solution.py:646
  72.5 46.1 %collective-permute-start.6 = (bf16[2,256,512]{1,2,0:T(8,128)(2,1)S(1)}, bf16[2,256,512]{1,2,0:T(8,128)(2,1)S(1)}, u32[]{:S(2)}, u32[]{:S(2)}) collective-permute-start(bf16[2,256,512]{1,2,0:T(8,128)(2,1)S(1)} %pad_maximum_fusion.14), channel_id=1, source_target_pairs={{0,8},{8,0},{1,9},{9,1},{2,10},{10,2},{3,11},{11,3},{4,12},{12,4},... | collective-permute-start | bytes 1572872 | tf_op jit(solution)/shard_map/ppermute | solution.py:646
  75.4 43.2 %collective-permute-start.5 = (bf16[2,16,256]{2,1,0:T(8,128)(2,1)S(1)}, bf16[2,16,256]{2,1,0:T(8,128)(2,1)S(1)}, u32[]{:S(2)}, u32[]{:S(2)}) collective-permute-start(bf16[2,16,256]{2,1,0:T(8,128)(2,1)S(1)} %pad_maximum_fusion.25), channel_id=1, source_target_pairs={{0,8},{8,0},{1,9},{9,1},{2,10},{10,2},{3,11},{11,3},{4,12},{12,4},... | collective-permute-start | bytes 49160 | tf_op jit(solution)/shard_map/ppermute | solution.py:646
  127.4 343.4 %all-gather.10.cloned.1.call-start = ((), (), s32[]{:S(2)}) async-start(), calls=%async_computation.4 | async-start | bytes 18874368 | tf_op jit(solution)/shard_map/all_gather | solution.py:1021
  197.8 71.0 %collective-permute-start.11 = (bf16[256,3072]{1,0:T(8,128)(2,1)S(1)}, bf16[256,3072]{1,0:T(8,128)(2,1)}, u32[]{:S(2)}, u32[]{:S(2)}) collective-permute-start(bf16[256,3072]{1,0:T(8,128)(2,1)S(1)} %get-tuple-element.638.refs_0_), channel_id=1, source_target_pairs={{0,16},{16,0},{1,17},{17,1},{2,18},{18,2},{3,19},{19,3},{4,20},{20... | collective-permute-start | bytes 4718600 | tf_op jit(solution)/shard_map/ppermute | solution.py:646
  200.5 68.3 %collective-permute-start.12 = (bf16[256,3072]{1,0:T(8,128)(2,1)S(1)}, bf16[256,3072]{1,0:T(8,128)(2,1)S(1)}, u32[]{:S(2)}, u32[]{:S(2)}) collective-permute-start(bf16[256,3072]{1,0:T(8,128)(2,1)S(1)} %get-tuple-element.638.refs_0_), channel_id=1, source_target_pairs={{0,4},{4,0},{1,5},{5,1},{2,6},{6,2},{3,7},{7,3},{8,12},{12,8},{9,1... | collective-permute-start | bytes 4718600 | tf_op jit(solution)/shard_map/ppermute | solution.py:646
  202.0 74.7 %collective-permute-start.13 = (bf16[256,3072]{1,0:T(8,128)(2,1)S(1)}, bf16[256,3072]{1,0:T(8,128)(2,1)}, u32[]{:S(2)}, u32[]{:S(2)}) collective-permute-start(bf16[256,3072]{1,0:T(8,128)(2,1)S(1)} %get-tuple-element.637), channel_id=1, source_target_pairs={{0,8},{8,0},{1,9},{9,1},{2,10},{10,2},{3,11},{11,3},{4,12},{12,4},... | collective-permute-start | bytes 4718600 | tf_op jit(solution)/shard_map/ppermute | solution.py:646
  202.7 52.7 %collective-permute-start.17 = (bf16[1,1024,512]{2,1,0:T(8,128)(2,1)S(1)}, bf16[1,1024,512]{2,1,0:T(8,128)(2,1)S(1)}, u32[]{:S(2)}, u32[]{:S(2)}) collective-permute-start(bf16[1,1024,512]{2,1,0:T(8,128)(2,1)S(1)} %fusion.66), channel_id=1, source_target_pairs={{0,2},{1,3},{2,0},{3,1},{4,6},{5,7},{6,4},{7,5},{8,10},{9,11},{10,... | collective-permute-start | bytes 3145736 | tf_op jit(solution)/shard_map/ppermute | solution.py:646
  278.9 1069.9 %reduce-scatter.2.cloned.1.call-start = ((), (), s32[]{:S(2)}) async-start(), calls=%async_computation.2 | async-start | bytes 18874368 | tf_op jit(solution)/shard_map/reduce_scatter | solution.py:1180
  292.4 71.4 %collective-permute-start.25 = (bf16[256,3072]{1,0:T(8,128)(2,1)}, bf16[256,3072]{1,0:T(8,128)(2,1)}, u32[]{:S(2)}, u32[]{:S(2)}) collective-permute-start(bf16[256,3072]{1,0:T(8,128)(2,1)} %collective-permute-done.13.refs_4_), channel_id=1, source_target_pairs={{0,16},{16,0},{1,17},{17,1},{2,18},{18,2},{3,19},{19,3},{4,20},{20... | collective-permute-start | bytes 4718600 | tf_op jit(solution)/shard_map/ppermute | solution.py:646
  295.1 68.8 %collective-permute-start.26 = (bf16[256,3072]{1,0:T(8,128)(2,1)}, bf16[256,3072]{1,0:T(8,128)(2,1)}, u32[]{:S(2)}, u32[]{:S(2)}) collective-permute-start(bf16[256,3072]{1,0:T(8,128)(2,1)} %collective-permute-done.13.refs_4_), channel_id=1, source_target_pairs={{0,4},{4,0},{1,5},{5,1},{2,6},{6,2},{3,7},{7,3},{8,12},{12,8},{9,1... | collective-permute-start | bytes 4718600 | tf_op jit(solution)/shard_map/ppermute | solution.py:646
  297.1 134.8 %collective-permute-start.29 = (bf16[256,3072]{1,0:T(8,128)(2,1)}, bf16[256,3072]{1,0:T(8,128)(2,1)}, u32[]{:S(2)}, u32[]{:S(2)}) collective-permute-start(bf16[256,3072]{1,0:T(8,128)(2,1)} %get-tuple-element.327), channel_id=1, source_target_pairs={{0,8},{8,0},{1,9},{9,1},{2,10},{10,2},{3,11},{11,3},{4,12},{12,4},... | collective-permute-start | bytes 4718600 | tf_op jit(solution)/shard_map/ppermute | solution.py:646
  363.8 68.2 %collective-permute-start.28 = (bf16[256,3072]{1,0:T(8,128)(2,1)}, bf16[256,3072]{1,0:T(8,128)(2,1)}, u32[]{:S(2)}, u32[]{:S(2)}) collective-permute-start(bf16[256,3072]{1,0:T(8,128)(2,1)} %collective-permute-done.25.refs_5_), channel_id=1, source_target_pairs={{0,4},{4,0},{1,5},{5,1},{2,6},{6,2},{3,7},{7,3},{8,12},{12,8},{9,1... | collective-permute-start | bytes 4718600 | tf_op jit(solution)/shard_map/ppermute | solution.py:646
  365.5 66.4 %collective-permute-start.27 = (f32[4,17,2048]{2,0,1:T(4,128)}, f32[4,17,2048]{2,0,1:T(4,128)S(1)}, u32[]{:S(2)}, u32[]{:S(2)}) collective-permute-start(f32[4,17,2048]{2,0,1:T(4,128)} %copy.103), channel_id=1, source_target_pairs={{0,2},{1,3},{2,0},{3,1},{4,6},{5,7},{6,4},{7,5},{8,10},{9,11},{10,... | collective-permute-start | bytes 1671176 | tf_op jit(solution)/shard_map/ppermute | solution.py:646
  370.3 197.4 %collective-permute-start.21 = (bf16[256,3072]{1,0:T(8,128)(2,1)}, bf16[256,3072]{1,0:T(8,128)(2,1)}, u32[]{:S(2)}, u32[]{:S(2)}) collective-permute-start(bf16[256,3072]{1,0:T(8,128)(2,1)} %get-tuple-element.312.refs_0_), channel_id=1, source_target_pairs={{0,16},{16,0},{1,17},{17,1},{2,18},{18,2},{3,19},{19,3},{4,20},{20... | collective-permute-start | bytes 4718600 | tf_op jit(solution)/shard_map/ppermute | solution.py:646
  373.8 193.9 %collective-permute-start.22 = (bf16[256,3072]{1,0:T(8,128)(2,1)}, bf16[256,3072]{1,0:T(8,128)(2,1)}, u32[]{:S(2)}, u32[]{:S(2)}) collective-permute-start(bf16[256,3072]{1,0:T(8,128)(2,1)} %get-tuple-element.312.refs_0_), channel_id=1, source_target_pairs={{0,4},{4,0},{1,5},{5,1},{2,6},{6,2},{3,7},{7,3},{8,12},{12,8},{9,1... | collective-permute-start | bytes 4718600 | tf_op jit(solution)/shard_map/ppermute | solution.py:646
  432.0 135.7 %collective-permute-start.30 = (bf16[256,3072]{1,0:T(8,128)(2,1)}, bf16[256,3072]{1,0:T(8,128)(2,1)}, u32[]{:S(2)}, u32[]{:S(2)}) collective-permute-start(bf16[256,3072]{1,0:T(8,128)(2,1)} %collective-permute-done.29.refs_4_), channel_id=1, source_target_pairs={{0,16},{16,0},{1,17},{17,1},{2,18},{18,2},{3,19},{19,3},{4,20},{20... | collective-permute-start | bytes 4718600 | tf_op jit(solution)/shard_map/ppermute | solution.py:646
  433.1 134.6 %collective-permute-start.31 = (bf16[256,3072]{1,0:T(8,128)(2,1)}, bf16[256,3072]{1,0:T(8,128)(2,1)}, u32[]{:S(2)}, u32[]{:S(2)}) collective-permute-start(bf16[256,3072]{1,0:T(8,128)(2,1)} %collective-permute-done.29.refs_4_), channel_id=1, source_target_pairs={{0,4},{4,0},{1,5},{5,1},{2,6},{6,2},{3,7},{7,3},{8,12},{12,8},{9,1... | collective-permute-start | bytes 4718600 | tf_op jit(solution)/shard_map/ppermute | solution.py:646
  567.7 50.2 %collective-permute-start.32 = (bf16[256,3072]{1,0:T(8,128)(2,1)}, bf16[256,3072]{1,0:T(8,128)(2,1)}, u32[]{:S(2)}, u32[]{:S(2)}) collective-permute-start(bf16[256,3072]{1,0:T(8,128)(2,1)} %collective-permute-done.21.refs_1_), channel_id=1, source_target_pairs={{0,4},{4,0},{1,5},{5,1},{2,6},{6,2},{3,7},{7,3},{8,12},{12,8},{9,1... | collective-permute-start | bytes 4718600 | tf_op jit(solution)/shard_map/ppermute | solution.py:646
  569.7 68.8 %collective-permute-start.33 = (bf16[256,3072]{1,0:T(8,128)(2,1)}, bf16[256,3072]{1,0:T(8,128)(2,1)}, u32[]{:S(2)}, u32[]{:S(2)}) collective-permute-start(bf16[256,3072]{1,0:T(8,128)(2,1)} %collective-permute-done.30.refs_5_), channel_id=1, source_target_pairs={{0,4},{4,0},{1,5},{5,1},{2,6},{6,2},{3,7},{7,3},{8,12},{12,8},{9,1... | collective-permute-start | bytes 4718600 | tf_op jit(solution)/shard_map/ppermute | solution.py:646
  644.5 85.3 %collective-permute-start.34 = (bf16[2,256,3072]{2,1,0:T(8,128)(2,1)}, bf16[2,256,3072]{2,1,0:T(8,128)(2,1)}, u32[]{:S(2)}, u32[]{:S(2)}) collective-permute-start(bf16[2,256,3072]{2,1,0:T(8,128)(2,1)} %get-tuple-element.622), channel_id=1, source_target_pairs={{0,4},{4,0},{1,5},{5,1},{2,6},{6,2},{3,7},{7,3},{8,12},{12,8},{9,1... | collective-permute-start | bytes 9437192 | tf_op jit(solution)/shard_map/ppermute | solution.py:646
  751.8 79.2 %collective-permute-start.35 = (bf16[2,2,1024,512]{3,2,1,0:T(8,128)(2,1)}, bf16[2,2,1024,512]{3,2,1,0:T(8,128)(2,1)}, u32[]{:S(2)}, u32[]{:S(2)}) collective-permute-start(bf16[2,2,1024,512]{3,2,1,0:T(8,128)(2,1)} %get-tuple-element.402), channel_id=1, source_target_pairs={{0,1},{1,0},{2,3},{3,2},{4,5},{5,4},{6,7},{7,6},{8,9},{9,8},{10,11... | collective-permute-start | bytes 12582920 | tf_op jit(solution)/shard_map/ppermute | solution.py:646
  751.8 79.2 %collective-permute-start.36 = (bf16[2,2,1024,512]{3,2,1,0:T(8,128)(2,1)}, bf16[2,2,1024,512]{3,2,1,0:T(8,128)(2,1)}, u32[]{:S(2)}, u32[]{:S(2)}) collective-permute-start(bf16[2,2,1024,512]{3,2,1,0:T(8,128)(2,1)} %get-tuple-element.403), channel_id=1, source_target_pairs={{0,1},{1,0},{2,3},{3,2},{4,5},{5,4},{6,7},{7,6},{8,9},{9,8},{10,11... | collective-permute-start | bytes 12582920 | tf_op jit(solution)/shard_map/ppermute | solution.py:646
  752.3 78.7 %collective-permute-start.39 = (bf16[2,256,3072]{2,1,0:T(8,128)(2,1)}, bf16[2,256,3072]{2,1,0:T(8,128)(2,1)}, u32[]{:S(2)}, u32[]{:S(2)}) collective-permute-start(bf16[2,256,3072]{2,1,0:T(8,128)(2,1)} %get-tuple-element.409), channel_id=1, source_target_pairs={{0,4},{4,0},{1,5},{5,1},{2,6},{6,2},{3,7},{7,3},{8,12},{12,8},{9,1... | collective-permute-start | bytes 9437192 | tf_op jit(solution)/shard_map/ppermute | solution.py:646
  759.5 71.5 %collective-permute-start.38 = (bf16[1,256,3072]{2,1,0:T(8,128)(2,1)}, bf16[1,256,3072]{2,1,0:T(8,128)(2,1)}, u32[]{:S(2)}, u32[]{:S(2)}) collective-permute-start(bf16[1,256,3072]{2,1,0:T(8,128)(2,1)} %slice.499), channel_id=1, source_target_pairs={{0,16},{16,0},{1,17},{17,1},{2,18},{18,2},{3,19},{19,3},{4,20},{20... | collective-permute-start | bytes 4718600 | tf_op jit(solution)/shard_map/ppermute | solution.py:646
  775.2 52.2 %collective-permute-start.37 = (f32[1,6,2048]{2,1,0:T(8,128)S(1)}, f32[1,6,2048]{2,1,0:T(8,128)S(1)}, u32[]{:S(2)}, u32[]{:S(2)}) collective-permute-start(f32[1,6,2048]{2,1,0:T(8,128)S(1)} %broadcast_in_dim_reshape.3), channel_id=1, source_target_pairs={{0,8},{8,0},{1,9},{9,1},{2,10},{10,2},{3,11},{11,3},{4,12},{12,4},... | collective-permute-start | bytes 147464 | tf_op jit(solution)/shard_map/ppermute | solution.py:646
  837.3 90.5 %collective-permute-start.43 = (bf16[2,256,3072]{2,1,0:T(8,128)(2,1)}, bf16[2,256,3072]{2,1,0:T(8,128)(2,1)S(1)}, u32[]{:S(2)}, u32[]{:S(2)}) collective-permute-start(bf16[2,256,3072]{2,1,0:T(8,128)(2,1)} %get-tuple-element.620), channel_id=1, source_target_pairs={{0,4},{4,0},{1,5},{5,1},{2,6},{6,2},{3,7},{7,3},{8,12},{12,8},{9,1... | collective-permute-start | bytes 9437192 | tf_op jit(solution)/shard_map/ppermute | solution.py:646
  843.1 84.6 %collective-permute-start.41 = (bf16[2,1024,512]{2,1,0:T(8,128)(2,1)}, bf16[2,1024,512]{2,1,0:T(8,128)(2,1)S(1)}, u32[]{:S(2)}, u32[]{:S(2)}) collective-permute-start(bf16[2,1024,512]{2,1,0:T(8,128)(2,1)} %get-tuple-element.626), channel_id=1, source_target_pairs={{0,8},{8,0},{1,9},{9,1},{2,10},{10,2},{3,11},{11,3},{4,12},{12,4},... | collective-permute-start | bytes 6291464 | tf_op jit(solution)/shard_map/ppermute | solution.py:646
  848.0 79.7 %collective-permute-start.40 = (bf16[2,1024,512]{2,1,0:T(8,128)(2,1)}, bf16[2,1024,512]{2,1,0:T(8,128)(2,1)}, u32[]{:S(2)}, u32[]{:S(2)}) collective-permute-start(bf16[2,1024,512]{2,1,0:T(8,128)(2,1)} %get-tuple-element.627), channel_id=1, source_target_pairs={{0,2},{1,3},{2,0},{3,1},{4,6},{5,7},{6,4},{7,5},{8,10},{9,11},{10,... | collective-permute-start | bytes 6291464 | tf_op jit(solution)/shard_map/ppermute | solution.py:646
  857.0 70.7 %collective-permute-start.42 = (bf16[1,256,3072]{2,1,0:T(8,128)(2,1)}, bf16[1,256,3072]{2,1,0:T(8,128)(2,1)}, u32[]{:S(2)}, u32[]{:S(2)}) collective-permute-start(bf16[1,256,3072]{2,1,0:T(8,128)(2,1)} %slice.501), channel_id=1, source_target_pairs={{0,16},{16,0},{1,17},{17,1},{2,18},{18,2},{3,19},{19,3},{4,20},{20... | collective-permute-start | bytes 4718600 | tf_op jit(solution)/shard_map/ppermute | solution.py:646
  974.7 44.8 %collective-permute-start.51 = (bf16[2048,512]{1,0:T(8,128)(2,1)S(1)}, bf16[2048,512]{1,0:T(8,128)(2,1)S(1)}, u32[]{:S(2)}, u32[]{:S(2)}) collective-permute-start(bf16[2048,512]{1,0:T(8,128)(2,1)S(1)} %get-tuple-element.624), channel_id=1, source_target_pairs={{0,2},{1,3},{2,0},{3,1},{4,6},{5,7},{6,4},{7,5},{8,10},{9,11},{10,... | collective-permute-start | bytes 6291464 | tf_op jit(solution)/shard_map/ppermute | solution.py:646
  1024.7 92.7 %collective-permute-start.49 = (bf16[2,256,3072]{2,1,0:T(8,128)(2,1)}, bf16[2,256,3072]{2,1,0:T(8,128)(2,1)}, u32[]{:S(2)}, u32[]{:S(2)}) collective-permute-start(bf16[2,256,3072]{2,1,0:T(8,128)(2,1)} %get-tuple-element.440), channel_id=1, source_target_pairs={{0,4},{4,0},{1,5},{5,1},{2,6},{6,2},{3,7},{7,3},{8,12},{12,8},{9,1... | collective-permute-start | bytes 9437192 | tf_op jit(solution)/shard_map/ppermute | solution.py:646
  1025.1 92.2 %collective-permute-start.48 = (bf16[1,256,3072]{2,1,0:T(8,128)(2,1)}, bf16[1,256,3072]{2,1,0:T(8,128)(2,1)}, u32[]{:S(2)}, u32[]{:S(2)}) collective-permute-start(bf16[1,256,3072]{2,1,0:T(8,128)(2,1)} %slice.505), channel_id=1, source_target_pairs={{0,16},{16,0},{1,17},{17,1},{2,18},{18,2},{3,19},{19,3},{4,20},{20... | collective-permute-start | bytes 4718600 | tf_op jit(solution)/shard_map/ppermute | solution.py:646
  1157.4 75.6 %collective-permute-start.67 = (bf16[1,256,3072]{2,1,0:T(8,128)(2,1)}, bf16[1,256,3072]{2,1,0:T(8,128)(2,1)}, u32[]{:S(2)}, u32[]{:S(2)}) collective-permute-start(bf16[1,256,3072]{2,1,0:T(8,128)(2,1)} %slice.525), channel_id=1, source_target_pairs={{0,16},{16,0},{1,17},{17,1},{2,18},{18,2},{3,19},{19,3},{4,20},{20... | collective-permute-start | bytes 4718600 | tf_op jit(solution)/shard_map/ppermute | solution.py:646
  1192.8 61.5 %collective-permute-start.66 = (bf16[1,2048,512]{2,1,0:T(8,128)(2,1)S(1)}, bf16[1,2048,512]{2,1,0:T(8,128)(2,1)}, u32[]{:S(2)}, u32[]{:S(2)}) collective-permute-start(bf16[1,2048,512]{2,1,0:T(8,128)(2,1)S(1)} %get-tuple-element.496), channel_id=1, source_target_pairs={{0,2},{1,3},{2,0},{3,1},{4,6},{5,7},{6,4},{7,5},{8,10},{9,11},{10,... | collective-permute-start | bytes 6291464 | tf_op jit(solution)/shard_map/ppermute | solution.py:646
  1228.7 60.3 %collective-permute-start.61 = (bf16[2,2,256,1024]{3,2,1,0:T(8,128)(2,1)S(1)}, bf16[2,2,256,1024]{3,2,1,0:T(8,128)(2,1)S(1)}, u32[]{:S(2)}, u32[]{:S(2)}) collective-permute-start(bf16[2,2,256,1024]{3,2,1,0:T(8,128)(2,1)S(1)} %slice_bitcast_fusion.10), channel_id=1, source_target_pairs={{0,4},{4,0},{1,5},{5,1},{2,6},{6,2},{3,7},{7,3},{8,12},{12,8},{9,1... | collective-permute-start | bytes 6291464 | tf_op jit(solution)/shard_map/ppermute | solution.py:646
  1232.1 56.9 %collective-permute-start.62 = (bf16[2,2,256,1024]{3,2,1,0:T(8,128)(2,1)S(1)}, bf16[2,2,256,1024]{3,2,1,0:T(8,128)(2,1)S(1)}, u32[]{:S(2)}, u32[]{:S(2)}) collective-permute-start(bf16[2,2,256,1024]{3,2,1,0:T(8,128)(2,1)S(1)} %slice_bitcast_fusion.9), channel_id=1, source_target_pairs={{0,8},{8,0},{1,9},{9,1},{2,10},{10,2},{3,11},{11,3},{4,12},{12,4},... | collective-permute-start | bytes 6291464 | tf_op jit(solution)/shard_map/ppermute | solution.py:646
  1236.7 44.5 %collective-permute-start.63 = (f32[19,2048]{1,0:T(8,128)}, f32[19,2048]{1,0:T(8,128)}, u32[]{:S(2)}, u32[]{:S(2)}) collective-permute-start(f32[19,2048]{1,0:T(8,128)} %add_add_fusion.1), channel_id=1, source_target_pairs={{0,4},{4,0},{8,12},{12,8},{1,5},{5,1},{9,13},{13,9},{2,6},{6,2},{1... | collective-permute-start | bytes 466952 | tf_op jit(solution)/shard_map/ppermute | solution.py:646
  1237.2 47.7 %collective-permute-start.64 = (f32[19,2048]{1,0:T(8,128)}, f32[19,2048]{1,0:T(8,128)S(1)}, u32[]{:S(2)}, u32[]{:S(2)}) collective-permute-start(f32[19,2048]{1,0:T(8,128)} %add_add_fusion.1), channel_id=1, source_target_pairs={{0,8},{4,12},{8,0},{12,4},{1,9},{5,13},{9,1},{13,5},{2,10},{6,14},... | collective-permute-start | bytes 466952 | tf_op jit(solution)/shard_map/ppermute | solution.py:646
  1281.2 45.8 %collective-permute-start.71 = (bf16[256,3072]{1,0:T(8,128)(2,1)S(1)}, bf16[256,3072]{1,0:T(8,128)(2,1)S(1)}, u32[]{:S(2)}, u32[]{:S(2)}) collective-permute-start(bf16[256,3072]{1,0:T(8,128)(2,1)S(1)} %copy-done.51), channel_id=1, source_target_pairs={{0,8},{8,0},{1,9},{9,1},{2,10},{10,2},{3,11},{11,3},{4,12},{12,4},... | collective-permute-start | bytes 4718600 | tf_op jit(solution)/shard_map/ppermute | solution.py:646
  1292.0 54.9 %collective-permute-start.69 = (bf16[2,256,1024]{2,1,0:T(8,128)(2,1)S(1)}, bf16[2,256,1024]{2,1,0:T(8,128)(2,1)S(1)}, u32[]{:S(2)}, u32[]{:S(2)}) collective-permute-start(bf16[2,256,1024]{2,1,0:T(8,128)(2,1)S(1)} %fusion.69), channel_id=1, source_target_pairs={{0,4},{4,0},{1,5},{5,1},{2,6},{6,2},{3,7},{7,3},{8,12},{12,8},{9,1... | collective-permute-start | bytes 3145736 | tf_op jit(solution)/shard_map/ppermute | solution.py:646
  1294.7 54.1 %collective-permute-start.68 = (bf16[2,256,1024]{2,1,0:T(8,128)(2,1)S(1)}, bf16[2,256,1024]{2,1,0:T(8,128)(2,1)}, u32[]{:S(2)}, u32[]{:S(2)}) collective-permute-start(bf16[2,256,1024]{2,1,0:T(8,128)(2,1)S(1)} %fusion.68), channel_id=1, source_target_pairs={{0,8},{8,0},{1,9},{9,1},{2,10},{10,2},{3,11},{11,3},{4,12},{12,4},... | collective-permute-start | bytes 3145736 | tf_op jit(solution)/shard_map/ppermute | solution.py:646
  1298.2 48.7 %collective-permute-start.70 = (f32[19,2048]{1,0:T(8,128)S(1)}, f32[19,2048]{1,0:T(8,128)S(1)}, u32[]{:S(2)}, u32[]{:S(2)}) collective-permute-start(f32[19,2048]{1,0:T(8,128)S(1)} %add_add_fusion), channel_id=1, source_target_pairs={{0,16},{16,0},{1,17},{17,1},{2,18},{18,2},{3,19},{19,3},{4,20},{20... | collective-permute-start | bytes 466952 | tf_op jit(solution)/shard_map/ppermute | solution.py:646
  (119 other events, 1501.2 us)
Sparse Core Ops, SparseCore 0:
  11.7 115.5 all-gather.5
  128.9 99.2 all-gather.7
  279.0 191.7 all-gather.9
  1021.0 193.3 reduce-scatter.1
where the time goes:
time: 1420 us
  waiting for transfers between devices  521 us (37%)
  Pallas kernels  490 us (35%)
  other arithmetic  138 us (10%)
  local copies, waits for them, and re-layouts  106 us (7%)
  starting transfers between devices  84 us (6%)
  matrix products  60.4 us (4%)
  between operations  15.8 us (1%)
    ppermute x74, waiting for transfers between devices, swap(): return lax.ppermute(values, axis, [(n, n ^ bit) for n in range(size)])  495 us
    pallas_call x2, Pallas kernels, expert_step(): pl.pallas_call(functools.partial(expert_kernel, count, hidden), grid_spec...  155 us
    pallas_call x3, Pallas kernels, weight_grads(): pl.pallas_call(functools.partial(weight_grad_kernel, mids), grid_spec=plt...  127 us
    ppermute x74, starting transfers between devices, swap(): return lax.ppermute(values, axis, [(n, n ^ bit) for n in range(size)])  83.4 us
    pallas_call x2, Pallas kernels, attend_backward(): pl.pallas_call(attend_backward_kernel, grid_spec=pltpu.PrefetchScalarGrid...  64.1 us
    dot_general x9, matrix products, dot_of(): lax.dot_general(a, b, (((da,), (db,)), ((), ())), preferred_element_type=...  60.4 us
    pallas_call x2, Pallas kernels, compact(): pl.pallas_call(compact_kernel, grid_spec=pltpu.PrefetchScalarGridSpec(num...  38.2 us
    pallas_call x2, Pallas kernels, attend_forward(): pl.pallas_call(attend_forward_kernel, grid_spec=pltpu.PrefetchScalarGridS...  36.4 us
  transfers between devices with their start and end apart: 78, of which 33 were waited for; matrix products, arithmetic and copies ran while one was open for 16% of the time, Pallas kernels for 33%

commit v1 on v0

--- a/solution.py
+++ b/solution.py
@@ -1027,7 +1027,10 @@
         live,
         [stat_flow, weight_flows[0, 0]] + firsts,
         [lambda: compact(starts, where, pos_row, moe_cot, groups, cols)],
-    )
+        sync=seconds[:1],
+    )
+    for flow in seconds[:1]:
+        flow.step(2)
     stage(live, [stat_flow] + firsts + seconds[1:])
     stat = stat_flow.finish()
 
@@ -1096,9 +1099,9 @@
         others = [flow for (number, _), flow in weight_flows.items() if number > expert]
         (outs,) = stage(
             live,
-            others + running()[:1],
+            others[1:] + running()[:1],
             [functools.partial(run_expert, expert)],
-            sync=running()[1:],
+            sync=others[:1] + running()[1:],
         )
         ran.append(outs)
         if expert + 1 < each:
@@ -1135,15 +1138,19 @@
     grad_flow(each - 1, grads)
     late = running()[len(early) :]
     scalar_flow.finish()
+    for flow in late[:1]:
+        flow.step()
     (branch_parts,) = stage(
         live,
-        [moe_in_flow] + early[1:] + late[:1],
+        [moe_in_flow],
         [lambda: expand_all(starts, where, pos_col, live["result"], groups, cols)],
-        sync=[scalar_flow],
-    )
+        sync=[scalar_flow] + early,
+    )
+    for flow in early[1:]:
+        flow.step()
     live["moe_branch"] = branch_parts.reshape(groups * cols, tok_rows, width)
     while moe_in_flow.sends is not None:
-        stage(live, [moe_in_flow], sync=early + late)
+        stage(live, [moe_in_flow], sync=late)
     scalar_all = scalar_flow.finish().reshape(groups, cols, each + 1, groups, tok_rows)
     scalar_all = jnp.stack([scalar_all[place, :, :, place] for place in range(groups)])
     by_expert = jnp.stack(
@@ -1170,11 +1177,12 @@
     cot_flow = Flow(spread_steps(middle_cot.astype(BF16), "col", col_bits))
     router_part, moe_gain_part = stage(
         live,
-        [cot_flow] + early[:1],
+        [cot_flow],
         [
             lambda: dot_of(scaled_logit, scaled_rows, 1, 0),
             lambda: jnp.sum(back * middle, axis=0)[None],
         ],
+        sync=early[1:],
     )
     cot_blocks = cot_flow.finish()
     moe_branch = lax.psum_scatter(
@@ -1210,7 +1218,7 @@
     live.update(qkv_rel=qkv_rel, mixture=mixture, cot_all=cot_all)
     done = stage(
         live,
-        late,
+        early[:1] + late,
         [functools.partial(attend_back, s) for s in range(seqs)],
     )
     share = width // (mids * depth)
@@ -1238,21 +1246,21 @@
             full = lax.dynamic_update_slice_in_dim(full, block, (col ^ place) * width, 1)
         return full
 
-    def input_cots():
-        partial = dot_of(live["qkv_cot"], live["qkv_rel"], 1, 1)
-        backs = [partial[:, n * width : (n + 1) * width] for n in range(cols)]
-        attn_flow = Flow(col_reduce_steps(backs, cols)).step(len(bits_of(cols)) - 1)
+    for flow in late:
+        flow.step()
+    (partial,) = stage(live, [], [lambda: dot_of(live["qkv_cot"], live["qkv_rel"], 1, 1)])
+    backs = [partial[:, n * width : (n + 1) * width] for n in range(cols)]
+    attn_flow = Flow(col_reduce_steps(backs, cols))
+
+    def gain_sums():
         attn_gain_parts = [
             jnp.sum(part * (block.astype(F32) * attn_inverse), axis=0)[None]
             for part, block in zip(backs, hidden_blocks)
         ]
-        token_inner = jnp.concatenate([outs[3] for outs in done], axis=0)
-        inner_flow = Flow(total_steps(token_inner, [("col",)]))
-        inner_flow.finish()
         query_part = sum(outs[1] for outs in done)
         key_part = sum(outs[2] for outs in done)
         head_parts = jnp.concatenate([query_part, key_part], 1)
-        small = jnp.concatenate(
+        return jnp.concatenate(
             [
                 widen([router_part]),
                 widen([moe_gain_part]),
@@ -1261,20 +1269,23 @@
             ],
             axis=0,
         )
-        small_flow = Flow(total_steps(small, [("col",), ("lo", "mid"), ("hi",)])).step()
-        flows.extend([attn_flow, inner_flow, small_flow])
-        return [flow.holds() for flow in flows]
-
-    flows = []
-    late[1].step()
-    (held,) = stage(live, [], [input_cots])
-    for flow, arrays in zip(flows, held):
-        flow.replace(arrays)
-    attn_flow, inner_flow, small_flow = flows
-    attn_flow.step()
-    (grads,) = stage(live, [], [projection_grads])
+
+    token_inner = jnp.concatenate([outs[3] for outs in done], axis=0)
+    inner_flow = Flow(total_steps(token_inner, [("col",)]))
+    (grads,) = stage(live, [attn_flow, inner_flow], [projection_grads])
     qkv_flow = Flow(row_reduce_steps(grads, groups, mids, high))
-    stage(live, [qkv_flow, small_flow], sync=[attn_flow, late[1]])
+    for _ in bits_of(cols)[2:]:
+        stage(live, [attn_flow])
+    small_flows = []
+
+    def small_sums():
+        flow = Flow(total_steps(gain_sums(), [("col",), ("lo", "mid"), ("hi",)])).step()
+        small_flows.append(flow)
+        return flow.holds()
+
+    (held,) = stage(live, [attn_flow, qkv_flow], [small_sums], sync=[late[1]])
+    (small_flow,) = small_flows
+    small_flow.replace(held)
     live["moe_branch"] = moe_branch
 
     def input_sums():
@@ -1284,7 +1295,7 @@
             - hidden * (attn_inverse * attn_inverse * (inner_flow.finish()[:, None] / D))
         )
 
-    (input_grad,) = stage(live, [qkv_flow, small_flow] + early[:1] + late, [input_sums])
+    (input_grad,) = stage(live, [qkv_flow, small_flow], [input_sums])
     flows = [qkv_flow, small_flow] + early + late
     while any(flow.sends is not None for flow in flows):
         stage(live, flows)

time: 1420 us -> 1400 us (0.986)
  waiting for transfers between devices: 521 us -> 491 us
    all_gather x1, waiting for transfers between devices: 17.4 us -> 0.15 us  [per_device(): moe_in = lax.all_gather(scaled_rows, cube, axis=0, tiled=False)]
    unnamed x200 -> x206, local copies, waits for them, and re-layouts: 35.6 us -> 29.2 us
  transfers between devices with their start and end apart: 78 -> 78, of which waited for: 33 -> 30; matrix products, arithmetic and copies ran while one was open for 16% -> 17% of each run, Pallas kernels for 33% -> 34%
where the time goes in v1:
time: 1400 us; the launch traced here: 1390 us
  waiting for transfers between devices  491 us (35%)
  Pallas kernels  490 us (35%)
  other arithmetic  144 us (10%)
  starting transfers between devices  95.5 us (7%)
  local copies, waits for them, and re-layouts  93.1 us (7%)
  matrix products  59.8 us (4%)
  between operations  16 us (1%)
    ppermute x74, waiting for transfers between devices, swap(): return lax.ppermute(values, axis, [(n, n ^ bit) for n in range(size)])  482 us
    pallas_call x2, Pallas kernels, expert_step(): pl.pallas_call(functools.partial(expert_kernel, count, hidden), grid_spec...  155 us
    pallas_call x3, Pallas kernels, weight_grads(): pl.pallas_call(functools.partial(weight_grad_kernel, mids), grid_spec=plt...  127 us
    ppermute x74, starting transfers between devices, swap(): return lax.ppermute(values, axis, [(n, n ^ bit) for n in range(size)])  95.2 us
    pallas_call x2, Pallas kernels, attend_backward(): pl.pallas_call(attend_backward_kernel, grid_spec=pltpu.PrefetchScalarGrid...  64.3 us
    dot_general x9, matrix products, dot_of(): lax.dot_general(a, b, (((da,), (db,)), ((), ())), preferred_element_type=...  59.8 us
    pallas_call x2, Pallas kernels, compact(): pl.pallas_call(compact_kernel, grid_spec=pltpu.PrefetchScalarGridSpec(num...  38.3 us
    pallas_call x2, Pallas kernels, attend_forward(): pl.pallas_call(attend_forward_kernel, grid_spec=pltpu.PrefetchScalarGridS...  36.2 us
  transfers between devices with their start and end apart: 78, of which 30 were waited for; matrix products, arithmetic and copies ran while one was open for 17% of the time, Pallas kernels for 34%

profile of v1, /device:TPU:0, one launch (start us, length us, event | category | flops | bytes accessed | tf_op | source)
XLA Modules:
  0.0 1388.6 jit_solution(2323485819996987184)
XLA Ops:
  25.8 34.6 %collective-permute-done.1 = f32[512]{0:T(512)S(1)} collective-permute-done((f32[512]{0:T(512)S(1)}, f32[512]{0:T(512)S(1)}, u32[]{:S(2)}, u32[]{:S(2)}) %collective-permute-start.1) | collective-permute-done | bytes 2080 | tf_op jit(solution)/shard_map/ppermute | solution.py:646
  62.9 8.3 pack_weights.1
  97.7 20.9 %collective-permute-done.5 = bf16[2,16,256]{2,1,0:T(8,128)(2,1)S(1)} collective-permute-done((bf16[2,16,256]{2,1,0:T(8,128)(2,1)S(1)}, bf16[2,16,256]{2,1,0:T(8,128)(2,1)S(1)}, u32[]{:S(2)}, u32[]{:S(2)}) %collective-permute-start.5) | collective-permute-done | bytes 16416 | tf_op jit(solution)/shard_map/ppermute | solution.py:646
  118.6 8.7 all-gather.6.cloned.1.call-done
  130.5 19.3 %fusion.110.q_ref.k_ref.v_ref = f32[2048,1536]{1,0:T(8,128)} fusion(bf16[2048,2048]{1,0:T(8,128)(2,1)} %fusion.43.x_ref, bf16[2048,1536]{1,0:T(8,128)(2,1)} %all-gather.6.cloned.1.call-done), kind=kOutput, calls=%fused_computation.307 | convolution fusion | flops 12884901888 | bytes 27262976 | tf_op jit(solution)/shard_map/dot_general | solution.py:36
  149.8 18.0 %attend_forward.2 = (bf16[1024,512]{1,0:T(8,128)(2,1)}, bf16[1024,512]{1,0:T(8,128)(2,1)}, bf16[1024,512]{1,0:T(8,128)(2,1)}, bf16[1024,512]{1,0:T(8,128)(2,1)}) custom-call(s32[1]{0:T(128)} %get-tuple-element.675.live_ref, f32[2048,1536]{1,0:T(8,128)} %fusion.110.q_ref.k_ref.v_ref, f32[2048,1536]{1,0:T(8,128)} %fusion.110.q_ref.k_ref.v_ref, ...), custom_call_target="tpu_custom_call" | custom-call | flops 85899344 | bytes 209715 | tf_op jit(solution)/shard_map/attend_forward/pallas_call | solution.py:96
  167.8 18.2 %attend_forward.3 = (bf16[1024,512]{1,0:T(8,128)(2,1)}, bf16[1024,512]{1,0:T(8,128)(2,1)}, bf16[1024,512]{1,0:T(8,128)(2,1)}, bf16[1024,512]{1,0:T(8,128)(2,1)}) custom-call(s32[1]{0:T(128)} %get-tuple-element.674.live_ref, f32[2048,1536]{1,0:T(8,128)} %fusion.110.q_ref.k_ref.v_ref, f32[2048,1536]{1,0:T(8,128)} %fusion.110.q_ref.k_ref.v_ref, ...), custom_call_target="tpu_custom_call" | custom-call | flops 85899344 | bytes 209715 | tf_op jit(solution)/shard_map/attend_forward/pallas_call | solution.py:96
  203.8 29.3 %collective-permute-done.19 = bf16[1,1024,512]{2,1,0:T(8,128)(2,1)S(1)} collective-permute-done((bf16[1,1024,512]{2,1,0:T(8,128)(2,1)S(1)}, bf16[1,1024,512]{2,1,0:T(8,128)(2,1)S(1)}, u32[]{:S(2)}, u32[]{:S(2)}) %collective-permute-start.19) | collective-permute-done | bytes 1048608 | tf_op jit(solution)/shard_map/ppermute | solution.py:646
  233.6 21.7 %collective-permute-done.17 = bf16[1,1024,512]{2,1,0:T(8,128)(2,1)S(1)} collective-permute-done((bf16[1,1024,512]{2,1,0:T(8,128)(2,1)S(1)}, bf16[1,1024,512]{2,1,0:T(8,128)(2,1)S(1)}, u32[]{:S(2)}, u32[]{:S(2)}) %collective-permute-start.17) | collective-permute-done | bytes 1048608 | tf_op jit(solution)/shard_map/ppermute | solution.py:646
  255.9 12.8 collective-permute-done.11.refs_1_
  269.9 6.9 collective-permute-done.13.refs_4_
  299.1 19.2 %compact.2 = (bf16[2304,2048]{1,0:T(8,128)(2,1)}, bf16[2304,2048]{1,0:T(8,128)(2,1)}) custom-call(s32[4,16]{1,0:T(4,128)} %fusion.93.start_ref, s32[2]{0:T(128)} %pad_add_fusion.1.where_ref, s32[2,2,1,2048]{3,2,1,0:T(1,128)} %select_n.148.pos_ref, bf16[8,2048,512]{2,1,0:T(8,128)(2,1)} %bitcast.346), custom_call_target="tpu_custom_call" | custom-call | flops 193273536 | bytes 713031 | tf_op jit(solution)/shard_map/compact/pallas_call | solution.py:260
  318.3 10.5 collective-permute-done.22.refs_3_
  328.8 35.3 %collective-permute-done.23.refs_5_ = bf16[256,3072]{1,0:T(8,128)(2,1)} collective-permute-done((bf16[256,3072]{1,0:T(8,128)(2,1)}, bf16[256,3072]{1,0:T(8,128)(2,1)}, u32[]{:S(2)}, u32[]{:S(2)}) %collective-permute-start.23) | collective-permute-done | bytes 1572896 | tf_op jit(solution)/shard_map/ppermute | solution.py:646
  375.7 56.6 %collective-permute-done.27.refs_4_ = bf16[256,3072]{1,0:T(8,128)(2,1)} collective-permute-done((bf16[256,3072]{1,0:T(8,128)(2,1)}, bf16[256,3072]{1,0:T(8,128)(2,1)}, u32[]{:S(2)}, u32[]{:S(2)}) %collective-permute-start.27) | collective-permute-done | bytes 1572896 | tf_op jit(solution)/shard_map/ppermute | solution.py:646
  443.3 5.7 compact_scalars.1
  449.1 11.7 collective-permute-done.30.refs_1_
  467.4 19.1 %compact.3 = (bf16[2304,2048]{1,0:T(8,128)(2,1)}, bf16[2304,2048]{1,0:T(8,128)(2,1)}) custom-call(s32[4,16]{1,0:T(4,128)} %fusion.93.start_ref, s32[2]{0:T(128)} %pad_add_fusion.1.where_ref, s32[2,2,1,2048]{3,2,1,0:T(1,128)} %select_n.148.pos_ref, bf16[8,2048,512]{2,1,0:T(8,128)(2,1)} %bitcast.347), custom_call_target="tpu_custom_call" | custom-call | flops 193273536 | bytes 713031 | tf_op jit(solution)/shard_map/compact/pallas_call | solution.py:260
  486.5 77.5 %expert_step.2 = (bf16[2304,2048]{1,0:T(8,128)(2,1)}, bf16[2304,2048]{1,0:T(8,128)(2,1)}, bf16[2304,1024]{1,0:T(8,128)(2,1)}, f32[2304,1]{1,0:T(8,128)}, f32[2304,1]{1,0:T(8,128)}, /*index=5*/bf16[2304,2048]{1,0:T(8,128)(2,1)}) custom-call(s32[8]{0:T(128)} %stack.252.row_ref, bf16[2304,2048]{1,0:T(8,128)(2,1)} %get-tuple-element.365.x_ref, ...), custom_call_target="tpu_custom_call" | custom-call | flops 1159641216 | bytes 1038090 | tf_op jit(solution)/shard_map/expert_step/pallas_call | solution.py:555
  566.7 47.5 %weight_grads.3 = bf16[2,2,2,256,3072]{4,3,2,1,0:T(8,128)(2,1)} custom-call(s32[9]{0:T(128)} %stack.258.place_ref, bf16[2304,2048]{1,0:T(8,128)(2,1)} %get-tuple-element.365.x_ref, bf16[2304,2048]{1,0:T(8,128)(2,1)} %get-tuple-element.366.m_ref, bf16[2304,2048]{1,0:T(8,128)(2,1)} %get-tuple-element.367.pre_ref, bf16[2304,1024]{1,0:T(8,128)(2,1)} %get-tuple-element.368.act_ref), custom_call_target="tpu_custom_call" | custom-call | flops 579820608 | bytes 660602 | tf_op jit(solution)/shard_map/weight_grads/pallas_call | solution.py:619
  614.2 6.0 slice_bitcast_fusion.2
  626.8 77.7 %expert_step.3 = (bf16[2304,2048]{1,0:T(8,128)(2,1)}, bf16[2304,2048]{1,0:T(8,128)(2,1)}, bf16[2304,1024]{1,0:T(8,128)(2,1)}, f32[2304,1]{1,0:T(8,128)}, f32[2304,1]{1,0:T(8,128)}, /*index=5*/bf16[2304,2048]{1,0:T(8,128)(2,1)}) custom-call(s32[8]{0:T(128)} %stack.259.row_ref, bf16[2304,2048]{1,0:T(8,128)(2,1)} %get-tuple-element.417.x_ref, ...), custom_call_target="tpu_custom_call" | custom-call | flops 1159641216 | bytes 1038090 | tf_op jit(solution)/shard_map/expert_step/pallas_call | solution.py:555
  707.9 18.7 %expand.1 = (bf16[2,2,1024,512]{3,2,1,0:T(8,128)(2,1)}, bf16[2,2,1024,512]{3,2,1,0:T(8,128)(2,1)}, bf16[2,2,1024,512]{3,2,1,0:T(8,128)(2,1)}, bf16[2,2,1024,512]{3,2,1,0:T(8,128)(2,1)}) custom-call(s32[4,16]{1,0:T(4,128)} %fusion.93.start_ref, s32[2]{0:T(128)} %pad_add_fusion.1.where_ref, s32[2,2,2048,1]{3,2,1,0:T(8,128)} %copy.111.pos_ref, ...), custom_call_target="tpu_custom_call" | custom-call | flops 193273536 | bytes 713031 | tf_op jit(solution)/shard_map/expand/pallas_call | solution.py:378
  745.0 6.4 expand_scalars.1
  757.5 47.5 %weight_grads.4 = bf16[2,2,2,256,3072]{4,3,2,1,0:T(8,128)(2,1)} custom-call(s32[9]{0:T(128)} %stack.258.place_ref, bf16[2304,2048]{1,0:T(8,128)(2,1)} %get-tuple-element.417.x_ref, bf16[2304,2048]{1,0:T(8,128)(2,1)} %get-tuple-element.418.m_ref, bf16[2304,2048]{1,0:T(8,128)(2,1)} %get-tuple-element.419.pre_ref, bf16[2304,1024]{1,0:T(8,128)(2,1)} %get-tuple-element.420.act_ref), custom_call_target="tpu_custom_call" | custom-call | flops 579820608 | bytes 660602 | tf_op jit(solution)/shard_map/weight_grads/pallas_call | solution.py:619
  812.7 4.7 add_convert_fusion.1
  818.1 5.1 add_convert_fusion.2
  837.0 20.3 %expand_all.1 = bf16[2,4,2048,512]{3,2,1,0:T(8,128)(2,1)} custom-call(s32[4,16]{1,0:T(4,128)} %fusion.93.start_ref, s32[2]{0:T(128)} %pad_add_fusion.1.where_ref, s32[2,2,2048,1]{3,2,1,0:T(8,128)} %copy.111.pos_ref, bf16[2304,2048]{1,0:T(8,128)(2,1)} %get-tuple-element.429.refs_0_, bf16[2304,2048]{1,0:T(8,128)(2,1)} %get-tuple-element.430.refs_1_), custom_call_target="tpu_custom_call" | custom-call | flops 193273536 | bytes 713031 | tf_op jit(solution)/shard_map/expand_all/pallas_call | solution.py:415
  857.4 20.5 %collective-permute-done.43 = f32[4,6,2048]{2,1,0:T(8,128)} collective-permute-done((f32[4,6,2048]{2,1,0:T(8,128)}, f32[4,6,2048]{2,1,0:T(8,128)}, u32[]{:S(2)}, u32[]{:S(2)}) %collective-permute-start.43) | collective-permute-done | bytes 196640 | tf_op jit(solution)/shard_map/ppermute | solution.py:646
  890.5 8.9 collective-permute-done.47
  909.9 27.4 %collective-permute-done.45 = bf16[1024,512]{1,0:T(8,128)(2,1)} collective-permute-done((bf16[1024,512]{1,0:T(8,128)(2,1)}, bf16[1024,512]{1,0:T(8,128)(2,1)}, u32[]{:S(2)}, u32[]{:S(2)}) %collective-permute-start.45) | collective-permute-done | bytes 1048608 | tf_op jit(solution)/shard_map/ppermute | solution.py:646
  943.1 4.9 multiply_reduce_fusion
  954.2 40.2 %collective-permute-done.51 = bf16[2048,512]{1,0:T(8,128)(2,1)S(1)} collective-permute-done((bf16[2048,512]{1,0:T(8,128)(2,1)S(1)}, bf16[2048,512]{1,0:T(8,128)(2,1)S(1)}, u32[]{:S(2)}, u32[]{:S(2)}) %collective-permute-start.51) | collective-permute-done | bytes 2097184 | tf_op jit(solution)/shard_map/ppermute | solution.py:646
  1019.2 31.9 %attend_backward.3 = (bf16[1024,512]{1,0:T(8,128)(2,1)}, bf16[1024,512]{1,0:T(8,128)(2,1)}, bf16[1024,512]{1,0:T(8,128)(2,1)}, f32[1,128]{1,0:T(1,128)}, f32[1,128]{1,0:T(1,128)}, /*index=5*/f32[1024,1]{1,0:T(8,128)}) custom-call(s32[1]{0:T(128)} %get-tuple-element.674.live_ref, bf16[1024,512]{1,0:T(8,128)(2,1)} %get-tuple-element.466.ql_ref, ...), custom_call_target="tpu_custom_call" | custom-call | flops 214748368 | bytes 251658 | tf_op jit(solution)/shard_map/attend_backward/pallas_call | solution.py:214
  1052.4 6.2 fusion.61.do_ref
  1058.7 32.4 %attend_backward.2 = (bf16[1024,512]{1,0:T(8,128)(2,1)}, bf16[1024,512]{1,0:T(8,128)(2,1)}, bf16[1024,512]{1,0:T(8,128)(2,1)}, f32[1,128]{1,0:T(1,128)}, f32[1,128]{1,0:T(1,128)}, /*index=5*/f32[1024,1]{1,0:T(8,128)}) custom-call(s32[1]{0:T(128)} %get-tuple-element.675.live_ref, bf16[1024,512]{1,0:T(8,128)(2,1)} %get-tuple-element.447.ql_ref, ...), custom_call_target="tpu_custom_call" | custom-call | flops 214748368 | bytes 251658 | tf_op jit(solution)/shard_map/attend_backward/pallas_call | solution.py:214
  1099.0 18.7 %fusion.111 = f32[2048,2048]{1,0:T(8,128)S(1)} fusion(bf16[2048,1536]{1,0:T(8,128)(2,1)} %constant_dynamic-update-slice_fusion.10.pre_ref, bf16[2048,1536]{1,0:T(8,128)(2,1)} %pad_maximum_fusion.1), kind=kOutput, calls=%fused_computation.308 | convolution fusion | flops 12884901888 | bytes 29360128 | tf_op jit(solution)/shard_map/dot_general | solution.py:36
  1117.8 6.1 copy-done.9
  1138.9 31.9 %weight_grads.5 = bf16[2,2,2,256,2048]{4,3,2,1,0:T(8,128)(2,1)} custom-call(s32[9]{0:T(128)} %stack.302.place_ref, bf16[2048,2048]{1,0:T(8,128)(2,1)} %fusion.43.x_ref, bf16[2048,2048]{1,0:T(8,128)(2,1)} %copy-done.10, bf16[2048,1536]{1,0:T(8,128)(2,1)} %constant_dynamic-update-slice_fusion.10.pre_ref, bf16[2048,512]{1,0:T(8,128)(2,1)} %pad_maximum_fusion.7.act_ref), custom_call_target="tpu_custom_call" | custom-call | flops 343597376 | bytes 503316 | tf_op jit(solution)/shard_map/weight_grads/pallas_call | solution.py:619
  1170.9 10.1 fusion.19
  1185.4 20.4 %collective-permute-done.64 = bf16[1,256,3072]{2,1,0:T(8,128)(2,1)} collective-permute-done((bf16[1,256,3072]{2,1,0:T(8,128)(2,1)S(1)}, bf16[1,256,3072]{2,1,0:T(8,128)(2,1)}, u32[]{:S(2)}, u32[]{:S(2)}) %collective-permute-start.64) | collective-permute-done | bytes 1572896 | tf_op jit(solution)/shard_map/ppermute | solution.py:646
  1211.5 43.1 %collective-permute-done.62 = f32[19,2048]{1,0:T(8,128)S(1)} collective-permute-done((f32[19,2048]{1,0:T(8,128)S(1)}, f32[19,2048]{1,0:T(8,128)S(1)}, u32[]{:S(2)}, u32[]{:S(2)}) %collective-permute-start.62) | collective-permute-done | bytes 155680 | tf_op jit(solution)/shard_map/ppermute | solution.py:646
  1254.6 4.5 collective-permute-done.63
  1271.5 7.3 fusion.25
  1278.8 12.8 collective-permute-done.67
  1296.2 4.8 collective-permute-done.69
  1314.4 45.7 %collective-permute-done.73.refs_3_ = bf16[256,3072]{1,0:T(8,128)(2,1)} collective-permute-done((bf16[256,3072]{1,0:T(8,128)(2,1)}, bf16[256,3072]{1,0:T(8,128)(2,1)}, u32[]{:S(2)}, u32[]{:S(2)}) %collective-permute-start.73) | collective-permute-done | bytes 1572896 | tf_op jit(solution)/shard_map/ppermute | solution.py:646
  1360.1 9.5 unpack_grads.1
  (542 shorter events, 316.5 us)
Async XLA Ops:
  7.2 120.1 %all-gather.6.cloned.1.call-start = ((), (), s32[]{:S(2)}) async-start(), calls=%async_computation.1 | async-start | bytes 7077888 | tf_op jit(solution)/shard_map/all_gather | solution.py:908
  11.6 287.5 %all-gather.8.cloned.1.call-start = ((), (), s32[]{:S(2)}) async-start(), calls=%async_computation.3 | async-start | bytes 18874368 | tf_op jit(solution)/shard_map/all_gather | solution.py:968
  11.7 59.5 %collective-permute-start = (bf16[2048,512]{1,0:T(8,128)(2,1)S(1)}, bf16[2048,512]{1,0:T(8,128)(2,1)}, u32[]{:S(2)}, u32[]{:S(2)}) collective-permute-start(bf16[2048,512]{1,0:T(8,128)(2,1)S(1)} %copy-done), channel_id=1, source_target_pairs={{0,2},{1,3},{2,0},{3,1},{4,6},{5,7},{6,4},{7,5},{8,10},{9,11},{10,... | collective-permute-start | bytes 6291464 | tf_op jit(solution)/shard_map/ppermute | solution.py:646
  14.7 60.7 %collective-permute-start.7 = (bf16[2048,512]{1,0:T(8,128)(2,1)S(1)}, bf16[2048,512]{1,0:T(8,128)(2,1)}, u32[]{:S(2)}, u32[]{:S(2)}) collective-permute-start(bf16[2048,512]{1,0:T(8,128)(2,1)S(1)} %copy-done), channel_id=1, source_target_pairs={{0,1},{1,0},{2,3},{3,2},{4,5},{5,4},{6,7},{7,6},{8,9},{9,8},{10,11... | collective-permute-start | bytes 6291464 | tf_op jit(solution)/shard_map/ppermute | solution.py:646
  15.4 55.8 %collective-permute-start.4 = (bf16[1,256,512]{1,2,0:T(8,128)(2,1)S(1)}, bf16[1,256,512]{1,2,0:T(8,128)(2,1)S(1)}, u32[]{:S(2)}, u32[]{:S(2)}) collective-permute-start(bf16[1,256,512]{1,2,0:T(8,128)(2,1)S(1)} %get-tuple-element.623), channel_id=1, source_target_pairs={{0,16},{16,0},{1,17},{17,1},{2,18},{18,2},{3,19},{19,3},{4,20},{20... | collective-permute-start | bytes 786440 | tf_op jit(solution)/shard_map/ppermute | solution.py:646
  18.6 52.6 %collective-permute-start.3 = (bf16[1,16,256]{2,1,0:T(8,128)(2,1)S(1)}, bf16[1,16,256]{2,1,0:T(8,128)(2,1)S(1)}, u32[]{:S(2)}, u32[]{:S(2)}) collective-permute-start(bf16[1,16,256]{2,1,0:T(8,128)(2,1)S(1)} %get-tuple-element.621), channel_id=1, source_target_pairs={{0,16},{16,0},{1,17},{17,1},{2,18},{18,2},{3,19},{19,3},{4,20},{20... | collective-permute-start | bytes 24584 | tf_op jit(solution)/shard_map/ppermute | solution.py:646
  127.4 340.0 %all-gather.10.cloned.1.call-start = ((), (), s32[]{:S(2)}) async-start(), calls=%async_computation.4 | async-start | bytes 18874368 | tf_op jit(solution)/shard_map/all_gather | solution.py:1021
  196.9 71.8 %collective-permute-start.11 = (bf16[256,3072]{1,0:T(8,128)(2,1)S(1)}, bf16[256,3072]{1,0:T(8,128)(2,1)}, u32[]{:S(2)}, u32[]{:S(2)}) collective-permute-start(bf16[256,3072]{1,0:T(8,128)(2,1)S(1)} %get-tuple-element.646.refs_0_), channel_id=1, source_target_pairs={{0,16},{16,0},{1,17},{17,1},{2,18},{18,2},{3,19},{19,3},{4,20},{20... | collective-permute-start | bytes 4718600 | tf_op jit(solution)/shard_map/ppermute | solution.py:646
  200.5 68.2 %collective-permute-start.12 = (bf16[256,3072]{1,0:T(8,128)(2,1)S(1)}, bf16[256,3072]{1,0:T(8,128)(2,1)S(1)}, u32[]{:S(2)}, u32[]{:S(2)}) collective-permute-start(bf16[256,3072]{1,0:T(8,128)(2,1)S(1)} %get-tuple-element.646.refs_0_), channel_id=1, source_target_pairs={{0,4},{4,0},{1,5},{5,1},{2,6},{6,2},{3,7},{7,3},{8,12},{12,8},{9,1... | collective-permute-start | bytes 4718600 | tf_op jit(solution)/shard_map/ppermute | solution.py:646
  201.7 75.1 %collective-permute-start.13 = (bf16[256,3072]{1,0:T(8,128)(2,1)S(1)}, bf16[256,3072]{1,0:T(8,128)(2,1)}, u32[]{:S(2)}, u32[]{:S(2)}) collective-permute-start(bf16[256,3072]{1,0:T(8,128)(2,1)S(1)} %get-tuple-element.645), channel_id=1, source_target_pairs={{0,8},{8,0},{1,9},{9,1},{2,10},{10,2},{3,11},{11,3},{4,12},{12,4},... | collective-permute-start | bytes 4718600 | tf_op jit(solution)/shard_map/ppermute | solution.py:646
  202.3 53.1 %collective-permute-start.17 = (bf16[1,1024,512]{2,1,0:T(8,128)(2,1)S(1)}, bf16[1,1024,512]{2,1,0:T(8,128)(2,1)S(1)}, u32[]{:S(2)}, u32[]{:S(2)}) collective-permute-start(bf16[1,1024,512]{2,1,0:T(8,128)(2,1)S(1)} %fusion.69), channel_id=1, source_target_pairs={{0,2},{1,3},{2,0},{3,1},{4,6},{5,7},{6,4},{7,5},{8,10},{9,11},{10,... | collective-permute-start | bytes 3145736 | tf_op jit(solution)/shard_map/ppermute | solution.py:646
  278.9 1022.8 %reduce-scatter.2.cloned.1.call-start = ((), (), s32[]{:S(2)}) async-start(), calls=%async_computation.2 | async-start | bytes 18874368 | tf_op jit(solution)/shard_map/reduce_scatter | solution.py:1188
  292.6 71.5 %collective-permute-start.23 = (bf16[256,3072]{1,0:T(8,128)(2,1)}, bf16[256,3072]{1,0:T(8,128)(2,1)}, u32[]{:S(2)}, u32[]{:S(2)}) collective-permute-start(bf16[256,3072]{1,0:T(8,128)(2,1)} %collective-permute-done.13.refs_4_), channel_id=1, source_target_pairs={{0,16},{16,0},{1,17},{17,1},{2,18},{18,2},{3,19},{19,3},{4,20},{20... | collective-permute-start | bytes 4718600 | tf_op jit(solution)/shard_map/ppermute | solution.py:646
  295.3 68.8 %collective-permute-start.24 = (bf16[256,3072]{1,0:T(8,128)(2,1)}, bf16[256,3072]{1,0:T(8,128)(2,1)}, u32[]{:S(2)}, u32[]{:S(2)}) collective-permute-start(bf16[256,3072]{1,0:T(8,128)(2,1)} %collective-permute-done.13.refs_4_), channel_id=1, source_target_pairs={{0,4},{4,0},{1,5},{5,1},{2,6},{6,2},{3,7},{7,3},{8,12},{12,8},{9,1... | collective-permute-start | bytes 4718600 | tf_op jit(solution)/shard_map/ppermute | solution.py:646
  297.4 134.9 %collective-permute-start.27 = (bf16[256,3072]{1,0:T(8,128)(2,1)}, bf16[256,3072]{1,0:T(8,128)(2,1)}, u32[]{:S(2)}, u32[]{:S(2)}) collective-permute-start(bf16[256,3072]{1,0:T(8,128)(2,1)} %get-tuple-element.331), channel_id=1, source_target_pairs={{0,8},{8,0},{1,9},{9,1},{2,10},{10,2},{3,11},{11,3},{4,12},{12,4},... | collective-permute-start | bytes 4718600 | tf_op jit(solution)/shard_map/ppermute | solution.py:646
  364.1 69.0 %collective-permute-start.26 = (bf16[256,3072]{1,0:T(8,128)(2,1)}, bf16[256,3072]{1,0:T(8,128)(2,1)}, u32[]{:S(2)}, u32[]{:S(2)}) collective-permute-start(bf16[256,3072]{1,0:T(8,128)(2,1)} %collective-permute-done.23.refs_5_), channel_id=1, source_target_pairs={{0,4},{4,0},{1,5},{5,1},{2,6},{6,2},{3,7},{7,3},{8,12},{12,8},{9,1... | collective-permute-start | bytes 4718600 | tf_op jit(solution)/shard_map/ppermute | solution.py:646
  365.8 66.5 %collective-permute-start.25 = (f32[4,17,2048]{2,0,1:T(4,128)}, f32[4,17,2048]{2,0,1:T(4,128)S(1)}, u32[]{:S(2)}, u32[]{:S(2)}) collective-permute-start(f32[4,17,2048]{2,0,1:T(4,128)} %copy.103), channel_id=1, source_target_pairs={{0,2},{1,3},{2,0},{3,1},{4,6},{5,7},{6,4},{7,5},{8,10},{9,11},{10,... | collective-permute-start | bytes 1671176 | tf_op jit(solution)/shard_map/ppermute | solution.py:646
  370.8 90.0 %collective-permute-start.30 = (bf16[256,3072]{1,0:T(8,128)(2,1)}, bf16[256,3072]{1,0:T(8,128)(2,1)}, u32[]{:S(2)}, u32[]{:S(2)}) collective-permute-start(bf16[256,3072]{1,0:T(8,128)(2,1)} %get-tuple-element.377.refs_0_), channel_id=1, source_target_pairs={{0,16},{16,0},{1,17},{17,1},{2,18},{18,2},{3,19},{19,3},{4,20},{20... | collective-permute-start | bytes 4718600 | tf_op jit(solution)/shard_map/ppermute | solution.py:646
  374.2 189.8 %collective-permute-start.32 = (bf16[256,3072]{1,0:T(8,128)(2,1)}, bf16[256,3072]{1,0:T(8,128)(2,1)}, u32[]{:S(2)}, u32[]{:S(2)}) collective-permute-start(bf16[256,3072]{1,0:T(8,128)(2,1)} %get-tuple-element.377.refs_0_), channel_id=1, source_target_pairs={{0,4},{4,0},{1,5},{5,1},{2,6},{6,2},{3,7},{7,3},{8,12},{12,8},{9,1... | collective-permute-start | bytes 4718600 | tf_op jit(solution)/shard_map/ppermute | solution.py:646
  438.3 125.7 %collective-permute-start.28 = (bf16[256,3072]{1,0:T(8,128)(2,1)}, bf16[256,3072]{1,0:T(8,128)(2,1)}, u32[]{:S(2)}, u32[]{:S(2)}) collective-permute-start(bf16[256,3072]{1,0:T(8,128)(2,1)} %collective-permute-done.27.refs_4_), channel_id=1, source_target_pairs={{0,16},{16,0},{1,17},{17,1},{2,18},{18,2},{3,19},{19,3},{4,20},{20... | collective-permute-start | bytes 4718600 | tf_op jit(solution)/shard_map/ppermute | solution.py:646
  439.5 124.5 %collective-permute-start.29 = (bf16[256,3072]{1,0:T(8,128)(2,1)}, bf16[256,3072]{1,0:T(8,128)(2,1)}, u32[]{:S(2)}, u32[]{:S(2)}) collective-permute-start(bf16[256,3072]{1,0:T(8,128)(2,1)} %collective-permute-done.27.refs_4_), channel_id=1, source_target_pairs={{0,4},{4,0},{1,5},{5,1},{2,6},{6,2},{3,7},{7,3},{8,12},{12,8},{9,1... | collective-permute-start | bytes 4718600 | tf_op jit(solution)/shard_map/ppermute | solution.py:646
  460.7 103.3 %collective-permute-start.31 = (bf16[256,3072]{1,0:T(8,128)(2,1)}, bf16[256,3072]{1,0:T(8,128)(2,1)}, u32[]{:S(2)}, u32[]{:S(2)}) collective-permute-start(bf16[256,3072]{1,0:T(8,128)(2,1)} %collective-permute-done.30.refs_1_), channel_id=1, source_target_pairs={{0,4},{4,0},{1,5},{5,1},{2,6},{6,2},{3,7},{7,3},{8,12},{12,8},{9,1... | collective-permute-start | bytes 4718600 | tf_op jit(solution)/shard_map/ppermute | solution.py:646
  564.1 50.1 %collective-permute-start.33 = (bf16[256,3072]{1,0:T(8,128)(2,1)}, bf16[256,3072]{1,0:T(8,128)(2,1)}, u32[]{:S(2)}, u32[]{:S(2)}) collective-permute-start(bf16[256,3072]{1,0:T(8,128)(2,1)} %collective-permute-done.28.refs_5_), channel_id=1, source_target_pairs={{0,4},{4,0},{1,5},{5,1},{2,6},{6,2},{3,7},{7,3},{8,12},{12,8},{9,1... | collective-permute-start | bytes 4718600 | tf_op jit(solution)/shard_map/ppermute | solution.py:646
  620.2 84.3 %collective-permute-start.34 = (bf16[2,256,3072]{2,1,0:T(8,128)(2,1)}, bf16[2,256,3072]{2,1,0:T(8,128)(2,1)}, u32[]{:S(2)}, u32[]{:S(2)}) collective-permute-start(bf16[2,256,3072]{2,1,0:T(8,128)(2,1)} %get-tuple-element.630), channel_id=1, source_target_pairs={{0,4},{4,0},{1,5},{5,1},{2,6},{6,2},{3,7},{7,3},{8,12},{12,8},{9,1... | collective-permute-start | bytes 9437192 | tf_op jit(solution)/shard_map/ppermute | solution.py:646
  726.5 81.2 %collective-permute-start.35 = (bf16[2,2,1024,512]{3,2,1,0:T(8,128)(2,1)}, bf16[2,2,1024,512]{3,2,1,0:T(8,128)(2,1)}, u32[]{:S(2)}, u32[]{:S(2)}) collective-permute-start(bf16[2,2,1024,512]{3,2,1,0:T(8,128)(2,1)} %get-tuple-element.409), channel_id=1, source_target_pairs={{0,1},{1,0},{2,3},{3,2},{4,5},{5,4},{6,7},{7,6},{8,9},{9,8},{10,11... | collective-permute-start | bytes 12582920 | tf_op jit(solution)/shard_map/ppermute | solution.py:646
  726.5 81.2 %collective-permute-start.36 = (bf16[2,2,1024,512]{3,2,1,0:T(8,128)(2,1)}, bf16[2,2,1024,512]{3,2,1,0:T(8,128)(2,1)}, u32[]{:S(2)}, u32[]{:S(2)}) collective-permute-start(bf16[2,2,1024,512]{3,2,1,0:T(8,128)(2,1)} %get-tuple-element.410), channel_id=1, source_target_pairs={{0,1},{1,0},{2,3},{3,2},{4,5},{5,4},{6,7},{7,6},{8,9},{9,8},{10,11... | collective-permute-start | bytes 12582920 | tf_op jit(solution)/shard_map/ppermute | solution.py:646
  727.0 80.7 %collective-permute-start.39 = (bf16[2,256,3072]{2,1,0:T(8,128)(2,1)}, bf16[2,256,3072]{2,1,0:T(8,128)(2,1)}, u32[]{:S(2)}, u32[]{:S(2)}) collective-permute-start(bf16[2,256,3072]{2,1,0:T(8,128)(2,1)} %get-tuple-element.416), channel_id=1, source_target_pairs={{0,4},{4,0},{1,5},{5,1},{2,6},{6,2},{3,7},{7,3},{8,12},{12,8},{9,1... | collective-permute-start | bytes 9437192 | tf_op jit(solution)/shard_map/ppermute | solution.py:646
  735.8 71.9 %collective-permute-start.38 = (bf16[1,256,3072]{2,1,0:T(8,128)(2,1)}, bf16[1,256,3072]{2,1,0:T(8,128)(2,1)}, u32[]{:S(2)}, u32[]{:S(2)}) collective-permute-start(bf16[1,256,3072]{2,1,0:T(8,128)(2,1)} %slice.499), channel_id=1, source_target_pairs={{0,16},{16,0},{1,17},{17,1},{2,18},{18,2},{3,19},{19,3},{4,20},{20... | collective-permute-start | bytes 4718600 | tf_op jit(solution)/shard_map/ppermute | solution.py:646
  753.2 51.8 %collective-permute-start.37 = (f32[1,6,2048]{2,1,0:T(8,128)S(1)}, f32[1,6,2048]{2,1,0:T(8,128)S(1)}, u32[]{:S(2)}, u32[]{:S(2)}) collective-permute-start(f32[1,6,2048]{2,1,0:T(8,128)S(1)} %broadcast_in_dim_reshape.3), channel_id=1, source_target_pairs={{0,8},{8,0},{1,9},{9,1},{2,10},{10,2},{3,11},{11,3},{4,12},{12,4},... | collective-permute-start | bytes 147464 | tf_op jit(solution)/shard_map/ppermute | solution.py:646
  817.4 61.8 %collective-permute-start.41 = (bf16[2,1024,512]{2,1,0:T(8,128)(2,1)}, bf16[2,1024,512]{2,1,0:T(8,128)(2,1)S(1)}, u32[]{:S(2)}, u32[]{:S(2)}) collective-permute-start(bf16[2,1024,512]{2,1,0:T(8,128)(2,1)} %get-tuple-element.634), channel_id=1, source_target_pairs={{0,8},{8,0},{1,9},{9,1},{2,10},{10,2},{3,11},{11,3},{4,12},{12,4},... | collective-permute-start | bytes 6291464 | tf_op jit(solution)/shard_map/ppermute | solution.py:646
  823.2 56.0 %collective-permute-start.40 = (bf16[2,1024,512]{2,1,0:T(8,128)(2,1)}, bf16[2,1024,512]{2,1,0:T(8,128)(2,1)S(1)}, u32[]{:S(2)}, u32[]{:S(2)}) collective-permute-start(bf16[2,1024,512]{2,1,0:T(8,128)(2,1)} %get-tuple-element.636), channel_id=1, source_target_pairs={{0,2},{1,3},{2,0},{3,1},{4,6},{5,7},{6,4},{7,5},{8,10},{9,11},{10,... | collective-permute-start | bytes 6291464 | tf_op jit(solution)/shard_map/ppermute | solution.py:646
  828.7 70.8 %collective-permute-start.47 = (bf16[2,256,3072]{2,1,0:T(8,128)(2,1)}, bf16[2,256,3072]{2,1,0:T(8,128)(2,1)}, u32[]{:S(2)}, u32[]{:S(2)}) collective-permute-start(bf16[2,256,3072]{2,1,0:T(8,128)(2,1)} %get-tuple-element.628), channel_id=1, source_target_pairs={{0,4},{4,0},{1,5},{5,1},{2,6},{6,2},{3,7},{7,3},{8,12},{12,8},{9,1... | collective-permute-start | bytes 9437192 | tf_op jit(solution)/shard_map/ppermute | solution.py:646
  830.7 47.2 %collective-permute-start.43 = (f32[4,6,2048]{2,1,0:T(8,128)}, f32[4,6,2048]{2,1,0:T(8,128)}, u32[]{:S(2)}, u32[]{:S(2)}) collective-permute-start(f32[4,6,2048]{2,1,0:T(8,128)} %pad_maximum_fusion.17), channel_id=1, source_target_pairs={{0,2},{1,3},{2,0},{3,1},{4,6},{5,7},{6,4},{7,5},{8,10},{9,11},{10,... | collective-permute-start | bytes 589832 | tf_op jit(solution)/shard_map/ppermute | solution.py:646
  879.2 71.4 %collective-permute-start.52 = (bf16[1,256,3072]{2,1,0:T(8,128)(2,1)}, bf16[1,256,3072]{2,1,0:T(8,128)(2,1)}, u32[]{:S(2)}, u32[]{:S(2)}) collective-permute-start(bf16[1,256,3072]{2,1,0:T(8,128)(2,1)} %slice.501), channel_id=1, source_target_pairs={{0,16},{16,0},{1,17},{17,1},{2,18},{18,2},{3,19},{19,3},{4,20},{20... | collective-permute-start | bytes 4718600 | tf_op jit(solution)/shard_map/ppermute | solution.py:646
  888.7 48.6 %collective-permute-start.45 = (bf16[1024,512]{1,0:T(8,128)(2,1)}, bf16[1024,512]{1,0:T(8,128)(2,1)}, u32[]{:S(2)}, u32[]{:S(2)}) collective-permute-start(bf16[1024,512]{1,0:T(8,128)(2,1)} %fusion.67), channel_id=1, source_target_pairs={{0,8},{8,0},{1,9},{9,1},{2,10},{10,2},{3,11},{11,3},{4,12},{12,4},... | collective-permute-start | bytes 3145736 | tf_op jit(solution)/shard_map/ppermute | solution.py:646
  948.1 46.3 %collective-permute-start.51 = (bf16[2048,512]{1,0:T(8,128)(2,1)S(1)}, bf16[2048,512]{1,0:T(8,128)(2,1)S(1)}, u32[]{:S(2)}, u32[]{:S(2)}) collective-permute-start(bf16[2048,512]{1,0:T(8,128)(2,1)S(1)} %get-tuple-element.632), channel_id=1, source_target_pairs={{0,2},{1,3},{2,0},{3,1},{4,6},{5,7},{6,4},{7,5},{8,10},{9,11},{10,... | collective-permute-start | bytes 6291464 | tf_op jit(solution)/shard_map/ppermute | solution.py:646
  999.6 95.6 %collective-permute-start.44 = (bf16[256,3072]{1,0:T(8,128)(2,1)}, bf16[256,3072]{1,0:T(8,128)(2,1)}, u32[]{:S(2)}, u32[]{:S(2)}) collective-permute-start(bf16[256,3072]{1,0:T(8,128)(2,1)} %fusion.59), channel_id=1, source_target_pairs={{0,8},{8,0},{1,9},{9,1},{2,10},{10,2},{3,11},{11,3},{4,12},{12,4},... | collective-permute-start | bytes 4718600 | tf_op jit(solution)/shard_map/ppermute | solution.py:646
  1002.1 93.1 %collective-permute-start.49 = (bf16[2,256,3072]{2,1,0:T(8,128)(2,1)}, bf16[2,256,3072]{2,1,0:T(8,128)(2,1)}, u32[]{:S(2)}, u32[]{:S(2)}) collective-permute-start(bf16[2,256,3072]{2,1,0:T(8,128)(2,1)} %get-tuple-element.446), channel_id=1, source_target_pairs={{0,4},{4,0},{1,5},{5,1},{2,6},{6,2},{3,7},{7,3},{8,12},{12,8},{9,1... | collective-permute-start | bytes 9437192 | tf_op jit(solution)/shard_map/ppermute | solution.py:646
  1002.6 92.6 %collective-permute-start.48 = (bf16[1,256,3072]{2,1,0:T(8,128)(2,1)}, bf16[1,256,3072]{2,1,0:T(8,128)(2,1)}, u32[]{:S(2)}, u32[]{:S(2)}) collective-permute-start(bf16[1,256,3072]{2,1,0:T(8,128)(2,1)} %slice.504), channel_id=1, source_target_pairs={{0,16},{16,0},{1,17},{17,1},{2,18},{18,2},{3,19},{19,3},{4,20},{20... | collective-permute-start | bytes 4718600 | tf_op jit(solution)/shard_map/ppermute | solution.py:646
  1133.8 71.9 %collective-permute-start.64 = (bf16[1,256,3072]{2,1,0:T(8,128)(2,1)S(1)}, bf16[1,256,3072]{2,1,0:T(8,128)(2,1)}, u32[]{:S(2)}, u32[]{:S(2)}) collective-permute-start(bf16[1,256,3072]{2,1,0:T(8,128)(2,1)S(1)} %slice.519), channel_id=1, source_target_pairs={{0,16},{16,0},{1,17},{17,1},{2,18},{18,2},{3,19},{19,3},{4,20},{20... | collective-permute-start | bytes 4718600 | tf_op jit(solution)/shard_map/ppermute | solution.py:646
  1181.1 78.1 %collective-permute-start.58 = (bf16[1,2048,512]{2,1,0:T(8,128)(2,1)S(1)}, bf16[1,2048,512]{2,1,0:T(8,128)(2,1)S(1)}, u32[]{:S(2)}, u32[]{:S(2)}) collective-permute-start(bf16[1,2048,512]{2,1,0:T(8,128)(2,1)S(1)} %get-tuple-element.624), channel_id=1, source_target_pairs={{0,2},{1,3},{2,0},{3,1},{4,6},{5,7},{6,4},{7,5},{8,10},{9,11},{10,... | collective-permute-start | bytes 6291464 | tf_op jit(solution)/shard_map/ppermute | solution.py:646
  1182.8 76.4 %collective-permute-start.59 = (bf16[2,2,256,1024]{3,2,1,0:T(8,128)(2,1)S(1)}, bf16[2,2,256,1024]{3,2,1,0:T(8,128)(2,1)S(1)}, u32[]{:S(2)}, u32[]{:S(2)}) collective-permute-start(bf16[2,2,256,1024]{3,2,1,0:T(8,128)(2,1)S(1)} %slice_bitcast_fusion.8), channel_id=1, source_target_pairs={{0,4},{4,0},{1,5},{5,1},{2,6},{6,2},{3,7},{7,3},{8,12},{12,8},{9,1... | collective-permute-start | bytes 6291464 | tf_op jit(solution)/shard_map/ppermute | solution.py:646
  1183.9 77.3 %collective-permute-start.60 = (bf16[2,2,256,1024]{3,2,1,0:T(8,128)(2,1)S(1)}, bf16[2,2,256,1024]{3,2,1,0:T(8,128)(2,1)S(1)}, u32[]{:S(2)}, u32[]{:S(2)}) collective-permute-start(bf16[2,2,256,1024]{3,2,1,0:T(8,128)(2,1)S(1)} %slice_bitcast_fusion.7), channel_id=1, source_target_pairs={{0,8},{8,0},{1,9},{9,1},{2,10},{10,2},{3,11},{11,3},{4,12},{12,4},... | collective-permute-start | bytes 6291464 | tf_op jit(solution)/shard_map/ppermute | solution.py:646
  1211.0 48.2 %collective-permute-start.63 = (f32[19,2048]{1,0:T(8,128)S(1)}, f32[19,2048]{1,0:T(8,128)S(1)}, u32[]{:S(2)}, u32[]{:S(2)}) collective-permute-start(f32[19,2048]{1,0:T(8,128)S(1)} %pad_maximum_fusion.18), channel_id=1, source_target_pairs={{0,3},{1,2},{2,1},{3,0},{4,7},{5,6},{6,5},{7,4},{8,11},{9,10},{10,... | collective-permute-start | bytes 466952 | tf_op jit(solution)/shard_map/ppermute | solution.py:646
  1291.7 68.5 %collective-permute-start.73 = (bf16[256,3072]{1,0:T(8,128)(2,1)}, bf16[256,3072]{1,0:T(8,128)(2,1)}, u32[]{:S(2)}, u32[]{:S(2)}) collective-permute-start(bf16[256,3072]{1,0:T(8,128)(2,1)} %fusion.60), channel_id=1, source_target_pairs={{0,8},{8,0},{1,9},{9,1},{2,10},{10,2},{3,11},{11,3},{4,12},{12,4},... | collective-permute-start | bytes 4718600 | tf_op jit(solution)/shard_map/ppermute | solution.py:646
  1305.2 64.4 %collective-permute-start.71 = (bf16[256,1024]{1,0:T(8,128)(2,1)}, bf16[256,1024]{1,0:T(8,128)(2,1)S(1)}, u32[]{:S(2)}, u32[]{:S(2)}) collective-permute-start(bf16[256,1024]{1,0:T(8,128)(2,1)} %fusion.76), channel_id=1, source_target_pairs={{0,16},{16,0},{1,17},{17,1},{2,18},{18,2},{3,19},{19,3},{4,20},{20... | collective-permute-start | bytes 1572872 | tf_op jit(solution)/shard_map/ppermute | solution.py:646
  1311.3 59.1 %collective-permute-start.70 = (bf16[256,1024]{1,0:T(8,128)(2,1)}, bf16[256,1024]{1,0:T(8,128)(2,1)}, u32[]{:S(2)}, u32[]{:S(2)}) collective-permute-start(bf16[256,1024]{1,0:T(8,128)(2,1)} %fusion.75), channel_id=1, source_target_pairs={{0,16},{16,0},{1,17},{17,1},{2,18},{18,2},{3,19},{19,3},{4,20},{20... | collective-permute-start | bytes 1572872 | tf_op jit(solution)/shard_map/ppermute | solution.py:646
  1312.0 57.6 %collective-permute-start.72 = (f32[19,2048]{1,0:T(8,128)S(1)}, f32[19,2048]{1,0:T(8,128)S(1)}, u32[]{:S(2)}, u32[]{:S(2)}) collective-permute-start(f32[19,2048]{1,0:T(8,128)S(1)} %add_add_fusion), channel_id=1, source_target_pairs={{0,16},{16,0},{1,17},{17,1},{2,18},{18,2},{3,19},{19,3},{4,20},{20... | collective-permute-start | bytes 466952 | tf_op jit(solution)/shard_map/ppermute | solution.py:646
  (123 other events, 1764.4 us)
Sparse Core Ops, SparseCore 0:
  11.7 115.5 all-gather.5
  128.9 99.2 all-gather.7
  279.0 188.3 all-gather.9
  995.9 248.5 reduce-scatter.1

commit v2 on v1

--- a/solution.py
+++ b/solution.py
@@ -1027,7 +1027,7 @@
         live,
         [stat_flow, weight_flows[0, 0]] + firsts,
         [lambda: compact(starts, where, pos_row, moe_cot, groups, cols)],
-        sync=seconds[:1],
+        sync=seconds,
     )
     for flow in seconds[:1]:
         flow.step(2)
@@ -1146,11 +1146,11 @@
         [lambda: expand_all(starts, where, pos_col, live["result"], groups, cols)],
         sync=[scalar_flow] + early,
     )
+    live["moe_branch"] = branch_parts.reshape(groups * cols, tok_rows, width)
+    while moe_in_flow.sends is not None:
+        stage(live, [moe_in_flow], sync=early + late)
     for flow in early[1:]:
         flow.step()
-    live["moe_branch"] = branch_parts.reshape(groups * cols, tok_rows, width)
-    while moe_in_flow.sends is not None:
-        stage(live, [moe_in_flow], sync=late)
     scalar_all = scalar_flow.finish().reshape(groups, cols, each + 1, groups, tok_rows)
     scalar_all = jnp.stack([scalar_all[place, :, :, place] for place in range(groups)])
     by_expert = jnp.stack(
@@ -1182,7 +1182,6 @@
             lambda: dot_of(scaled_logit, scaled_rows, 1, 0),
             lambda: jnp.sum(back * middle, axis=0)[None],
         ],
-        sync=early[1:],
     )
     cot_blocks = cot_flow.finish()
     moe_branch = lax.psum_scatter(
@@ -1220,6 +1219,7 @@
         live,
         early[:1] + late,
         [functools.partial(attend_back, s) for s in range(seqs)],
+        sync=early[1:],
     )
     share = width // (mids * depth)
     cot_places = [((n // share) ^ col) * share + n % share for n in blocks_here]

time: 1400 us -> 1440 us (1.029)
  waiting for transfers between devices: 491 us -> 548 us
  starting transfers between devices: 95.5 us -> 74.5 us
    ppermute x74, waiting for transfers between devices: 482 us -> 540 us  [swap(): return lax.ppermute(values, axis, [(n, n ^ bit) for n in range(size)])]
    ppermute x74, starting transfers between devices: 95.2 us -> 74.2 us  [swap(): return lax.ppermute(values, axis, [(n, n ^ bit) for n in range(size)])]
  transfers between devices with their start and end apart: 78 -> 78, of which waited for: 30 -> 30; matrix products, arithmetic and copies ran while one was open for 17% -> 16% of each run, Pallas kernels for 34% -> 33%
where the time goes in v2:
time: 1440 us; the launch traced here: 1430 us
  waiting for transfers between devices  548 us (38%)
  Pallas kernels  490 us (34%)
  other arithmetic  142 us (10%)
  local copies, waits for them, and re-layouts  95.9 us (7%)
  starting transfers between devices  74.5 us (5%)
  matrix products  59.8 us (4%)
  between operations  16 us (1%)
    ppermute x74, waiting for transfers between devices, swap(): return lax.ppermute(values, axis, [(n, n ^ bit) for n in range(size)])  540 us
    pallas_call x2, Pallas kernels, expert_step(): pl.pallas_call(functools.partial(expert_kernel, count, hidden), grid_spec...  155 us
    pallas_call x3, Pallas kernels, weight_grads(): pl.pallas_call(functools.partial(weight_grad_kernel, mids), grid_spec=plt...  127 us
    ppermute x74, starting transfers between devices, swap(): return lax.ppermute(values, axis, [(n, n ^ bit) for n in range(size)])  74.2 us
    pallas_call x2, Pallas kernels, attend_backward(): pl.pallas_call(attend_backward_kernel, grid_spec=pltpu.PrefetchScalarGrid...  64.3 us
    dot_general x9, matrix products, dot_of(): lax.dot_general(a, b, (((da,), (db,)), ((), ())), preferred_element_type=...  59.8 us
    pallas_call x2, Pallas kernels, compact(): pl.pallas_call(compact_kernel, grid_spec=pltpu.PrefetchScalarGridSpec(num...  38.3 us
    pallas_call x2, Pallas kernels, attend_forward(): pl.pallas_call(attend_forward_kernel, grid_spec=pltpu.PrefetchScalarGridS...  36.2 us
  transfers between devices with their start and end apart: 78, of which 30 were waited for; matrix products, arithmetic and copies ran while one was open for 16% of the time, Pallas kernels for 33%

profile of v2, /device:TPU:0, one launch (start us, length us, event | category | flops | bytes accessed | tf_op | source)
XLA Modules:
  0.0 1426.5 jit_solution(15091994521606991610)
XLA Ops:
  25.8 34.6 %collective-permute-done.1 = f32[512]{0:T(512)S(1)} collective-permute-done((f32[512]{0:T(512)S(1)}, f32[512]{0:T(512)S(1)}, u32[]{:S(2)}, u32[]{:S(2)}) %collective-permute-start.1) | collective-permute-done | bytes 2080 | tf_op jit(solution)/shard_map/ppermute | solution.py:646
  62.9 8.3 pack_weights.1
  97.7 20.9 %collective-permute-done.5 = bf16[2,16,256]{2,1,0:T(8,128)(2,1)S(1)} collective-permute-done((bf16[2,16,256]{2,1,0:T(8,128)(2,1)S(1)}, bf16[2,16,256]{2,1,0:T(8,128)(2,1)S(1)}, u32[]{:S(2)}, u32[]{:S(2)}) %collective-permute-start.5) | collective-permute-done | bytes 16416 | tf_op jit(solution)/shard_map/ppermute | solution.py:646
  118.6 8.7 all-gather.6.cloned.1.call-done
  130.5 19.3 %fusion.110.q_ref.k_ref.v_ref = f32[2048,1536]{1,0:T(8,128)} fusion(bf16[2048,2048]{1,0:T(8,128)(2,1)} %fusion.43.x_ref, bf16[2048,1536]{1,0:T(8,128)(2,1)} %all-gather.6.cloned.1.call-done), kind=kOutput, calls=%fused_computation.307 | convolution fusion | flops 12884901888 | bytes 27262976 | tf_op jit(solution)/shard_map/dot_general | solution.py:36
  149.8 18.0 %attend_forward.2 = (bf16[1024,512]{1,0:T(8,128)(2,1)}, bf16[1024,512]{1,0:T(8,128)(2,1)}, bf16[1024,512]{1,0:T(8,128)(2,1)}, bf16[1024,512]{1,0:T(8,128)(2,1)}) custom-call(s32[1]{0:T(128)} %get-tuple-element.681.live_ref, f32[2048,1536]{1,0:T(8,128)} %fusion.110.q_ref.k_ref.v_ref, f32[2048,1536]{1,0:T(8,128)} %fusion.110.q_ref.k_ref.v_ref, ...), custom_call_target="tpu_custom_call" | custom-call | flops 85899344 | bytes 209715 | tf_op jit(solution)/shard_map/attend_forward/pallas_call | solution.py:96
  167.8 18.2 %attend_forward.3 = (bf16[1024,512]{1,0:T(8,128)(2,1)}, bf16[1024,512]{1,0:T(8,128)(2,1)}, bf16[1024,512]{1,0:T(8,128)(2,1)}, bf16[1024,512]{1,0:T(8,128)(2,1)}) custom-call(s32[1]{0:T(128)} %get-tuple-element.680.live_ref, f32[2048,1536]{1,0:T(8,128)} %fusion.110.q_ref.k_ref.v_ref, f32[2048,1536]{1,0:T(8,128)} %fusion.110.q_ref.k_ref.v_ref, ...), custom_call_target="tpu_custom_call" | custom-call | flops 85899344 | bytes 209715 | tf_op jit(solution)/shard_map/attend_forward/pallas_call | solution.py:96
  203.8 29.3 %collective-permute-done.19 = bf16[1,1024,512]{2,1,0:T(8,128)(2,1)S(1)} collective-permute-done((bf16[1,1024,512]{2,1,0:T(8,128)(2,1)S(1)}, bf16[1,1024,512]{2,1,0:T(8,128)(2,1)S(1)}, u32[]{:S(2)}, u32[]{:S(2)}) %collective-permute-start.19) | collective-permute-done | bytes 1048608 | tf_op jit(solution)/shard_map/ppermute | solution.py:646
  233.6 21.7 %collective-permute-done.17 = bf16[1,1024,512]{2,1,0:T(8,128)(2,1)S(1)} collective-permute-done((bf16[1,1024,512]{2,1,0:T(8,128)(2,1)S(1)}, bf16[1,1024,512]{2,1,0:T(8,128)(2,1)S(1)}, u32[]{:S(2)}, u32[]{:S(2)}) %collective-permute-start.17) | collective-permute-done | bytes 1048608 | tf_op jit(solution)/shard_map/ppermute | solution.py:646
  255.9 12.8 collective-permute-done.11.refs_1_
  269.9 6.9 collective-permute-done.13.refs_4_
  297.4 19.2 %compact.2 = (bf16[2304,2048]{1,0:T(8,128)(2,1)}, bf16[2304,2048]{1,0:T(8,128)(2,1)}) custom-call(s32[4,16]{1,0:T(4,128)} %fusion.93.start_ref, s32[2]{0:T(128)} %pad_add_fusion.1.where_ref, s32[2,2,1,2048]{3,2,1,0:T(1,128)} %select_n.148.pos_ref, bf16[8,2048,512]{2,1,0:T(8,128)(2,1)} %bitcast.346), custom_call_target="tpu_custom_call" | custom-call | flops 193273536 | bytes 713031 | tf_op jit(solution)/shard_map/compact/pallas_call | solution.py:260
  316.6 12.2 collective-permute-done.22.refs_3_
  328.8 34.7 %collective-permute-done.23.refs_5_ = bf16[256,3072]{1,0:T(8,128)(2,1)} collective-permute-done((bf16[256,3072]{1,0:T(8,128)(2,1)}, bf16[256,3072]{1,0:T(8,128)(2,1)}, u32[]{:S(2)}, u32[]{:S(2)}) %collective-permute-start.23) | collective-permute-done | bytes 1572896 | tf_op jit(solution)/shard_map/ppermute | solution.py:646
  374.9 10.5 collective-permute-done.25
  385.4 15.7 %collective-permute-done.26.refs_7_ = bf16[256,3072]{1,0:T(8,128)(2,1)} collective-permute-done((bf16[256,3072]{1,0:T(8,128)(2,1)}, bf16[256,3072]{1,0:T(8,128)(2,1)}, u32[]{:S(2)}, u32[]{:S(2)}) %collective-permute-start.26) | collective-permute-done | bytes 1572896 | tf_op jit(solution)/shard_map/ppermute | solution.py:646
  401.1 59.9 %collective-permute-done.27.refs_4_ = bf16[256,3072]{1,0:T(8,128)(2,1)} collective-permute-done((bf16[256,3072]{1,0:T(8,128)(2,1)}, bf16[256,3072]{1,0:T(8,128)(2,1)}, u32[]{:S(2)}, u32[]{:S(2)}) %collective-permute-start.27) | collective-permute-done | bytes 1572896 | tf_op jit(solution)/shard_map/ppermute | solution.py:646
  472.3 5.7 compact_scalars.1
  483.5 19.1 %compact.3 = (bf16[2304,2048]{1,0:T(8,128)(2,1)}, bf16[2304,2048]{1,0:T(8,128)(2,1)}) custom-call(s32[4,16]{1,0:T(4,128)} %fusion.93.start_ref, s32[2]{0:T(128)} %pad_add_fusion.1.where_ref, s32[2,2,1,2048]{3,2,1,0:T(1,128)} %select_n.148.pos_ref, bf16[8,2048,512]{2,1,0:T(8,128)(2,1)} %bitcast.347), custom_call_target="tpu_custom_call" | custom-call | flops 193273536 | bytes 713031 | tf_op jit(solution)/shard_map/compact/pallas_call | solution.py:260
  502.6 77.5 %expert_step.2 = (bf16[2304,2048]{1,0:T(8,128)(2,1)}, bf16[2304,2048]{1,0:T(8,128)(2,1)}, bf16[2304,1024]{1,0:T(8,128)(2,1)}, f32[2304,1]{1,0:T(8,128)}, f32[2304,1]{1,0:T(8,128)}, /*index=5*/bf16[2304,2048]{1,0:T(8,128)(2,1)}) custom-call(s32[8]{0:T(128)} %stack.252.row_ref, bf16[2304,2048]{1,0:T(8,128)(2,1)} %get-tuple-element.369.x_ref, ...), custom_call_target="tpu_custom_call" | custom-call | flops 1159641216 | bytes 1038090 | tf_op jit(solution)/shard_map/expert_step/pallas_call | solution.py:555
  582.3 47.5 %weight_grads.3 = bf16[2,2,2,256,3072]{4,3,2,1,0:T(8,128)(2,1)} custom-call(s32[9]{0:T(128)} %stack.258.place_ref, bf16[2304,2048]{1,0:T(8,128)(2,1)} %get-tuple-element.369.x_ref, bf16[2304,2048]{1,0:T(8,128)(2,1)} %get-tuple-element.370.m_ref, bf16[2304,2048]{1,0:T(8,128)(2,1)} %get-tuple-element.371.pre_ref, bf16[2304,1024]{1,0:T(8,128)(2,1)} %get-tuple-element.372.act_ref), custom_call_target="tpu_custom_call" | custom-call | flops 579820608 | bytes 660602 | tf_op jit(solution)/shard_map/weight_grads/pallas_call | solution.py:619
  629.8 6.0 slice_bitcast_fusion.2
  642.9 77.7 %expert_step.3 = (bf16[2304,2048]{1,0:T(8,128)(2,1)}, bf16[2304,2048]{1,0:T(8,128)(2,1)}, bf16[2304,1024]{1,0:T(8,128)(2,1)}, f32[2304,1]{1,0:T(8,128)}, f32[2304,1]{1,0:T(8,128)}, /*index=5*/bf16[2304,2048]{1,0:T(8,128)(2,1)}) custom-call(s32[8]{0:T(128)} %stack.259.row_ref, bf16[2304,2048]{1,0:T(8,128)(2,1)} %get-tuple-element.421.x_ref, ...), custom_call_target="tpu_custom_call" | custom-call | flops 1159641216 | bytes 1038090 | tf_op jit(solution)/shard_map/expert_step/pallas_call | solution.py:555
  724.0 18.7 %expand.1 = (bf16[2,2,1024,512]{3,2,1,0:T(8,128)(2,1)}, bf16[2,2,1024,512]{3,2,1,0:T(8,128)(2,1)}, bf16[2,2,1024,512]{3,2,1,0:T(8,128)(2,1)}, bf16[2,2,1024,512]{3,2,1,0:T(8,128)(2,1)}) custom-call(s32[4,16]{1,0:T(4,128)} %fusion.93.start_ref, s32[2]{0:T(128)} %pad_add_fusion.1.where_ref, s32[2,2,2048,1]{3,2,1,0:T(8,128)} %copy.111.pos_ref, ...), custom_call_target="tpu_custom_call" | custom-call | flops 193273536 | bytes 713031 | tf_op jit(solution)/shard_map/expand/pallas_call | solution.py:378
  758.3 6.4 expand_scalars.1
  768.0 47.6 %weight_grads.4 = bf16[2,2,2,256,3072]{4,3,2,1,0:T(8,128)(2,1)} custom-call(s32[9]{0:T(128)} %stack.258.place_ref, bf16[2304,2048]{1,0:T(8,128)(2,1)} %get-tuple-element.421.x_ref, bf16[2304,2048]{1,0:T(8,128)(2,1)} %get-tuple-element.422.m_ref, bf16[2304,2048]{1,0:T(8,128)(2,1)} %get-tuple-element.423.pre_ref, bf16[2304,1024]{1,0:T(8,128)(2,1)} %get-tuple-element.424.act_ref), custom_call_target="tpu_custom_call" | custom-call | flops 579820608 | bytes 660602 | tf_op jit(solution)/shard_map/weight_grads/pallas_call | solution.py:619
  815.5 6.9 collective-permute-done.38
  832.1 5.1 fusion.39
  849.4 20.3 %expand_all.1 = bf16[2,4,2048,512]{3,2,1,0:T(8,128)(2,1)} custom-call(s32[4,16]{1,0:T(4,128)} %fusion.93.start_ref, s32[2]{0:T(128)} %pad_add_fusion.1.where_ref, s32[2,2,2048,1]{3,2,1,0:T(8,128)} %copy.111.pos_ref, bf16[2304,2048]{1,0:T(8,128)(2,1)} %get-tuple-element.433.refs_0_, bf16[2304,2048]{1,0:T(8,128)(2,1)} %get-tuple-element.434.refs_1_), custom_call_target="tpu_custom_call" | custom-call | flops 193273536 | bytes 713031 | tf_op jit(solution)/shard_map/expand_all/pallas_call | solution.py:415
  869.7 21.0 %collective-permute-done.43 = f32[4,6,2048]{2,1,0:T(8,128)} collective-permute-done((f32[4,6,2048]{2,1,0:T(8,128)}, f32[4,6,2048]{2,1,0:T(8,128)}, u32[]{:S(2)}, u32[]{:S(2)}) %collective-permute-start.43) | collective-permute-done | bytes 196640 | tf_op jit(solution)/shard_map/ppermute | solution.py:646
  903.2 8.8 collective-permute-done.46
  937.8 44.4 %collective-permute-done.51 = bf16[2048,512]{1,0:T(8,128)(2,1)S(1)} collective-permute-done((bf16[2048,512]{1,0:T(8,128)(2,1)S(1)}, bf16[2048,512]{1,0:T(8,128)(2,1)S(1)}, u32[]{:S(2)}, u32[]{:S(2)}) %collective-permute-start.51) | collective-permute-done | bytes 2097184 | tf_op jit(solution)/shard_map/ppermute | solution.py:646
  990.6 61.5 %collective-permute-done.53 = bf16[1,256,3072]{2,1,0:T(8,128)(2,1)S(1)} collective-permute-done((bf16[1,256,3072]{2,1,0:T(8,128)(2,1)}, bf16[1,256,3072]{2,1,0:T(8,128)(2,1)S(1)}, u32[]{:S(2)}, u32[]{:S(2)}) %collective-permute-start.53) | collective-permute-done | bytes 1572896 | tf_op jit(solution)/shard_map/ppermute | solution.py:646
  1069.7 31.9 %attend_backward.3 = (bf16[1024,512]{1,0:T(8,128)(2,1)}, bf16[1024,512]{1,0:T(8,128)(2,1)}, bf16[1024,512]{1,0:T(8,128)(2,1)}, f32[1,128]{1,0:T(1,128)}, f32[1,128]{1,0:T(1,128)}, /*index=5*/f32[1024,1]{1,0:T(8,128)}) custom-call(s32[1]{0:T(128)} %get-tuple-element.680.live_ref, bf16[1024,512]{1,0:T(8,128)(2,1)} %get-tuple-element.471.ql_ref, ...), custom_call_target="tpu_custom_call" | custom-call | flops 214748368 | bytes 251658 | tf_op jit(solution)/shard_map/attend_backward/pallas_call | solution.py:214
  1102.9 6.3 fusion.61.do_ref
  1109.2 32.3 %attend_backward.2 = (bf16[1024,512]{1,0:T(8,128)(2,1)}, bf16[1024,512]{1,0:T(8,128)(2,1)}, bf16[1024,512]{1,0:T(8,128)(2,1)}, f32[1,128]{1,0:T(1,128)}, f32[1,128]{1,0:T(1,128)}, /*index=5*/f32[1024,1]{1,0:T(8,128)}) custom-call(s32[1]{0:T(128)} %get-tuple-element.681.live_ref, bf16[1024,512]{1,0:T(8,128)(2,1)} %get-tuple-element.453.ql_ref, ...), custom_call_target="tpu_custom_call" | custom-call | flops 214748368 | bytes 251658 | tf_op jit(solution)/shard_map/attend_backward/pallas_call | solution.py:214
  1149.4 18.7 %fusion.111 = f32[2048,2048]{1,0:T(8,128)S(1)} fusion(bf16[2048,1536]{1,0:T(8,128)(2,1)} %constant_dynamic-update-slice_fusion.10.pre_ref, bf16[2048,1536]{1,0:T(8,128)(2,1)} %pad_maximum_fusion.1), kind=kOutput, calls=%fused_computation.308 | convolution fusion | flops 12884901888 | bytes 29360128 | tf_op jit(solution)/shard_map/dot_general | solution.py:36
  1168.1 5.8 copy-done.9
  1190.1 32.0 %weight_grads.5 = bf16[2,2,2,256,2048]{4,3,2,1,0:T(8,128)(2,1)} custom-call(s32[9]{0:T(128)} %stack.302.place_ref, bf16[2048,2048]{1,0:T(8,128)(2,1)} %fusion.43.x_ref, bf16[2048,2048]{1,0:T(8,128)(2,1)} %copy-done.10, bf16[2048,1536]{1,0:T(8,128)(2,1)} %constant_dynamic-update-slice_fusion.10.pre_ref, bf16[2048,512]{1,0:T(8,128)(2,1)} %pad_maximum_fusion.7.act_ref), custom_call_target="tpu_custom_call" | custom-call | flops 343597376 | bytes 503316 | tf_op jit(solution)/shard_map/weight_grads/pallas_call | solution.py:619
  1222.2 10.0 fusion.19
  1236.6 19.4 %collective-permute-done.64 = bf16[1,256,3072]{2,1,0:T(8,128)(2,1)} collective-permute-done((bf16[1,256,3072]{2,1,0:T(8,128)(2,1)S(1)}, bf16[1,256,3072]{2,1,0:T(8,128)(2,1)}, u32[]{:S(2)}, u32[]{:S(2)}) %collective-permute-start.64) | collective-permute-done | bytes 1572896 | tf_op jit(solution)/shard_map/ppermute | solution.py:646
  1261.7 23.1 %collective-permute-done.62 = f32[19,2048]{1,0:T(8,128)S(1)} collective-permute-done((f32[19,2048]{1,0:T(8,128)S(1)}, f32[19,2048]{1,0:T(8,128)S(1)}, u32[]{:S(2)}, u32[]{:S(2)}) %collective-permute-start.62) | collective-permute-done | bytes 155680 | tf_op jit(solution)/shard_map/ppermute | solution.py:646
  1288.2 12.5 collective-permute-done.60
  1308.8 7.3 fusion.25
  1316.1 15.2 %collective-permute-done.67 = f32[19,2048]{1,0:T(8,128)S(1)} collective-permute-done((f32[19,2048]{1,0:T(8,128)S(1)}, f32[19,2048]{1,0:T(8,128)S(1)}, u32[]{:S(2)}, u32[]{:S(2)}) %collective-permute-start.67) | collective-permute-done | bytes 155680 | tf_op jit(solution)/shard_map/ppermute | solution.py:646
  1334.2 5.0 collective-permute-done.69
  1351.0 47.1 %collective-permute-done.73.refs_3_ = bf16[256,3072]{1,0:T(8,128)(2,1)} collective-permute-done((bf16[256,3072]{1,0:T(8,128)(2,1)}, bf16[256,3072]{1,0:T(8,128)(2,1)}, u32[]{:S(2)}, u32[]{:S(2)}) %collective-permute-start.73) | collective-permute-done | bytes 1572896 | tf_op jit(solution)/shard_map/ppermute | solution.py:646
  1398.0 9.5 unpack_grads.1
  (542 shorter events, 309.5 us)
Async XLA Ops:
  7.2 120.1 %all-gather.6.cloned.1.call-start = ((), (), s32[]{:S(2)}) async-start(), calls=%async_computation.1 | async-start | bytes 7077888 | tf_op jit(solution)/shard_map/all_gather | solution.py:908
  11.6 285.8 %all-gather.8.cloned.1.call-start = ((), (), s32[]{:S(2)}) async-start(), calls=%async_computation.3 | async-start | bytes 18874368 | tf_op jit(solution)/shard_map/all_gather | solution.py:968
  11.7 59.5 %collective-permute-start = (bf16[2048,512]{1,0:T(8,128)(2,1)S(1)}, bf16[2048,512]{1,0:T(8,128)(2,1)}, u32[]{:S(2)}, u32[]{:S(2)}) collective-permute-start(bf16[2048,512]{1,0:T(8,128)(2,1)S(1)} %copy-done), channel_id=1, source_target_pairs={{0,2},{1,3},{2,0},{3,1},{4,6},{5,7},{6,4},{7,5},{8,10},{9,11},{10,... | collective-permute-start | bytes 6291464 | tf_op jit(solution)/shard_map/ppermute | solution.py:646
  14.7 60.7 %collective-permute-start.7 = (bf16[2048,512]{1,0:T(8,128)(2,1)S(1)}, bf16[2048,512]{1,0:T(8,128)(2,1)}, u32[]{:S(2)}, u32[]{:S(2)}) collective-permute-start(bf16[2048,512]{1,0:T(8,128)(2,1)S(1)} %copy-done), channel_id=1, source_target_pairs={{0,1},{1,0},{2,3},{3,2},{4,5},{5,4},{6,7},{7,6},{8,9},{9,8},{10,11... | collective-permute-start | bytes 6291464 | tf_op jit(solution)/shard_map/ppermute | solution.py:646
  15.4 55.8 %collective-permute-start.4 = (bf16[1,256,512]{1,2,0:T(8,128)(2,1)S(1)}, bf16[1,256,512]{1,2,0:T(8,128)(2,1)S(1)}, u32[]{:S(2)}, u32[]{:S(2)}) collective-permute-start(bf16[1,256,512]{1,2,0:T(8,128)(2,1)S(1)} %get-tuple-element.629), channel_id=1, source_target_pairs={{0,16},{16,0},{1,17},{17,1},{2,18},{18,2},{3,19},{19,3},{4,20},{20... | collective-permute-start | bytes 786440 | tf_op jit(solution)/shard_map/ppermute | solution.py:646
  18.6 52.6 %collective-permute-start.3 = (bf16[1,16,256]{2,1,0:T(8,128)(2,1)S(1)}, bf16[1,16,256]{2,1,0:T(8,128)(2,1)S(1)}, u32[]{:S(2)}, u32[]{:S(2)}) collective-permute-start(bf16[1,16,256]{2,1,0:T(8,128)(2,1)S(1)} %get-tuple-element.627), channel_id=1, source_target_pairs={{0,16},{16,0},{1,17},{17,1},{2,18},{18,2},{3,19},{19,3},{4,20},{20... | collective-permute-start | bytes 24584 | tf_op jit(solution)/shard_map/ppermute | solution.py:646
  72.5 46.1 %collective-permute-start.6 = (bf16[2,256,512]{1,2,0:T(8,128)(2,1)S(1)}, bf16[2,256,512]{1,2,0:T(8,128)(2,1)S(1)}, u32[]{:S(2)}, u32[]{:S(2)}) collective-permute-start(bf16[2,256,512]{1,2,0:T(8,128)(2,1)S(1)} %pad_maximum_fusion.14), channel_id=1, source_target_pairs={{0,8},{8,0},{1,9},{9,1},{2,10},{10,2},{3,11},{11,3},{4,12},{12,4},... | collective-permute-start | bytes 1572872 | tf_op jit(solution)/shard_map/ppermute | solution.py:646
  127.4 356.1 %all-gather.10.cloned.1.call-start = ((), (), s32[]{:S(2)}) async-start(), calls=%async_computation.4 | async-start | bytes 18874368 | tf_op jit(solution)/shard_map/all_gather | solution.py:1021
  196.9 71.8 %collective-permute-start.11 = (bf16[256,3072]{1,0:T(8,128)(2,1)S(1)}, bf16[256,3072]{1,0:T(8,128)(2,1)}, u32[]{:S(2)}, u32[]{:S(2)}) collective-permute-start(bf16[256,3072]{1,0:T(8,128)(2,1)S(1)} %get-tuple-element.652.refs_0_), channel_id=1, source_target_pairs={{0,16},{16,0},{1,17},{17,1},{2,18},{18,2},{3,19},{19,3},{4,20},{20... | collective-permute-start | bytes 4718600 | tf_op jit(solution)/shard_map/ppermute | solution.py:646
  200.5 68.2 %collective-permute-start.12 = (bf16[256,3072]{1,0:T(8,128)(2,1)S(1)}, bf16[256,3072]{1,0:T(8,128)(2,1)S(1)}, u32[]{:S(2)}, u32[]{:S(2)}) collective-permute-start(bf16[256,3072]{1,0:T(8,128)(2,1)S(1)} %get-tuple-element.652.refs_0_), channel_id=1, source_target_pairs={{0,4},{4,0},{1,5},{5,1},{2,6},{6,2},{3,7},{7,3},{8,12},{12,8},{9,1... | collective-permute-start | bytes 4718600 | tf_op jit(solution)/shard_map/ppermute | solution.py:646
  201.7 75.1 %collective-permute-start.13 = (bf16[256,3072]{1,0:T(8,128)(2,1)S(1)}, bf16[256,3072]{1,0:T(8,128)(2,1)}, u32[]{:S(2)}, u32[]{:S(2)}) collective-permute-start(bf16[256,3072]{1,0:T(8,128)(2,1)S(1)} %get-tuple-element.651), channel_id=1, source_target_pairs={{0,8},{8,0},{1,9},{9,1},{2,10},{10,2},{3,11},{11,3},{4,12},{12,4},... | collective-permute-start | bytes 4718600 | tf_op jit(solution)/shard_map/ppermute | solution.py:646
  202.3 53.1 %collective-permute-start.17 = (bf16[1,1024,512]{2,1,0:T(8,128)(2,1)S(1)}, bf16[1,1024,512]{2,1,0:T(8,128)(2,1)S(1)}, u32[]{:S(2)}, u32[]{:S(2)}) collective-permute-start(bf16[1,1024,512]{2,1,0:T(8,128)(2,1)S(1)} %fusion.69), channel_id=1, source_target_pairs={{0,2},{1,3},{2,0},{3,1},{4,6},{5,7},{6,4},{7,5},{8,10},{9,11},{10,... | collective-permute-start | bytes 3145736 | tf_op jit(solution)/shard_map/ppermute | solution.py:646
  278.9 1060.9 %reduce-scatter.2.cloned.1.call-start = ((), (), s32[]{:S(2)}) async-start(), calls=%async_computation.2 | async-start | bytes 18874368 | tf_op jit(solution)/shard_map/reduce_scatter | solution.py:1187
  292.6 70.8 %collective-permute-start.23 = (bf16[256,3072]{1,0:T(8,128)(2,1)}, bf16[256,3072]{1,0:T(8,128)(2,1)}, u32[]{:S(2)}, u32[]{:S(2)}) collective-permute-start(bf16[256,3072]{1,0:T(8,128)(2,1)} %collective-permute-done.13.refs_4_), channel_id=1, source_target_pairs={{0,16},{16,0},{1,17},{17,1},{2,18},{18,2},{3,19},{19,3},{4,20},{20... | collective-permute-start | bytes 4718600 | tf_op jit(solution)/shard_map/ppermute | solution.py:646
  295.3 68.1 %collective-permute-start.24 = (bf16[256,3072]{1,0:T(8,128)(2,1)}, bf16[256,3072]{1,0:T(8,128)(2,1)}, u32[]{:S(2)}, u32[]{:S(2)}) collective-permute-start(bf16[256,3072]{1,0:T(8,128)(2,1)} %collective-permute-done.13.refs_4_), channel_id=1, source_target_pairs={{0,4},{4,0},{1,5},{5,1},{2,6},{6,2},{3,7},{7,3},{8,12},{12,8},{9,1... | collective-permute-start | bytes 4718600 | tf_op jit(solution)/shard_map/ppermute | solution.py:646
  363.9 97.1 %collective-permute-start.27 = (bf16[256,3072]{1,0:T(8,128)(2,1)}, bf16[256,3072]{1,0:T(8,128)(2,1)}, u32[]{:S(2)}, u32[]{:S(2)}) collective-permute-start(bf16[256,3072]{1,0:T(8,128)(2,1)} %get-tuple-element.335), channel_id=1, source_target_pairs={{0,8},{8,0},{1,9},{9,1},{2,10},{10,2},{3,11},{11,3},{4,12},{12,4},... | collective-permute-start | bytes 4718600 | tf_op jit(solution)/shard_map/ppermute | solution.py:646
  371.3 106.7 %collective-permute-start.30 = (bf16[256,3072]{1,0:T(8,128)(2,1)}, bf16[256,3072]{1,0:T(8,128)(2,1)}, u32[]{:S(2)}, u32[]{:S(2)}) collective-permute-start(bf16[256,3072]{1,0:T(8,128)(2,1)} %get-tuple-element.381.refs_0_), channel_id=1, source_target_pairs={{0,16},{16,0},{1,17},{17,1},{2,18},{18,2},{3,19},{19,3},{4,20},{20... | collective-permute-start | bytes 4718600 | tf_op jit(solution)/shard_map/ppermute | solution.py:646
  373.4 206.7 %collective-permute-start.32 = (bf16[256,3072]{1,0:T(8,128)(2,1)}, bf16[256,3072]{1,0:T(8,128)(2,1)}, u32[]{:S(2)}, u32[]{:S(2)}) collective-permute-start(bf16[256,3072]{1,0:T(8,128)(2,1)} %get-tuple-element.381.refs_0_), channel_id=1, source_target_pairs={{0,4},{4,0},{1,5},{5,1},{2,6},{6,2},{3,7},{7,3},{8,12},{12,8},{9,1... | collective-permute-start | bytes 4718600 | tf_op jit(solution)/shard_map/ppermute | solution.py:646
  466.3 113.9 %collective-permute-start.28 = (bf16[256,3072]{1,0:T(8,128)(2,1)}, bf16[256,3072]{1,0:T(8,128)(2,1)}, u32[]{:S(2)}, u32[]{:S(2)}) collective-permute-start(bf16[256,3072]{1,0:T(8,128)(2,1)} %collective-permute-done.27.refs_4_), channel_id=1, source_target_pairs={{0,16},{16,0},{1,17},{17,1},{2,18},{18,2},{3,19},{19,3},{4,20},{20... | collective-permute-start | bytes 4718600 | tf_op jit(solution)/shard_map/ppermute | solution.py:646
  468.0 112.1 %collective-permute-start.29 = (bf16[256,3072]{1,0:T(8,128)(2,1)}, bf16[256,3072]{1,0:T(8,128)(2,1)}, u32[]{:S(2)}, u32[]{:S(2)}) collective-permute-start(bf16[256,3072]{1,0:T(8,128)(2,1)} %collective-permute-done.27.refs_4_), channel_id=1, source_target_pairs={{0,4},{4,0},{1,5},{5,1},{2,6},{6,2},{3,7},{7,3},{8,12},{12,8},{9,1... | collective-permute-start | bytes 4718600 | tf_op jit(solution)/shard_map/ppermute | solution.py:646
  478.0 102.1 %collective-permute-start.31 = (bf16[256,3072]{1,0:T(8,128)(2,1)}, bf16[256,3072]{1,0:T(8,128)(2,1)}, u32[]{:S(2)}, u32[]{:S(2)}) collective-permute-start(bf16[256,3072]{1,0:T(8,128)(2,1)} %collective-permute-done.30.refs_1_), channel_id=1, source_target_pairs={{0,4},{4,0},{1,5},{5,1},{2,6},{6,2},{3,7},{7,3},{8,12},{12,8},{9,1... | collective-permute-start | bytes 4718600 | tf_op jit(solution)/shard_map/ppermute | solution.py:646
  580.2 49.6 %collective-permute-start.33 = (bf16[256,3072]{1,0:T(8,128)(2,1)}, bf16[256,3072]{1,0:T(8,128)(2,1)}, u32[]{:S(2)}, u32[]{:S(2)}) collective-permute-start(bf16[256,3072]{1,0:T(8,128)(2,1)} %collective-permute-done.28.refs_5_), channel_id=1, source_target_pairs={{0,4},{4,0},{1,5},{5,1},{2,6},{6,2},{3,7},{7,3},{8,12},{12,8},{9,1... | collective-permute-start | bytes 4718600 | tf_op jit(solution)/shard_map/ppermute | solution.py:646
  635.8 84.9 %collective-permute-start.34 = (bf16[2,256,3072]{2,1,0:T(8,128)(2,1)}, bf16[2,256,3072]{2,1,0:T(8,128)(2,1)}, u32[]{:S(2)}, u32[]{:S(2)}) collective-permute-start(bf16[2,256,3072]{2,1,0:T(8,128)(2,1)} %get-tuple-element.636), channel_id=1, source_target_pairs={{0,4},{4,0},{1,5},{5,1},{2,6},{6,2},{3,7},{7,3},{8,12},{12,8},{9,1... | collective-permute-start | bytes 9437192 | tf_op jit(solution)/shard_map/ppermute | solution.py:646
  742.6 79.8 %collective-permute-start.35 = (bf16[2,2,1024,512]{3,2,1,0:T(8,128)(2,1)}, bf16[2,2,1024,512]{3,2,1,0:T(8,128)(2,1)}, u32[]{:S(2)}, u32[]{:S(2)}) collective-permute-start(bf16[2,2,1024,512]{3,2,1,0:T(8,128)(2,1)} %get-tuple-element.413), channel_id=1, source_target_pairs={{0,1},{1,0},{2,3},{3,2},{4,5},{5,4},{6,7},{7,6},{8,9},{9,8},{10,11... | collective-permute-start | bytes 12582920 | tf_op jit(solution)/shard_map/ppermute | solution.py:646
  742.6 79.8 %collective-permute-start.36 = (bf16[2,2,1024,512]{3,2,1,0:T(8,128)(2,1)}, bf16[2,2,1024,512]{3,2,1,0:T(8,128)(2,1)}, u32[]{:S(2)}, u32[]{:S(2)}) collective-permute-start(bf16[2,2,1024,512]{3,2,1,0:T(8,128)(2,1)} %get-tuple-element.414), channel_id=1, source_target_pairs={{0,1},{1,0},{2,3},{3,2},{4,5},{5,4},{6,7},{7,6},{8,9},{9,8},{10,11... | collective-permute-start | bytes 12582920 | tf_op jit(solution)/shard_map/ppermute | solution.py:646
  743.1 79.3 %collective-permute-start.39 = (bf16[2,256,3072]{2,1,0:T(8,128)(2,1)}, bf16[2,256,3072]{2,1,0:T(8,128)(2,1)}, u32[]{:S(2)}, u32[]{:S(2)}) collective-permute-start(bf16[2,256,3072]{2,1,0:T(8,128)(2,1)} %get-tuple-element.420), channel_id=1, source_target_pairs={{0,4},{4,0},{1,5},{5,1},{2,6},{6,2},{3,7},{7,3},{8,12},{12,8},{9,1... | collective-permute-start | bytes 9437192 | tf_op jit(solution)/shard_map/ppermute | solution.py:646
  751.4 71.0 %collective-permute-start.38 = (bf16[1,256,3072]{2,1,0:T(8,128)(2,1)}, bf16[1,256,3072]{2,1,0:T(8,128)(2,1)}, u32[]{:S(2)}, u32[]{:S(2)}) collective-permute-start(bf16[1,256,3072]{2,1,0:T(8,128)(2,1)} %slice.499), channel_id=1, source_target_pairs={{0,16},{16,0},{1,17},{17,1},{2,18},{18,2},{3,19},{19,3},{4,20},{20... | collective-permute-start | bytes 4718600 | tf_op jit(solution)/shard_map/ppermute | solution.py:646
  766.5 49.0 %collective-permute-start.37 = (f32[1,6,2048]{2,1,0:T(8,128)S(1)}, f32[1,6,2048]{2,1,0:T(8,128)S(1)}, u32[]{:S(2)}, u32[]{:S(2)}) collective-permute-start(f32[1,6,2048]{2,1,0:T(8,128)S(1)} %broadcast_in_dim_reshape.3), channel_id=1, source_target_pairs={{0,8},{8,0},{1,9},{9,1},{2,10},{10,2},{3,11},{11,3},{4,12},{12,4},... | collective-permute-start | bytes 147464 | tf_op jit(solution)/shard_map/ppermute | solution.py:646
  832.1 59.9 %collective-permute-start.41 = (bf16[2,1024,512]{2,1,0:T(8,128)(2,1)}, bf16[2,1024,512]{2,1,0:T(8,128)(2,1)S(1)}, u32[]{:S(2)}, u32[]{:S(2)}) collective-permute-start(bf16[2,1024,512]{2,1,0:T(8,128)(2,1)} %get-tuple-element.640), channel_id=1, source_target_pairs={{0,8},{8,0},{1,9},{9,1},{2,10},{10,2},{3,11},{11,3},{4,12},{12,4},... | collective-permute-start | bytes 6291464 | tf_op jit(solution)/shard_map/ppermute | solution.py:646
  837.2 54.8 %collective-permute-start.40 = (bf16[2,1024,512]{2,1,0:T(8,128)(2,1)}, bf16[2,1024,512]{2,1,0:T(8,128)(2,1)S(1)}, u32[]{:S(2)}, u32[]{:S(2)}) collective-permute-start(bf16[2,1024,512]{2,1,0:T(8,128)(2,1)} %get-tuple-element.641), channel_id=1, source_target_pairs={{0,2},{1,3},{2,0},{3,1},{4,6},{5,7},{6,4},{7,5},{8,10},{9,11},{10,... | collective-permute-start | bytes 6291464 | tf_op jit(solution)/shard_map/ppermute | solution.py:646
  842.4 69.6 %collective-permute-start.46 = (bf16[2,256,3072]{2,1,0:T(8,128)(2,1)}, bf16[2,256,3072]{2,1,0:T(8,128)(2,1)}, u32[]{:S(2)}, u32[]{:S(2)}) collective-permute-start(bf16[2,256,3072]{2,1,0:T(8,128)(2,1)} %get-tuple-element.634), channel_id=1, source_target_pairs={{0,4},{4,0},{1,5},{5,1},{2,6},{6,2},{3,7},{7,3},{8,12},{12,8},{9,1... | collective-permute-start | bytes 9437192 | tf_op jit(solution)/shard_map/ppermute | solution.py:646
  843.7 47.0 %collective-permute-start.43 = (f32[4,6,2048]{2,1,0:T(8,128)}, f32[4,6,2048]{2,1,0:T(8,128)}, u32[]{:S(2)}, u32[]{:S(2)}) collective-permute-start(f32[4,6,2048]{2,1,0:T(8,128)} %pad_maximum_fusion.17), channel_id=1, source_target_pairs={{0,2},{1,3},{2,0},{3,1},{4,6},{5,7},{6,4},{7,5},{8,10},{9,11},{10,... | collective-permute-start | bytes 589832 | tf_op jit(solution)/shard_map/ppermute | solution.py:646
  936.5 45.8 %collective-permute-start.51 = (bf16[2048,512]{1,0:T(8,128)(2,1)S(1)}, bf16[2048,512]{1,0:T(8,128)(2,1)S(1)}, u32[]{:S(2)}, u32[]{:S(2)}) collective-permute-start(bf16[2048,512]{1,0:T(8,128)(2,1)S(1)} %get-tuple-element.638), channel_id=1, source_target_pairs={{0,2},{1,3},{2,0},{3,1},{4,6},{5,7},{6,4},{7,5},{8,10},{9,11},{10,... | collective-permute-start | bytes 6291464 | tf_op jit(solution)/shard_map/ppermute | solution.py:646
  983.6 68.5 %collective-permute-start.53 = (bf16[1,256,3072]{2,1,0:T(8,128)(2,1)}, bf16[1,256,3072]{2,1,0:T(8,128)(2,1)S(1)}, u32[]{:S(2)}, u32[]{:S(2)}) collective-permute-start(bf16[1,256,3072]{2,1,0:T(8,128)(2,1)} %slice.502), channel_id=1, source_target_pairs={{0,16},{16,0},{1,17},{17,1},{2,18},{18,2},{3,19},{19,3},{4,20},{20... | collective-permute-start | bytes 4718600 | tf_op jit(solution)/shard_map/ppermute | solution.py:646
  984.8 76.0 %collective-permute-start.50 = (bf16[2048,512]{1,0:T(8,128)(2,1)}, bf16[2048,512]{1,0:T(8,128)(2,1)S(1)}, u32[]{:S(2)}, u32[]{:S(2)}) collective-permute-start(bf16[2048,512]{1,0:T(8,128)(2,1)} %copy-done.29), channel_id=1, source_target_pairs={{0,1},{1,0},{2,3},{3,2},{4,5},{5,4},{6,7},{7,6},{8,9},{9,8},{10,11... | collective-permute-start | bytes 6291464 | tf_op jit(solution)/shard_map/ppermute | solution.py:646
  984.8 76.0 %collective-permute-start.52 = (bf16[2048,512]{1,0:T(8,128)(2,1)}, bf16[2048,512]{1,0:T(8,128)(2,1)S(1)}, u32[]{:S(2)}, u32[]{:S(2)}) collective-permute-start(bf16[2048,512]{1,0:T(8,128)(2,1)} %copy-done.45), channel_id=1, source_target_pairs={{0,1},{1,0},{2,3},{3,2},{4,5},{5,4},{6,7},{7,6},{8,9},{9,8},{10,11... | collective-permute-start | bytes 6291464 | tf_op jit(solution)/shard_map/ppermute | solution.py:646
  988.0 157.6 %collective-permute-start.49 = (bf16[2,256,3072]{2,1,0:T(8,128)(2,1)}, bf16[2,256,3072]{2,1,0:T(8,128)(2,1)}, u32[]{:S(2)}, u32[]{:S(2)}) collective-permute-start(bf16[2,256,3072]{2,1,0:T(8,128)(2,1)} %get-tuple-element.452), channel_id=1, source_target_pairs={{0,4},{4,0},{1,5},{5,1},{2,6},{6,2},{3,7},{7,3},{8,12},{12,8},{9,1... | collective-permute-start | bytes 9437192 | tf_op jit(solution)/shard_map/ppermute | solution.py:646
  988.7 156.9 %collective-permute-start.47 = (bf16[256,3072]{1,0:T(8,128)(2,1)}, bf16[256,3072]{1,0:T(8,128)(2,1)}, u32[]{:S(2)}, u32[]{:S(2)}) collective-permute-start(bf16[256,3072]{1,0:T(8,128)(2,1)} %fusion.59), channel_id=1, source_target_pairs={{0,8},{8,0},{1,9},{9,1},{2,10},{10,2},{3,11},{11,3},{4,12},{12,4},... | collective-permute-start | bytes 4718600 | tf_op jit(solution)/shard_map/ppermute | solution.py:646
  1052.1 93.4 %collective-permute-start.48 = (bf16[1,256,3072]{2,1,0:T(8,128)(2,1)}, bf16[1,256,3072]{2,1,0:T(8,128)(2,1)}, u32[]{:S(2)}, u32[]{:S(2)}) collective-permute-start(bf16[1,256,3072]{2,1,0:T(8,128)(2,1)} %slice.504), channel_id=1, source_target_pairs={{0,16},{16,0},{1,17},{17,1},{2,18},{18,2},{3,19},{19,3},{4,20},{20... | collective-permute-start | bytes 4718600 | tf_op jit(solution)/shard_map/ppermute | solution.py:646
  1176.9 45.3 %collective-permute-start.54 = (bf16[2,2048,512]{2,1,0:T(8,128)(2,1)}, bf16[2,2048,512]{2,1,0:T(8,128)(2,1)}, u32[]{:S(2)}, u32[]{:S(2)}) collective-permute-start(bf16[2,2048,512]{2,1,0:T(8,128)(2,1)} %pad_maximum_fusion.2), channel_id=1, source_target_pairs={{0,1},{1,0},{2,3},{3,2},{4,5},{5,4},{6,7},{7,6},{8,9},{9,8},{10,11... | collective-permute-start | bytes 12582920 | tf_op jit(solution)/shard_map/ppermute | solution.py:646
  1183.7 72.3 %collective-permute-start.64 = (bf16[1,256,3072]{2,1,0:T(8,128)(2,1)S(1)}, bf16[1,256,3072]{2,1,0:T(8,128)(2,1)}, u32[]{:S(2)}, u32[]{:S(2)}) collective-permute-start(bf16[1,256,3072]{2,1,0:T(8,128)(2,1)S(1)} %slice.519), channel_id=1, source_target_pairs={{0,16},{16,0},{1,17},{17,1},{2,18},{18,2},{3,19},{19,3},{4,20},{20... | collective-permute-start | bytes 4718600 | tf_op jit(solution)/shard_map/ppermute | solution.py:646
  1232.1 56.1 %collective-permute-start.58 = (bf16[1,2048,512]{2,1,0:T(8,128)(2,1)S(1)}, bf16[1,2048,512]{2,1,0:T(8,128)(2,1)S(1)}, u32[]{:S(2)}, u32[]{:S(2)}) collective-permute-start(bf16[1,2048,512]{2,1,0:T(8,128)(2,1)S(1)} %get-tuple-element.630), channel_id=1, source_target_pairs={{0,2},{1,3},{2,0},{3,1},{4,6},{5,7},{6,4},{7,5},{8,10},{9,11},{10,... | collective-permute-start | bytes 6291464 | tf_op jit(solution)/shard_map/ppermute | solution.py:646
  1233.1 55.1 %collective-permute-start.59 = (bf16[2,2,256,1024]{3,2,1,0:T(8,128)(2,1)S(1)}, bf16[2,2,256,1024]{3,2,1,0:T(8,128)(2,1)S(1)}, u32[]{:S(2)}, u32[]{:S(2)}) collective-permute-start(bf16[2,2,256,1024]{3,2,1,0:T(8,128)(2,1)S(1)} %slice_bitcast_fusion.8), channel_id=1, source_target_pairs={{0,4},{4,0},{1,5},{5,1},{2,6},{6,2},{3,7},{7,3},{8,12},{12,8},{9,1... | collective-permute-start | bytes 6291464 | tf_op jit(solution)/shard_map/ppermute | solution.py:646
  1234.0 66.7 %collective-permute-start.60 = (bf16[2,2,256,1024]{3,2,1,0:T(8,128)(2,1)S(1)}, bf16[2,2,256,1024]{3,2,1,0:T(8,128)(2,1)S(1)}, u32[]{:S(2)}, u32[]{:S(2)}) collective-permute-start(bf16[2,2,256,1024]{3,2,1,0:T(8,128)(2,1)S(1)} %slice_bitcast_fusion.7), channel_id=1, source_target_pairs={{0,8},{8,0},{1,9},{9,1},{2,10},{10,2},{3,11},{11,3},{4,12},{12,4},... | collective-permute-start | bytes 6291464 | tf_op jit(solution)/shard_map/ppermute | solution.py:646
  1331.3 66.8 %collective-permute-start.73 = (bf16[256,3072]{1,0:T(8,128)(2,1)}, bf16[256,3072]{1,0:T(8,128)(2,1)}, u32[]{:S(2)}, u32[]{:S(2)}) collective-permute-start(bf16[256,3072]{1,0:T(8,128)(2,1)} %fusion.60), channel_id=1, source_target_pairs={{0,8},{8,0},{1,9},{9,1},{2,10},{10,2},{3,11},{11,3},{4,12},{12,4},... | collective-permute-start | bytes 4718600 | tf_op jit(solution)/shard_map/ppermute | solution.py:646
  1343.3 64.2 %collective-permute-start.71 = (bf16[256,1024]{1,0:T(8,128)(2,1)}, bf16[256,1024]{1,0:T(8,128)(2,1)S(1)}, u32[]{:S(2)}, u32[]{:S(2)}) collective-permute-start(bf16[256,1024]{1,0:T(8,128)(2,1)} %fusion.76), channel_id=1, source_target_pairs={{0,16},{16,0},{1,17},{17,1},{2,18},{18,2},{3,19},{19,3},{4,20},{20... | collective-permute-start | bytes 1572872 | tf_op jit(solution)/shard_map/ppermute | solution.py:646
  1347.9 60.4 %collective-permute-start.70 = (bf16[256,1024]{1,0:T(8,128)(2,1)}, bf16[256,1024]{1,0:T(8,128)(2,1)}, u32[]{:S(2)}, u32[]{:S(2)}) collective-permute-start(bf16[256,1024]{1,0:T(8,128)(2,1)} %fusion.75), channel_id=1, source_target_pairs={{0,16},{16,0},{1,17},{17,1},{2,18},{18,2},{3,19},{19,3},{4,20},{20... | collective-permute-start | bytes 1572872 | tf_op jit(solution)/shard_map/ppermute | solution.py:646
  1350.2 57.3 %collective-permute-start.72 = (f32[19,2048]{1,0:T(8,128)S(1)}, f32[19,2048]{1,0:T(8,128)S(1)}, u32[]{:S(2)}, u32[]{:S(2)}) collective-permute-start(f32[19,2048]{1,0:T(8,128)S(1)} %add_add_fusion), channel_id=1, source_target_pairs={{0,16},{16,0},{1,17},{17,1},{2,18},{18,2},{3,19},{19,3},{4,20},{20... | collective-permute-start | bytes 466952 | tf_op jit(solution)/shard_map/ppermute | solution.py:646
  (123 other events, 1741.7 us)
Sparse Core Ops, SparseCore 0:
  11.7 115.5 all-gather.5
  128.9 99.2 all-gather.7
  279.0 178.0 all-gather.9
  983.7 231.4 reduce-scatter.1

commit v3 on v1

--- a/solution.py
+++ b/solution.py
@@ -1146,8 +1146,6 @@
         [lambda: expand_all(starts, where, pos_col, live["result"], groups, cols)],
         sync=[scalar_flow] + early,
     )
-    for flow in early[1:]:
-        flow.step()
     live["moe_branch"] = branch_parts.reshape(groups * cols, tok_rows, width)
     while moe_in_flow.sends is not None:
         stage(live, [moe_in_flow], sync=late)
@@ -1182,7 +1180,6 @@
             lambda: dot_of(scaled_logit, scaled_rows, 1, 0),
             lambda: jnp.sum(back * middle, axis=0)[None],
         ],
-        sync=early[1:],
     )
     cot_blocks = cot_flow.finish()
     moe_branch = lax.psum_scatter(
@@ -1220,6 +1217,7 @@
         live,
         early[:1] + late,
         [functools.partial(attend_back, s) for s in range(seqs)],
+        sync=early[1:],
     )
     share = width // (mids * depth)
     cot_places = [((n // share) ^ col) * share + n % share for n in blocks_here]
@@ -1246,7 +1244,7 @@
             full = lax.dynamic_update_slice_in_dim(full, block, (col ^ place) * width, 1)
         return full
 
-    for flow in late:
+    for flow in late + early[1:]:
         flow.step()
     (partial,) = stage(live, [], [lambda: dot_of(live["qkv_cot"], live["qkv_rel"], 1, 1)])
     backs = [partial[:, n * width : (n + 1) * width] for n in range(cols)]
@@ -1283,7 +1281,7 @@
         small_flows.append(flow)
         return flow.holds()
 
-    (held,) = stage(live, [attn_flow, qkv_flow], [small_sums], sync=[late[1]])
+    (held,) = stage(live, [attn_flow, qkv_flow], [small_sums])
     (small_flow,) = small_flows
     small_flow.replace(held)
     live["moe_branch"] = moe_branch
@@ -1295,7 +1293,9 @@
             - hidden * (attn_inverse * attn_inverse * (inner_flow.finish()[:, None] / D))
         )
 
-    (input_grad,) = stage(live, [qkv_flow, small_flow], [input_sums])
+    (input_grad,) = stage(
+        live, [qkv_flow, small_flow], [input_sums], sync=late[1:] + early[1:]
+    )
     flows = [qkv_flow, small_flow] + early + late
     while any(flow.sends is not None for flow in flows):
         stage(live, flows)

time: 1400 us -> 1400 us (level)
    unnamed x206 -> x212, local copies, waits for them, and re-layouts: 29.2 us -> 34 us
where the time goes in v3:
time: 1400 us; the launch traced here: 1390 us
  waiting for transfers between devices  502 us (36%)
  Pallas kernels  490 us (35%)
  other arithmetic  143 us (10%)
  local copies, waits for them, and re-layouts  97.7 us (7%)
  starting transfers between devices  86.5 us (6%)
  matrix products  59.8 us (4%)
  between operations  16 us (1%)
    ppermute x74, waiting for transfers between devices, swap(): return lax.ppermute(values, axis, [(n, n ^ bit) for n in range(size)])  492 us
    pallas_call x2, Pallas kernels, expert_step(): pl.pallas_call(functools.partial(expert_kernel, count, hidden), grid_spec...  155 us
    pallas_call x3, Pallas kernels, weight_grads(): pl.pallas_call(functools.partial(weight_grad_kernel, mids), grid_spec=plt...  127 us
    ppermute x74, starting transfers between devices, swap(): return lax.ppermute(values, axis, [(n, n ^ bit) for n in range(size)])  86.2 us
    pallas_call x2, Pallas kernels, attend_backward(): pl.pallas_call(attend_backward_kernel, grid_spec=pltpu.PrefetchScalarGrid...  64.4 us
    dot_general x9, matrix products, dot_of(): lax.dot_general(a, b, (((da,), (db,)), ((), ())), preferred_element_type=...  59.8 us
    pallas_call x2, Pallas kernels, compact(): pl.pallas_call(compact_kernel, grid_spec=pltpu.PrefetchScalarGridSpec(num...  38.3 us
    pallas_call x2, Pallas kernels, attend_forward(): pl.pallas_call(attend_forward_kernel, grid_spec=pltpu.PrefetchScalarGridS...  36.3 us
  transfers between devices with their start and end apart: 78, of which 30 were waited for; matrix products, arithmetic and copies ran while one was open for 17% of the time, Pallas kernels for 34%

profile of v3, /device:TPU:0, one launch (start us, length us, event | category | flops | bytes accessed | tf_op | source)
XLA Modules:
  0.0 1394.1 jit_solution(7993071464033973595)
XLA Ops:
  25.8 34.6 %collective-permute-done.1 = f32[512]{0:T(512)S(1)} collective-permute-done((f32[512]{0:T(512)S(1)}, f32[512]{0:T(512)S(1)}, u32[]{:S(2)}, u32[]{:S(2)}) %collective-permute-start.1) | collective-permute-done | bytes 2080 | tf_op jit(solution)/shard_map/ppermute | solution.py:646
  62.9 8.3 pack_weights.1
  97.6 21.0 %collective-permute-done.5 = bf16[2,16,256]{2,1,0:T(8,128)(2,1)S(1)} collective-permute-done((bf16[2,16,256]{2,1,0:T(8,128)(2,1)S(1)}, bf16[2,16,256]{2,1,0:T(8,128)(2,1)S(1)}, u32[]{:S(2)}, u32[]{:S(2)}) %collective-permute-start.5) | collective-permute-done | bytes 16416 | tf_op jit(solution)/shard_map/ppermute | solution.py:646
  118.6 8.7 all-gather.6.cloned.1.call-done
  130.5 19.3 %fusion.110.q_ref.k_ref.v_ref = f32[2048,1536]{1,0:T(8,128)} fusion(bf16[2048,2048]{1,0:T(8,128)(2,1)} %fusion.43.x_ref, bf16[2048,1536]{1,0:T(8,128)(2,1)} %all-gather.6.cloned.1.call-done), kind=kOutput, calls=%fused_computation.307 | convolution fusion | flops 12884901888 | bytes 27262976 | tf_op jit(solution)/shard_map/dot_general | solution.py:36
  149.7 18.0 %attend_forward.2 = (bf16[1024,512]{1,0:T(8,128)(2,1)}, bf16[1024,512]{1,0:T(8,128)(2,1)}, bf16[1024,512]{1,0:T(8,128)(2,1)}, bf16[1024,512]{1,0:T(8,128)(2,1)}) custom-call(s32[1]{0:T(128)} %get-tuple-element.677.live_ref, f32[2048,1536]{1,0:T(8,128)} %fusion.110.q_ref.k_ref.v_ref, f32[2048,1536]{1,0:T(8,128)} %fusion.110.q_ref.k_ref.v_ref, ...), custom_call_target="tpu_custom_call" | custom-call | flops 85899344 | bytes 209715 | tf_op jit(solution)/shard_map/attend_forward/pallas_call | solution.py:96
  167.7 18.3 %attend_forward.3 = (bf16[1024,512]{1,0:T(8,128)(2,1)}, bf16[1024,512]{1,0:T(8,128)(2,1)}, bf16[1024,512]{1,0:T(8,128)(2,1)}, bf16[1024,512]{1,0:T(8,128)(2,1)}) custom-call(s32[1]{0:T(128)} %get-tuple-element.676.live_ref, f32[2048,1536]{1,0:T(8,128)} %fusion.110.q_ref.k_ref.v_ref, f32[2048,1536]{1,0:T(8,128)} %fusion.110.q_ref.k_ref.v_ref, ...), custom_call_target="tpu_custom_call" | custom-call | flops 85899344 | bytes 209715 | tf_op jit(solution)/shard_map/attend_forward/pallas_call | solution.py:96
  203.8 29.3 %collective-permute-done.19 = bf16[1,1024,512]{2,1,0:T(8,128)(2,1)S(1)} collective-permute-done((bf16[1,1024,512]{2,1,0:T(8,128)(2,1)S(1)}, bf16[1,1024,512]{2,1,0:T(8,128)(2,1)S(1)}, u32[]{:S(2)}, u32[]{:S(2)}) %collective-permute-start.19) | collective-permute-done | bytes 1048608 | tf_op jit(solution)/shard_map/ppermute | solution.py:646
  233.6 21.7 %collective-permute-done.17 = bf16[1,1024,512]{2,1,0:T(8,128)(2,1)S(1)} collective-permute-done((bf16[1,1024,512]{2,1,0:T(8,128)(2,1)S(1)}, bf16[1,1024,512]{2,1,0:T(8,128)(2,1)S(1)}, u32[]{:S(2)}, u32[]{:S(2)}) %collective-permute-start.17) | collective-permute-done | bytes 1048608 | tf_op jit(solution)/shard_map/ppermute | solution.py:646
  255.9 12.6 collective-permute-done.11.refs_1_
  269.7 7.1 collective-permute-done.13.refs_4_
  299.1 19.2 %compact.2 = (bf16[2304,2048]{1,0:T(8,128)(2,1)}, bf16[2304,2048]{1,0:T(8,128)(2,1)}) custom-call(s32[4,16]{1,0:T(4,128)} %fusion.93.start_ref, s32[2]{0:T(128)} %pad_add_fusion.1.where_ref, s32[2,2,1,2048]{3,2,1,0:T(1,128)} %select_n.148.pos_ref, bf16[8,2048,512]{2,1,0:T(8,128)(2,1)} %bitcast.348), custom_call_target="tpu_custom_call" | custom-call | flops 193273536 | bytes 713031 | tf_op jit(solution)/shard_map/compact/pallas_call | solution.py:260
  318.3 10.5 collective-permute-done.22.refs_3_
  328.8 35.2 %collective-permute-done.23.refs_5_ = bf16[256,3072]{1,0:T(8,128)(2,1)} collective-permute-done((bf16[256,3072]{1,0:T(8,128)(2,1)}, bf16[256,3072]{1,0:T(8,128)(2,1)}, u32[]{:S(2)}, u32[]{:S(2)}) %collective-permute-start.23) | collective-permute-done | bytes 1572896 | tf_op jit(solution)/shard_map/ppermute | solution.py:646
  375.6 56.6 %collective-permute-done.27.refs_4_ = bf16[256,3072]{1,0:T(8,128)(2,1)} collective-permute-done((bf16[256,3072]{1,0:T(8,128)(2,1)}, bf16[256,3072]{1,0:T(8,128)(2,1)}, u32[]{:S(2)}, u32[]{:S(2)}) %collective-permute-start.27) | collective-permute-done | bytes 1572896 | tf_op jit(solution)/shard_map/ppermute | solution.py:646
  443.3 5.7 compact_scalars.1
  449.0 11.7 collective-permute-done.30.refs_1_
  467.5 19.1 %compact.3 = (bf16[2304,2048]{1,0:T(8,128)(2,1)}, bf16[2304,2048]{1,0:T(8,128)(2,1)}) custom-call(s32[4,16]{1,0:T(4,128)} %fusion.93.start_ref, s32[2]{0:T(128)} %pad_add_fusion.1.where_ref, s32[2,2,1,2048]{3,2,1,0:T(1,128)} %select_n.148.pos_ref, bf16[8,2048,512]{2,1,0:T(8,128)(2,1)} %bitcast.349), custom_call_target="tpu_custom_call" | custom-call | flops 193273536 | bytes 713031 | tf_op jit(solution)/shard_map/compact/pallas_call | solution.py:260
  486.6 77.5 %expert_step.2 = (bf16[2304,2048]{1,0:T(8,128)(2,1)}, bf16[2304,2048]{1,0:T(8,128)(2,1)}, bf16[2304,1024]{1,0:T(8,128)(2,1)}, f32[2304,1]{1,0:T(8,128)}, f32[2304,1]{1,0:T(8,128)}, /*index=5*/bf16[2304,2048]{1,0:T(8,128)(2,1)}) custom-call(s32[8]{0:T(128)} %stack.252.row_ref, bf16[2304,2048]{1,0:T(8,128)(2,1)} %get-tuple-element.366.x_ref, ...), custom_call_target="tpu_custom_call" | custom-call | flops 1159641216 | bytes 1038090 | tf_op jit(solution)/shard_map/expert_step/pallas_call | solution.py:555
  566.7 47.4 %weight_grads.3 = bf16[2,2,2,256,3072]{4,3,2,1,0:T(8,128)(2,1)} custom-call(s32[9]{0:T(128)} %stack.258.place_ref, bf16[2304,2048]{1,0:T(8,128)(2,1)} %get-tuple-element.366.x_ref, bf16[2304,2048]{1,0:T(8,128)(2,1)} %get-tuple-element.367.m_ref, bf16[2304,2048]{1,0:T(8,128)(2,1)} %get-tuple-element.368.pre_ref, bf16[2304,1024]{1,0:T(8,128)(2,1)} %get-tuple-element.369.act_ref), custom_call_target="tpu_custom_call" | custom-call | flops 579820608 | bytes 660602 | tf_op jit(solution)/shard_map/weight_grads/pallas_call | solution.py:619
  614.1 6.0 slice_bitcast_fusion.2
  626.9 77.7 %expert_step.3 = (bf16[2304,2048]{1,0:T(8,128)(2,1)}, bf16[2304,2048]{1,0:T(8,128)(2,1)}, bf16[2304,1024]{1,0:T(8,128)(2,1)}, f32[2304,1]{1,0:T(8,128)}, f32[2304,1]{1,0:T(8,128)}, /*index=5*/bf16[2304,2048]{1,0:T(8,128)(2,1)}) custom-call(s32[8]{0:T(128)} %stack.259.row_ref, bf16[2304,2048]{1,0:T(8,128)(2,1)} %get-tuple-element.418.x_ref, ...), custom_call_target="tpu_custom_call" | custom-call | flops 1159641216 | bytes 1038090 | tf_op jit(solution)/shard_map/expert_step/pallas_call | solution.py:555
  707.9 18.7 %expand.1 = (bf16[2,2,1024,512]{3,2,1,0:T(8,128)(2,1)}, bf16[2,2,1024,512]{3,2,1,0:T(8,128)(2,1)}, bf16[2,2,1024,512]{3,2,1,0:T(8,128)(2,1)}, bf16[2,2,1024,512]{3,2,1,0:T(8,128)(2,1)}) custom-call(s32[4,16]{1,0:T(4,128)} %fusion.93.start_ref, s32[2]{0:T(128)} %pad_add_fusion.1.where_ref, s32[2,2,2048,1]{3,2,1,0:T(8,128)} %copy.111.pos_ref, ...), custom_call_target="tpu_custom_call" | custom-call | flops 193273536 | bytes 713031 | tf_op jit(solution)/shard_map/expand/pallas_call | solution.py:378
  744.9 6.4 expand_scalars.1
  757.4 47.5 %weight_grads.4 = bf16[2,2,2,256,3072]{4,3,2,1,0:T(8,128)(2,1)} custom-call(s32[9]{0:T(128)} %stack.258.place_ref, bf16[2304,2048]{1,0:T(8,128)(2,1)} %get-tuple-element.418.x_ref, bf16[2304,2048]{1,0:T(8,128)(2,1)} %get-tuple-element.419.m_ref, bf16[2304,2048]{1,0:T(8,128)(2,1)} %get-tuple-element.420.pre_ref, bf16[2304,1024]{1,0:T(8,128)(2,1)} %get-tuple-element.421.act_ref), custom_call_target="tpu_custom_call" | custom-call | flops 579820608 | bytes 660602 | tf_op jit(solution)/shard_map/weight_grads/pallas_call | solution.py:619
  812.6 4.7 add_convert_fusion.1
  818.0 5.1 add_convert_fusion.2
  836.9 20.3 %expand_all.1 = bf16[2,4,2048,512]{3,2,1,0:T(8,128)(2,1)} custom-call(s32[4,16]{1,0:T(4,128)} %fusion.93.start_ref, s32[2]{0:T(128)} %pad_add_fusion.1.where_ref, s32[2,2,2048,1]{3,2,1,0:T(8,128)} %copy.111.pos_ref, bf16[2304,2048]{1,0:T(8,128)(2,1)} %get-tuple-element.430.refs_0_, bf16[2304,2048]{1,0:T(8,128)(2,1)} %get-tuple-element.431.refs_1_), custom_call_target="tpu_custom_call" | custom-call | flops 193273536 | bytes 713031 | tf_op jit(solution)/shard_map/expand_all/pallas_call | solution.py:415
  857.3 20.5 %collective-permute-done.43 = f32[4,6,2048]{2,1,0:T(8,128)} collective-permute-done((f32[4,6,2048]{2,1,0:T(8,128)}, f32[4,6,2048]{2,1,0:T(8,128)}, u32[]{:S(2)}, u32[]{:S(2)}) %collective-permute-start.43) | collective-permute-done | bytes 196640 | tf_op jit(solution)/shard_map/ppermute | solution.py:646
  890.3 9.0 collective-permute-done.47
  919.4 4.9 multiply_reduce_fusion
  925.6 44.9 %collective-permute-done.51 = bf16[2048,512]{1,0:T(8,128)(2,1)S(1)} collective-permute-done((bf16[2048,512]{1,0:T(8,128)(2,1)S(1)}, bf16[2048,512]{1,0:T(8,128)(2,1)S(1)}, u32[]{:S(2)}, u32[]{:S(2)}) %collective-permute-start.51) | collective-permute-done | bytes 2097184 | tf_op jit(solution)/shard_map/ppermute | solution.py:646
  992.9 32.0 %attend_backward.3 = (bf16[1024,512]{1,0:T(8,128)(2,1)}, bf16[1024,512]{1,0:T(8,128)(2,1)}, bf16[1024,512]{1,0:T(8,128)(2,1)}, f32[1,128]{1,0:T(1,128)}, f32[1,128]{1,0:T(1,128)}, /*index=5*/f32[1024,1]{1,0:T(8,128)}) custom-call(s32[1]{0:T(128)} %get-tuple-element.676.live_ref, bf16[1024,512]{1,0:T(8,128)(2,1)} %get-tuple-element.466.ql_ref, ...), custom_call_target="tpu_custom_call" | custom-call | flops 214748368 | bytes 251658 | tf_op jit(solution)/shard_map/attend_backward/pallas_call | solution.py:214
  1026.1 6.2 fusion.61.do_ref
  1032.3 32.4 %attend_backward.2 = (bf16[1024,512]{1,0:T(8,128)(2,1)}, bf16[1024,512]{1,0:T(8,128)(2,1)}, bf16[1024,512]{1,0:T(8,128)(2,1)}, f32[1,128]{1,0:T(1,128)}, f32[1,128]{1,0:T(1,128)}, /*index=5*/f32[1024,1]{1,0:T(8,128)}) custom-call(s32[1]{0:T(128)} %get-tuple-element.677.live_ref, bf16[1024,512]{1,0:T(8,128)(2,1)} %get-tuple-element.448.ql_ref, ...), custom_call_target="tpu_custom_call" | custom-call | flops 214748368 | bytes 251658 | tf_op jit(solution)/shard_map/attend_backward/pallas_call | solution.py:214
  1072.7 18.8 %fusion.111 = f32[2048,2048]{1,0:T(8,128)S(1)} fusion(bf16[2048,1536]{1,0:T(8,128)(2,1)} %constant_dynamic-update-slice_fusion.10.pre_ref, bf16[2048,1536]{1,0:T(8,128)(2,1)} %pad_maximum_fusion.1), kind=kOutput, calls=%fused_computation.308 | convolution fusion | flops 12884901888 | bytes 29360128 | tf_op jit(solution)/shard_map/dot_general | solution.py:36
  1091.4 6.4 copy-done.9
  1111.4 32.1 %weight_grads.5 = bf16[2,2,2,256,2048]{4,3,2,1,0:T(8,128)(2,1)} custom-call(s32[9]{0:T(128)} %stack.302.place_ref, bf16[2048,2048]{1,0:T(8,128)(2,1)} %fusion.43.x_ref, bf16[2048,2048]{1,0:T(8,128)(2,1)} %copy-done.10, bf16[2048,1536]{1,0:T(8,128)(2,1)} %constant_dynamic-update-slice_fusion.10.pre_ref, bf16[2048,512]{1,0:T(8,128)(2,1)} %pad_maximum_fusion.7.act_ref), custom_call_target="tpu_custom_call" | custom-call | flops 343597376 | bytes 503316 | tf_op jit(solution)/shard_map/weight_grads/pallas_call | solution.py:619
  1147.0 28.7 %collective-permute-done.69 = bf16[1,256,3072]{2,1,0:T(8,128)(2,1)} collective-permute-done((bf16[1,256,3072]{2,1,0:T(8,128)(2,1)}, bf16[1,256,3072]{2,1,0:T(8,128)(2,1)}, u32[]{:S(2)}, u32[]{:S(2)}) %collective-permute-start.69) | collective-permute-done | bytes 1572896 | tf_op jit(solution)/shard_map/ppermute | solution.py:646
  1179.4 10.2 fusion.19
  1195.2 51.2 %collective-permute-done.68 = bf16[1,256,3072]{2,1,0:T(8,128)(2,1)S(1)} collective-permute-done((bf16[1,256,3072]{2,1,0:T(8,128)(2,1)S(1)}, bf16[1,256,3072]{2,1,0:T(8,128)(2,1)S(1)}, u32[]{:S(2)}, u32[]{:S(2)}) %collective-permute-start.68) | collective-permute-done | bytes 1572896 | tf_op jit(solution)/shard_map/ppermute | solution.py:646
  1250.9 5.7 collective-permute-done.61
  1259.9 8.9 collective-permute-done.59
  1277.3 7.3 fusion.25
  1284.6 13.7 collective-permute-done.65
  1298.4 4.8 collective-permute-done.66
  1320.4 45.2 %collective-permute-done.73.refs_3_ = bf16[256,3072]{1,0:T(8,128)(2,1)} collective-permute-done((bf16[256,3072]{1,0:T(8,128)(2,1)}, bf16[256,3072]{1,0:T(8,128)(2,1)}, u32[]{:S(2)}, u32[]{:S(2)}) %collective-permute-start.73) | collective-permute-done | bytes 1572896 | tf_op jit(solution)/shard_map/ppermute | solution.py:646
  1365.7 9.5 unpack_grads.1
  (549 shorter events, 317.6 us)
Async XLA Ops:
  7.2 120.1 %all-gather.6.cloned.1.call-start = ((), (), s32[]{:S(2)}) async-start(), calls=%async_computation.1 | async-start | bytes 7077888 | tf_op jit(solution)/shard_map/all_gather | solution.py:908
  11.6 287.5 %all-gather.8.cloned.1.call-start = ((), (), s32[]{:S(2)}) async-start(), calls=%async_computation.3 | async-start | bytes 18874368 | tf_op jit(solution)/shard_map/all_gather | solution.py:968
  11.7 59.5 %collective-permute-start = (bf16[2048,512]{1,0:T(8,128)(2,1)S(1)}, bf16[2048,512]{1,0:T(8,128)(2,1)}, u32[]{:S(2)}, u32[]{:S(2)}) collective-permute-start(bf16[2048,512]{1,0:T(8,128)(2,1)S(1)} %copy-done), channel_id=1, source_target_pairs={{0,2},{1,3},{2,0},{3,1},{4,6},{5,7},{6,4},{7,5},{8,10},{9,11},{10,... | collective-permute-start | bytes 6291464 | tf_op jit(solution)/shard_map/ppermute | solution.py:646
  14.7 60.7 %collective-permute-start.7 = (bf16[2048,512]{1,0:T(8,128)(2,1)S(1)}, bf16[2048,512]{1,0:T(8,128)(2,1)}, u32[]{:S(2)}, u32[]{:S(2)}) collective-permute-start(bf16[2048,512]{1,0:T(8,128)(2,1)S(1)} %copy-done), channel_id=1, source_target_pairs={{0,1},{1,0},{2,3},{3,2},{4,5},{5,4},{6,7},{7,6},{8,9},{9,8},{10,11... | collective-permute-start | bytes 6291464 | tf_op jit(solution)/shard_map/ppermute | solution.py:646
  15.4 55.8 %collective-permute-start.4 = (bf16[1,256,512]{1,2,0:T(8,128)(2,1)S(1)}, bf16[1,256,512]{1,2,0:T(8,128)(2,1)S(1)}, u32[]{:S(2)}, u32[]{:S(2)}) collective-permute-start(bf16[1,256,512]{1,2,0:T(8,128)(2,1)S(1)} %get-tuple-element.625), channel_id=1, source_target_pairs={{0,16},{16,0},{1,17},{17,1},{2,18},{18,2},{3,19},{19,3},{4,20},{20... | collective-permute-start | bytes 786440 | tf_op jit(solution)/shard_map/ppermute | solution.py:646
  18.6 52.6 %collective-permute-start.3 = (bf16[1,16,256]{2,1,0:T(8,128)(2,1)S(1)}, bf16[1,16,256]{2,1,0:T(8,128)(2,1)S(1)}, u32[]{:S(2)}, u32[]{:S(2)}) collective-permute-start(bf16[1,16,256]{2,1,0:T(8,128)(2,1)S(1)} %get-tuple-element.623), channel_id=1, source_target_pairs={{0,16},{16,0},{1,17},{17,1},{2,18},{18,2},{3,19},{19,3},{4,20},{20... | collective-permute-start | bytes 24584 | tf_op jit(solution)/shard_map/ppermute | solution.py:646
  127.4 340.2 %all-gather.10.cloned.1.call-start = ((), (), s32[]{:S(2)}) async-start(), calls=%async_computation.4 | async-start | bytes 18874368 | tf_op jit(solution)/shard_map/all_gather | solution.py:1021
  196.9 71.6 %collective-permute-start.11 = (bf16[256,3072]{1,0:T(8,128)(2,1)S(1)}, bf16[256,3072]{1,0:T(8,128)(2,1)}, u32[]{:S(2)}, u32[]{:S(2)}) collective-permute-start(bf16[256,3072]{1,0:T(8,128)(2,1)S(1)} %get-tuple-element.648.refs_0_), channel_id=1, source_target_pairs={{0,16},{16,0},{1,17},{17,1},{2,18},{18,2},{3,19},{19,3},{4,20},{20... | collective-permute-start | bytes 4718600 | tf_op jit(solution)/shard_map/ppermute | solution.py:646
  200.2 68.3 %collective-permute-start.12 = (bf16[256,3072]{1,0:T(8,128)(2,1)S(1)}, bf16[256,3072]{1,0:T(8,128)(2,1)S(1)}, u32[]{:S(2)}, u32[]{:S(2)}) collective-permute-start(bf16[256,3072]{1,0:T(8,128)(2,1)S(1)} %get-tuple-element.648.refs_0_), channel_id=1, source_target_pairs={{0,4},{4,0},{1,5},{5,1},{2,6},{6,2},{3,7},{7,3},{8,12},{12,8},{9,1... | collective-permute-start | bytes 4718600 | tf_op jit(solution)/shard_map/ppermute | solution.py:646
  201.7 75.0 %collective-permute-start.13 = (bf16[256,3072]{1,0:T(8,128)(2,1)S(1)}, bf16[256,3072]{1,0:T(8,128)(2,1)}, u32[]{:S(2)}, u32[]{:S(2)}) collective-permute-start(bf16[256,3072]{1,0:T(8,128)(2,1)S(1)} %get-tuple-element.647), channel_id=1, source_target_pairs={{0,8},{8,0},{1,9},{9,1},{2,10},{10,2},{3,11},{11,3},{4,12},{12,4},... | collective-permute-start | bytes 4718600 | tf_op jit(solution)/shard_map/ppermute | solution.py:646
  202.3 53.1 %collective-permute-start.17 = (bf16[1,1024,512]{2,1,0:T(8,128)(2,1)S(1)}, bf16[1,1024,512]{2,1,0:T(8,128)(2,1)S(1)}, u32[]{:S(2)}, u32[]{:S(2)}) collective-permute-start(bf16[1,1024,512]{2,1,0:T(8,128)(2,1)S(1)} %fusion.69), channel_id=1, source_target_pairs={{0,2},{1,3},{2,0},{3,1},{4,6},{5,7},{6,4},{7,5},{8,10},{9,11},{10,... | collective-permute-start | bytes 3145736 | tf_op jit(solution)/shard_map/ppermute | solution.py:646
  278.9 1029.5 %reduce-scatter.2.cloned.1.call-start = ((), (), s32[]{:S(2)}) async-start(), calls=%async_computation.2 | async-start | bytes 18874368 | tf_op jit(solution)/shard_map/reduce_scatter | solution.py:1185
  292.6 71.4 %collective-permute-start.23 = (bf16[256,3072]{1,0:T(8,128)(2,1)}, bf16[256,3072]{1,0:T(8,128)(2,1)}, u32[]{:S(2)}, u32[]{:S(2)}) collective-permute-start(bf16[256,3072]{1,0:T(8,128)(2,1)} %collective-permute-done.13.refs_4_), channel_id=1, source_target_pairs={{0,16},{16,0},{1,17},{17,1},{2,18},{18,2},{3,19},{19,3},{4,20},{20... | collective-permute-start | bytes 4718600 | tf_op jit(solution)/shard_map/ppermute | solution.py:646
  295.3 68.8 %collective-permute-start.24 = (bf16[256,3072]{1,0:T(8,128)(2,1)}, bf16[256,3072]{1,0:T(8,128)(2,1)}, u32[]{:S(2)}, u32[]{:S(2)}) collective-permute-start(bf16[256,3072]{1,0:T(8,128)(2,1)} %collective-permute-done.13.refs_4_), channel_id=1, source_target_pairs={{0,4},{4,0},{1,5},{5,1},{2,6},{6,2},{3,7},{7,3},{8,12},{12,8},{9,1... | collective-permute-start | bytes 4718600 | tf_op jit(solution)/shard_map/ppermute | solution.py:646
  297.4 134.8 %collective-permute-start.27 = (bf16[256,3072]{1,0:T(8,128)(2,1)}, bf16[256,3072]{1,0:T(8,128)(2,1)}, u32[]{:S(2)}, u32[]{:S(2)}) collective-permute-start(bf16[256,3072]{1,0:T(8,128)(2,1)} %get-tuple-element.332), channel_id=1, source_target_pairs={{0,8},{8,0},{1,9},{9,1},{2,10},{10,2},{3,11},{11,3},{4,12},{12,4},... | collective-permute-start | bytes 4718600 | tf_op jit(solution)/shard_map/ppermute | solution.py:646
  364.0 68.9 %collective-permute-start.26 = (bf16[256,3072]{1,0:T(8,128)(2,1)}, bf16[256,3072]{1,0:T(8,128)(2,1)}, u32[]{:S(2)}, u32[]{:S(2)}) collective-permute-start(bf16[256,3072]{1,0:T(8,128)(2,1)} %collective-permute-done.23.refs_5_), channel_id=1, source_target_pairs={{0,4},{4,0},{1,5},{5,1},{2,6},{6,2},{3,7},{7,3},{8,12},{12,8},{9,1... | collective-permute-start | bytes 4718600 | tf_op jit(solution)/shard_map/ppermute | solution.py:646
  365.8 66.4 %collective-permute-start.25 = (f32[4,17,2048]{2,0,1:T(4,128)}, f32[4,17,2048]{2,0,1:T(4,128)S(1)}, u32[]{:S(2)}, u32[]{:S(2)}) collective-permute-start(f32[4,17,2048]{2,0,1:T(4,128)} %copy.103), channel_id=1, source_target_pairs={{0,2},{1,3},{2,0},{3,1},{4,6},{5,7},{6,4},{7,5},{8,10},{9,11},{10,... | collective-permute-start | bytes 1671176 | tf_op jit(solution)/shard_map/ppermute | solution.py:646
  370.7 90.1 %collective-permute-start.30 = (bf16[256,3072]{1,0:T(8,128)(2,1)}, bf16[256,3072]{1,0:T(8,128)(2,1)}, u32[]{:S(2)}, u32[]{:S(2)}) collective-permute-start(bf16[256,3072]{1,0:T(8,128)(2,1)} %get-tuple-element.378.refs_0_), channel_id=1, source_target_pairs={{0,16},{16,0},{1,17},{17,1},{2,18},{18,2},{3,19},{19,3},{4,20},{20... | collective-permute-start | bytes 4718600 | tf_op jit(solution)/shard_map/ppermute | solution.py:646
  374.1 190.0 %collective-permute-start.32 = (bf16[256,3072]{1,0:T(8,128)(2,1)}, bf16[256,3072]{1,0:T(8,128)(2,1)}, u32[]{:S(2)}, u32[]{:S(2)}) collective-permute-start(bf16[256,3072]{1,0:T(8,128)(2,1)} %get-tuple-element.378.refs_0_), channel_id=1, source_target_pairs={{0,4},{4,0},{1,5},{5,1},{2,6},{6,2},{3,7},{7,3},{8,12},{12,8},{9,1... | collective-permute-start | bytes 4718600 | tf_op jit(solution)/shard_map/ppermute | solution.py:646
  438.2 125.9 %collective-permute-start.28 = (bf16[256,3072]{1,0:T(8,128)(2,1)}, bf16[256,3072]{1,0:T(8,128)(2,1)}, u32[]{:S(2)}, u32[]{:S(2)}) collective-permute-start(bf16[256,3072]{1,0:T(8,128)(2,1)} %collective-permute-done.27.refs_4_), channel_id=1, source_target_pairs={{0,16},{16,0},{1,17},{17,1},{2,18},{18,2},{3,19},{19,3},{4,20},{20... | collective-permute-start | bytes 4718600 | tf_op jit(solution)/shard_map/ppermute | solution.py:646
  439.4 124.8 %collective-permute-start.29 = (bf16[256,3072]{1,0:T(8,128)(2,1)}, bf16[256,3072]{1,0:T(8,128)(2,1)}, u32[]{:S(2)}, u32[]{:S(2)}) collective-permute-start(bf16[256,3072]{1,0:T(8,128)(2,1)} %collective-permute-done.27.refs_4_), channel_id=1, source_target_pairs={{0,4},{4,0},{1,5},{5,1},{2,6},{6,2},{3,7},{7,3},{8,12},{12,8},{9,1... | collective-permute-start | bytes 4718600 | tf_op jit(solution)/shard_map/ppermute | solution.py:646
  460.8 103.4 %collective-permute-start.31 = (bf16[256,3072]{1,0:T(8,128)(2,1)}, bf16[256,3072]{1,0:T(8,128)(2,1)}, u32[]{:S(2)}, u32[]{:S(2)}) collective-permute-start(bf16[256,3072]{1,0:T(8,128)(2,1)} %collective-permute-done.30.refs_1_), channel_id=1, source_target_pairs={{0,4},{4,0},{1,5},{5,1},{2,6},{6,2},{3,7},{7,3},{8,12},{12,8},{9,1... | collective-permute-start | bytes 4718600 | tf_op jit(solution)/shard_map/ppermute | solution.py:646
  564.2 50.0 %collective-permute-start.33 = (bf16[256,3072]{1,0:T(8,128)(2,1)}, bf16[256,3072]{1,0:T(8,128)(2,1)}, u32[]{:S(2)}, u32[]{:S(2)}) collective-permute-start(bf16[256,3072]{1,0:T(8,128)(2,1)} %collective-permute-done.28.refs_5_), channel_id=1, source_target_pairs={{0,4},{4,0},{1,5},{5,1},{2,6},{6,2},{3,7},{7,3},{8,12},{12,8},{9,1... | collective-permute-start | bytes 4718600 | tf_op jit(solution)/shard_map/ppermute | solution.py:646
  620.1 84.4 %collective-permute-start.34 = (bf16[2,256,3072]{2,1,0:T(8,128)(2,1)}, bf16[2,256,3072]{2,1,0:T(8,128)(2,1)}, u32[]{:S(2)}, u32[]{:S(2)}) collective-permute-start(bf16[2,256,3072]{2,1,0:T(8,128)(2,1)} %get-tuple-element.632), channel_id=1, source_target_pairs={{0,4},{4,0},{1,5},{5,1},{2,6},{6,2},{3,7},{7,3},{8,12},{12,8},{9,1... | collective-permute-start | bytes 9437192 | tf_op jit(solution)/shard_map/ppermute | solution.py:646
  726.6 81.1 %collective-permute-start.35 = (bf16[2,2,1024,512]{3,2,1,0:T(8,128)(2,1)}, bf16[2,2,1024,512]{3,2,1,0:T(8,128)(2,1)}, u32[]{:S(2)}, u32[]{:S(2)}) collective-permute-start(bf16[2,2,1024,512]{3,2,1,0:T(8,128)(2,1)} %get-tuple-element.410), channel_id=1, source_target_pairs={{0,1},{1,0},{2,3},{3,2},{4,5},{5,4},{6,7},{7,6},{8,9},{9,8},{10,11... | collective-permute-start | bytes 12582920 | tf_op jit(solution)/shard_map/ppermute | solution.py:646
  726.6 81.1 %collective-permute-start.36 = (bf16[2,2,1024,512]{3,2,1,0:T(8,128)(2,1)}, bf16[2,2,1024,512]{3,2,1,0:T(8,128)(2,1)}, u32[]{:S(2)}, u32[]{:S(2)}) collective-permute-start(bf16[2,2,1024,512]{3,2,1,0:T(8,128)(2,1)} %get-tuple-element.411), channel_id=1, source_target_pairs={{0,1},{1,0},{2,3},{3,2},{4,5},{5,4},{6,7},{7,6},{8,9},{9,8},{10,11... | collective-permute-start | bytes 12582920 | tf_op jit(solution)/shard_map/ppermute | solution.py:646
  727.1 80.6 %collective-permute-start.39 = (bf16[2,256,3072]{2,1,0:T(8,128)(2,1)}, bf16[2,256,3072]{2,1,0:T(8,128)(2,1)}, u32[]{:S(2)}, u32[]{:S(2)}) collective-permute-start(bf16[2,256,3072]{2,1,0:T(8,128)(2,1)} %get-tuple-element.417), channel_id=1, source_target_pairs={{0,4},{4,0},{1,5},{5,1},{2,6},{6,2},{3,7},{7,3},{8,12},{12,8},{9,1... | collective-permute-start | bytes 9437192 | tf_op jit(solution)/shard_map/ppermute | solution.py:646
  735.8 71.9 %collective-permute-start.38 = (bf16[1,256,3072]{2,1,0:T(8,128)(2,1)}, bf16[1,256,3072]{2,1,0:T(8,128)(2,1)}, u32[]{:S(2)}, u32[]{:S(2)}) collective-permute-start(bf16[1,256,3072]{2,1,0:T(8,128)(2,1)} %slice.499), channel_id=1, source_target_pairs={{0,16},{16,0},{1,17},{17,1},{2,18},{18,2},{3,19},{19,3},{4,20},{20... | collective-permute-start | bytes 4718600 | tf_op jit(solution)/shard_map/ppermute | solution.py:646
  753.2 51.8 %collective-permute-start.37 = (f32[1,6,2048]{2,1,0:T(8,128)S(1)}, f32[1,6,2048]{2,1,0:T(8,128)S(1)}, u32[]{:S(2)}, u32[]{:S(2)}) collective-permute-start(f32[1,6,2048]{2,1,0:T(8,128)S(1)} %broadcast_in_dim_reshape.3), channel_id=1, source_target_pairs={{0,8},{8,0},{1,9},{9,1},{2,10},{10,2},{3,11},{11,3},{4,12},{12,4},... | collective-permute-start | bytes 147464 | tf_op jit(solution)/shard_map/ppermute | solution.py:646
  817.3 61.7 %collective-permute-start.41 = (bf16[2,1024,512]{2,1,0:T(8,128)(2,1)}, bf16[2,1024,512]{2,1,0:T(8,128)(2,1)S(1)}, u32[]{:S(2)}, u32[]{:S(2)}) collective-permute-start(bf16[2,1024,512]{2,1,0:T(8,128)(2,1)} %get-tuple-element.636), channel_id=1, source_target_pairs={{0,8},{8,0},{1,9},{9,1},{2,10},{10,2},{3,11},{11,3},{4,12},{12,4},... | collective-permute-start | bytes 6291464 | tf_op jit(solution)/shard_map/ppermute | solution.py:646
  823.1 55.9 %collective-permute-start.40 = (bf16[2,1024,512]{2,1,0:T(8,128)(2,1)}, bf16[2,1024,512]{2,1,0:T(8,128)(2,1)S(1)}, u32[]{:S(2)}, u32[]{:S(2)}) collective-permute-start(bf16[2,1024,512]{2,1,0:T(8,128)(2,1)} %get-tuple-element.638), channel_id=1, source_target_pairs={{0,2},{1,3},{2,0},{3,1},{4,6},{5,7},{6,4},{7,5},{8,10},{9,11},{10,... | collective-permute-start | bytes 6291464 | tf_op jit(solution)/shard_map/ppermute | solution.py:646
  828.5 70.8 %collective-permute-start.47 = (bf16[2,256,3072]{2,1,0:T(8,128)(2,1)}, bf16[2,256,3072]{2,1,0:T(8,128)(2,1)}, u32[]{:S(2)}, u32[]{:S(2)}) collective-permute-start(bf16[2,256,3072]{2,1,0:T(8,128)(2,1)} %get-tuple-element.630), channel_id=1, source_target_pairs={{0,4},{4,0},{1,5},{5,1},{2,6},{6,2},{3,7},{7,3},{8,12},{12,8},{9,1... | collective-permute-start | bytes 9437192 | tf_op jit(solution)/shard_map/ppermute | solution.py:646
  975.7 93.2 %collective-permute-start.44 = (bf16[256,3072]{1,0:T(8,128)(2,1)}, bf16[256,3072]{1,0:T(8,128)(2,1)}, u32[]{:S(2)}, u32[]{:S(2)}) collective-permute-start(bf16[256,3072]{1,0:T(8,128)(2,1)} %fusion.59), channel_id=1, source_target_pairs={{0,8},{8,0},{1,9},{9,1},{2,10},{10,2},{3,11},{11,3},{4,12},{12,4},... | collective-permute-start | bytes 4718600 | tf_op jit(solution)/shard_map/ppermute | solution.py:646
  976.0 92.8 %collective-permute-start.49 = (bf16[2,256,3072]{2,1,0:T(8,128)(2,1)}, bf16[2,256,3072]{2,1,0:T(8,128)(2,1)}, u32[]{:S(2)}, u32[]{:S(2)}) collective-permute-start(bf16[2,256,3072]{2,1,0:T(8,128)(2,1)} %get-tuple-element.447), channel_id=1, source_target_pairs={{0,4},{4,0},{1,5},{5,1},{2,6},{6,2},{3,7},{7,3},{8,12},{12,8},{9,1... | collective-permute-start | bytes 9437192 | tf_op jit(solution)/shard_map/ppermute | solution.py:646
  977.2 91.6 %collective-permute-start.48 = (bf16[1,256,3072]{2,1,0:T(8,128)(2,1)}, bf16[1,256,3072]{2,1,0:T(8,128)(2,1)}, u32[]{:S(2)}, u32[]{:S(2)}) collective-permute-start(bf16[1,256,3072]{2,1,0:T(8,128)(2,1)} %slice.504), channel_id=1, source_target_pairs={{0,16},{16,0},{1,17},{17,1},{2,18},{18,2},{3,19},{19,3},{4,20},{20... | collective-permute-start | bytes 4718600 | tf_op jit(solution)/shard_map/ppermute | solution.py:646
  1100.8 78.5 %collective-permute-start.53 = (bf16[2,2048,512]{2,1,0:T(8,128)(2,1)}, bf16[2,2048,512]{2,1,0:T(8,128)(2,1)}, u32[]{:S(2)}, u32[]{:S(2)}) collective-permute-start(bf16[2,2048,512]{2,1,0:T(8,128)(2,1)} %pad_maximum_fusion.2), channel_id=1, source_target_pairs={{0,1},{1,0},{2,3},{3,2},{4,5},{5,4},{6,7},{7,6},{8,9},{9,8},{10,11... | collective-permute-start | bytes 12582920 | tf_op jit(solution)/shard_map/ppermute | solution.py:646
  1101.5 77.8 %collective-permute-start.54 = (f32[2048]{0:T(1024)S(1)}, f32[2048]{0:T(1024)S(1)}, u32[]{:S(2)}, u32[]{:S(2)}) collective-permute-start(f32[2048]{0:T(1024)S(1)} %constant_dynamic-update-slice_fusion.13), channel_id=1, source_target_pairs={{0,1},{1,0},{2,3},{3,2},{4,5},{5,4},{6,7},{7,6},{8,9},{9,8},{10,11... | collective-permute-start | bytes 24584 | tf_op jit(solution)/shard_map/ppermute | solution.py:646
  1102.1 77.2 %collective-permute-start.55 = (f32[2048]{0:T(1024)S(1)}, f32[2048]{0:T(1024)S(1)}, u32[]{:S(2)}, u32[]{:S(2)}) collective-permute-start(f32[2048]{0:T(1024)S(1)} %constant_dynamic-update-slice_fusion.13), channel_id=1, source_target_pairs={{0,2},{1,3},{2,0},{3,1},{4,6},{5,7},{6,4},{7,5},{8,10},{9,11},{10,... | collective-permute-start | bytes 24584 | tf_op jit(solution)/shard_map/ppermute | solution.py:646
  1103.1 76.3 %collective-permute-start.56 = (f32[2048]{0:T(1024)S(1)}, f32[2048]{0:T(1024)S(1)}, u32[]{:S(2)}, u32[]{:S(2)}) collective-permute-start(f32[2048]{0:T(1024)S(1)} %constant_dynamic-update-slice_fusion.13), channel_id=1, source_target_pairs={{0,3},{1,2},{2,1},{3,0},{4,7},{5,6},{6,5},{7,4},{8,11},{9,10},{10,... | collective-permute-start | bytes 24584 | tf_op jit(solution)/shard_map/ppermute | solution.py:646
  1103.5 72.1 %collective-permute-start.69 = (bf16[1,256,3072]{2,1,0:T(8,128)(2,1)}, bf16[1,256,3072]{2,1,0:T(8,128)(2,1)}, u32[]{:S(2)}, u32[]{:S(2)}) collective-permute-start(bf16[1,256,3072]{2,1,0:T(8,128)(2,1)} %slice.501), channel_id=1, source_target_pairs={{0,16},{16,0},{1,17},{17,1},{2,18},{18,2},{3,19},{19,3},{4,20},{20... | collective-permute-start | bytes 4718600 | tf_op jit(solution)/shard_map/ppermute | solution.py:646
  1175.6 70.8 %collective-permute-start.68 = (bf16[1,256,3072]{2,1,0:T(8,128)(2,1)S(1)}, bf16[1,256,3072]{2,1,0:T(8,128)(2,1)S(1)}, u32[]{:S(2)}, u32[]{:S(2)}) collective-permute-start(bf16[1,256,3072]{2,1,0:T(8,128)(2,1)S(1)} %slice.521), channel_id=1, source_target_pairs={{0,16},{16,0},{1,17},{17,1},{2,18},{18,2},{3,19},{19,3},{4,20},{20... | collective-permute-start | bytes 4718600 | tf_op jit(solution)/shard_map/ppermute | solution.py:646
  1189.6 70.3 %collective-permute-start.57 = (bf16[1,2048,512]{2,1,0:T(8,128)(2,1)S(1)}, bf16[1,2048,512]{2,1,0:T(8,128)(2,1)S(1)}, u32[]{:S(2)}, u32[]{:S(2)}) collective-permute-start(bf16[1,2048,512]{2,1,0:T(8,128)(2,1)S(1)} %get-tuple-element.626), channel_id=1, source_target_pairs={{0,2},{1,3},{2,0},{3,1},{4,6},{5,7},{6,4},{7,5},{8,10},{9,11},{10,... | collective-permute-start | bytes 6291464 | tf_op jit(solution)/shard_map/ppermute | solution.py:646
  1190.8 69.2 %collective-permute-start.58 = (bf16[2,2,256,1024]{3,2,1,0:T(8,128)(2,1)S(1)}, bf16[2,2,256,1024]{3,2,1,0:T(8,128)(2,1)S(1)}, u32[]{:S(2)}, u32[]{:S(2)}) collective-permute-start(bf16[2,2,256,1024]{3,2,1,0:T(8,128)(2,1)S(1)} %slice_bitcast_fusion.8), channel_id=1, source_target_pairs={{0,4},{4,0},{1,5},{5,1},{2,6},{6,2},{3,7},{7,3},{8,12},{12,8},{9,1... | collective-permute-start | bytes 6291464 | tf_op jit(solution)/shard_map/ppermute | solution.py:646
  1192.9 75.9 %collective-permute-start.59 = (bf16[2,2,256,1024]{3,2,1,0:T(8,128)(2,1)S(1)}, bf16[2,2,256,1024]{3,2,1,0:T(8,128)(2,1)S(1)}, u32[]{:S(2)}, u32[]{:S(2)}) collective-permute-start(bf16[2,2,256,1024]{3,2,1,0:T(8,128)(2,1)S(1)} %slice_bitcast_fusion.7), channel_id=1, source_target_pairs={{0,8},{8,0},{1,9},{9,1},{2,10},{10,2},{3,11},{11,3},{4,12},{12,4},... | collective-permute-start | bytes 6291464 | tf_op jit(solution)/shard_map/ppermute | solution.py:646
  1298.4 67.3 %collective-permute-start.73 = (bf16[256,3072]{1,0:T(8,128)(2,1)}, bf16[256,3072]{1,0:T(8,128)(2,1)}, u32[]{:S(2)}, u32[]{:S(2)}) collective-permute-start(bf16[256,3072]{1,0:T(8,128)(2,1)} %fusion.60), channel_id=1, source_target_pairs={{0,8},{8,0},{1,9},{9,1},{2,10},{10,2},{3,11},{11,3},{4,12},{12,4},... | collective-permute-start | bytes 4718600 | tf_op jit(solution)/shard_map/ppermute | solution.py:646
  1311.9 63.3 %collective-permute-start.71 = (bf16[256,1024]{1,0:T(8,128)(2,1)}, bf16[256,1024]{1,0:T(8,128)(2,1)S(1)}, u32[]{:S(2)}, u32[]{:S(2)}) collective-permute-start(bf16[256,1024]{1,0:T(8,128)(2,1)} %fusion.76), channel_id=1, source_target_pairs={{0,16},{16,0},{1,17},{17,1},{2,18},{18,2},{3,19},{19,3},{4,20},{20... | collective-permute-start | bytes 1572872 | tf_op jit(solution)/shard_map/ppermute | solution.py:646
  1317.4 58.6 %collective-permute-start.70 = (bf16[256,1024]{1,0:T(8,128)(2,1)}, bf16[256,1024]{1,0:T(8,128)(2,1)}, u32[]{:S(2)}, u32[]{:S(2)}) collective-permute-start(bf16[256,1024]{1,0:T(8,128)(2,1)} %fusion.75), channel_id=1, source_target_pairs={{0,16},{16,0},{1,17},{17,1},{2,18},{18,2},{3,19},{19,3},{4,20},{20... | collective-permute-start | bytes 1572872 | tf_op jit(solution)/shard_map/ppermute | solution.py:646
  1318.7 56.4 %collective-permute-start.72 = (f32[19,2048]{1,0:T(8,128)S(1)}, f32[19,2048]{1,0:T(8,128)S(1)}, u32[]{:S(2)}, u32[]{:S(2)}) collective-permute-start(f32[19,2048]{1,0:T(8,128)S(1)} %add_add_fusion), channel_id=1, source_target_pairs={{0,16},{16,0},{1,17},{17,1},{2,18},{18,2},{3,19},{19,3},{4,20},{20... | collective-permute-start | bytes 466952 | tf_op jit(solution)/shard_map/ppermute | solution.py:646
  (126 other events, 1728.5 us)
Sparse Core Ops, SparseCore 0:
  11.7 115.5 all-gather.5
  128.9 99.6 all-gather.7
  279.0 188.4 all-gather.9
  971.9 232.9 reduce-scatter.1
